TPU v7x, 128 devices: a whole 4x4x4 slice. The times are simulated.
128 devices in a mesh: dp: 8 (over y_hi, x), seq: 16 (over y_lo, z, core).
Axes of the slice: x: 4, y: 4 (y_hi: 2, y_lo: 2; y = y_hi * 2 + y_lo), z: 4, core: 2. Of those that a mesh axis runs over, the one named last changes fastest.
Arguments:
- latents: bfloat16 [8, 16, 256, 1152], P('dp', 'seq'), may hold values from -6 to 6
- cotangent: bfloat16 [8, 16, 256, 1152], P('dp', 'seq'), may hold values from -6 to 6
- modulation: float32 [8, 6, 1152], P('dp'), may hold values from -0.6 to 0.6
- spatial_qkv: bfloat16 [1152, 1728], replicated, may hold values from -0.1875 to 0.1875
- spatial_out: bfloat16 [1152, 576], replicated, may hold values from -0.25 to 0.25
- temporal_qkv: bfloat16 [1152, 1728], replicated, may hold values from -0.1875 to 0.1875
- temporal_out: bfloat16 [1152, 576], replicated, may hold values from -0.25 to 0.25
Outputs:
- grad_latents: bfloat16 [8, 16, 256, 1152], P('dp', 'seq')
- grad_modulation: float32 [8, 6, 1152], P('dp')
- spatial_dqkv: float32 [1152, 1728], P(('dp', 'seq'))
- spatial_dout: float32 [1152, 576], P(('dp', 'seq'))
- temporal_dqkv: float32 [1152, 1728], P(('dp', 'seq'))
- temporal_dout: float32 [1152, 576], P(('dp', 'seq'))
All inputs are finite; a program needn't handle non-finite values.
Results may differ from a plain program's by a relative error of at most 0.018.
Values may be sent and summed in bfloat16 or wider, within the bound.
A program may use at most 128 MiB of HBM per device.

v0:
```python
from functools import partial

import jax
import jax.numpy as jnp
from jax import lax
from jax.sharding import PartitionSpec as P

HEADS = 8
HEAD_DIM = 72


EPSILON = 1e-06


def norm_modulate(signal, offset, stretch):
    average = jnp.mean(signal, axis=-1, keepdims=True)
    centred = signal - average
    spread = jnp.mean(centred * centred, axis=-1, keepdims=True)
    normed = centred * lax.rsqrt(spread + EPSILON)
    return (normed * (1.0 + stretch) + offset).astype(jnp.bfloat16)


def matmul(former, latter):
    return jnp.dot(former, latter, preferred_element_type=jnp.float32)


def matmul_nt(former, latter):
    return lax.dot_general(
        former, latter, (((1,), (1,)), ((), ())), preferred_element_type=jnp.float32
    )


def matmul_tn(former, latter):
    return lax.dot_general(
        former, latter, (((0,), (0,)), ((), ())), preferred_element_type=jnp.float32
    )


def attend(packed, over_frames):
    leading = packed.shape[:3]
    stacked = packed.reshape(leading + (3, HEADS, HEAD_DIM))
    query_rows = stacked[:, :, :, 0]
    key_rows = stacked[:, :, :, 1]
    value_rows = stacked[:, :, :, 2]
    factor = HEAD_DIM ** (-0.5)
    if over_frames:
        scores = jnp.einsum(
            "cfphe,cgphe->cphfg", query_rows, key_rows, preferred_element_type=jnp.float32
        )
    else:
        scores = jnp.einsum(
            "cfphe,cfqhe->cfhpq", query_rows, key_rows, preferred_element_type=jnp.float32
        )
    raised = jnp.exp(scores * factor)
    weights = (raised / jnp.sum(raised, axis=-1, keepdims=True)).astype(jnp.bfloat16)
    if over_frames:
        attended = jnp.einsum(
            "cphfg,cgphe->cfphe", weights, value_rows, preferred_element_type=jnp.float32
        )
    else:
        attended = jnp.einsum(
            "cfhpq,cfqhe->cfphe", weights, value_rows, preferred_element_type=jnp.float32
        )
    return attended.reshape(leading + (HEADS * HEAD_DIM,)).astype(jnp.bfloat16)


def sublayer_forward(signal, offset, stretch, gating, qkv_weight, out_weight):
    widened = signal.astype(jnp.float32)
    modulated, norm_back = jax.vjp(norm_modulate, widened, offset, stretch)
    channels = signal.shape[-1]
    flattened = modulated.reshape(-1, channels)
    packed = matmul(flattened, qkv_weight).astype(jnp.bfloat16).reshape(signal.shape[:3] + (-1,))
    attended, core_back = jax.vjp(partial(attend, over_frames=False), packed)
    branch = matmul_nt(attended.reshape(-1, attended.shape[-1]), out_weight)
    result = (widened + gating * branch.reshape(signal.shape)).astype(jnp.bfloat16)
    return (result, (flattened, attended, branch, norm_back, core_back))


def sublayer_backward(stashed, cotangent, gating, qkv_weight, out_weight):
    flattened, attended, branch, norm_back, core_back = stashed
    upstream = cotangent.astype(jnp.float32)
    clips_here = upstream.shape[0]
    channels = upstream.shape[-1]
    d_gate = jnp.sum(
        (upstream.reshape(-1, channels) * branch).reshape(clips_here, -1, channels), axis=1
    )
    d_branch = (gating * upstream).astype(jnp.bfloat16).reshape(-1, channels)
    d_mixed = matmul(d_branch, out_weight).astype(jnp.bfloat16).reshape(attended.shape)
    (d_packed,) = core_back(d_mixed)
    d_rows = d_packed.reshape(-1, d_packed.shape[-1])
    d_modulated = matmul_nt(d_rows, qkv_weight).astype(jnp.bfloat16).reshape(upstream.shape)
    d_signal, d_offset, d_stretch = norm_back(d_modulated)
    moments = jnp.stack(
        [d_offset.reshape(clips_here, channels), d_stretch.reshape(clips_here, channels), d_gate],
        axis=1,
    )
    grad_terms = (flattened, d_rows, d_branch, attended.reshape(-1, attended.shape[-1]))
    return (upstream + d_signal, moments, grad_terms)


def reduce_terms(grad_terms, divisor):
    flattened, d_rows, d_branch, mixed_rows = grad_terms
    packed_cols = d_rows.shape[1]
    summed = lax.psum_scatter(
        jnp.concatenate([matmul_tn(flattened, d_rows), matmul_tn(d_branch, mixed_rows)], axis=1),
        ("dp", "seq"),
        scatter_dimension=0,
        tiled=True,
    )
    scaled = summed / divisor
    return (scaled[:, :packed_cols], scaled[:, packed_cols:])


def local(latents, cotangent, modulation, spatial_qkv, spatial_out, temporal_qkv, temporal_out):
    clips_here = latents.shape[0]
    channels = latents.shape[-1]
    pieces = modulation.reshape(clips_here, 6, 1, 1, channels)
    hidden, spatial_saved = sublayer_forward(
        latents, pieces[:, 0], pieces[:, 1], pieces[:, 2], spatial_qkv, spatial_out
    )
    widened = hidden.astype(jnp.float32)
    modulated, norm_back = jax.vjp(norm_modulate, widened, pieces[:, 3], pieces[:, 4])
    flattened = modulated.reshape(-1, channels)
    packed = matmul(flattened, temporal_qkv).astype(jnp.bfloat16).reshape(hidden.shape[:3] + (-1,))
    upstream = cotangent.astype(jnp.float32)
    d_branch = (pieces[:, 5] * upstream).astype(jnp.bfloat16).reshape(-1, channels)
    d_mixed = matmul(d_branch, temporal_out).astype(jnp.bfloat16).reshape(hidden.shape[:3] + (-1,))
    attended_pos, core_back = jax.vjp(
        partial(attend, over_frames=True),
        lax.all_to_all(packed, "seq", split_axis=2, concat_axis=1, tiled=True),
    )
    (d_pos,) = core_back(lax.all_to_all(d_mixed, "seq", split_axis=2, concat_axis=1, tiled=True))
    attended_pos, d_packed_pos = (attended_pos, d_pos)
    attended, d_packed = (
        lax.all_to_all(attended_pos, "seq", split_axis=1, concat_axis=2, tiled=True),
        lax.all_to_all(d_packed_pos, "seq", split_axis=1, concat_axis=2, tiled=True),
    )
    mixed_rows = attended.reshape(-1, attended.shape[-1])
    branch = matmul_nt(mixed_rows, temporal_out)
    d_gate = jnp.sum(
        (upstream.reshape(-1, channels) * branch).reshape(clips_here, -1, channels), axis=1
    )
    d_rows = d_packed.reshape(-1, d_packed.shape[-1])
    d_modulated = matmul_nt(d_rows, temporal_qkv).astype(jnp.bfloat16).reshape(upstream.shape)
    d_signal, d_offset, d_stretch = norm_back(d_modulated)
    temporal_moments = jnp.stack(
        [d_offset.reshape(clips_here, channels), d_stretch.reshape(clips_here, channels), d_gate],
        axis=1,
    )
    temporal_terms = (flattened, d_rows, d_branch, mixed_rows)
    grad_hidden = (upstream + d_signal).astype(jnp.bfloat16)
    divisor = clips_here * lax.axis_size("dp")
    temporal_dqkv, temporal_dout = reduce_terms(temporal_terms, divisor)
    grad_field, spatial_moments, spatial_terms = sublayer_backward(
        spatial_saved, grad_hidden, pieces[:, 2], spatial_qkv, spatial_out
    )
    grad_latents = grad_field.astype(jnp.bfloat16)
    spatial_dqkv, spatial_dout = reduce_terms(spatial_terms, divisor)
    grad_modulation = lax.psum(jnp.concatenate([spatial_moments, temporal_moments], axis=1), "seq")
    return (grad_latents, grad_modulation, spatial_dqkv, spatial_dout, temporal_dqkv, temporal_dout)


def solution(mesh):
    in_specs = (
        P("dp", "seq", None, None),
        P("dp", "seq", None, None),
        P("dp", None, None),
        P(),
        P(),
        P(),
        P(),
    )
    out_specs = (
        P("dp", "seq", None, None),
        P("dp", None, None),
        P(("dp", "seq"), None),
        P(("dp", "seq"), None),
        P(("dp", "seq"), None),
        P(("dp", "seq"), None),
    )
    return jax.shard_map(local, mesh=mesh, in_specs=in_specs, out_specs=out_specs, check_vma=False)
```

profile of v0, /device:TPU:5, one launch (start us, length us, event | category | flops | bytes accessed | tf_op | source)
XLA Modules:
  0.0 415.5 jit_solution(12729692855603111059)
XLA Ops:
  15.8 7.3 %all-to-all-start = ((bf16[16,2,4608]{2,1,0:T(2,128)(2,1)}), bf16[16,2,4608]{2,1,0:T(2,128)(2,1)}, u32[]{:S(2)}, u32[]{:S(2)}) async-start(bf16[16,2,4608]{2,1,0:T(2,128)(2,1)} %reshape.450), calls=%async_computation | async-start | bytes 589824 | tf_op jit(solution)/shard_map/all_to_all | solution.py:132
  24.2 3.6 convolution_convert_fusion.1
  35.9 5.0 %copy.48 = bf16[1,1,256,1728]{3,1,0,2:T(2,128)(2,1)} copy(bf16[1,1,256,1728]{2,3,1,0:T(8,128)(2,1)} %fusion.2) | data formatting | bytes 1769472 | tf_op jit(solution)/shard_map/reshape | solution.py:124
  40.9 8.4 %reduce.42 = bf16[256,1728]{1,0:T(8,128)(2,1)} reduce(bf16[256,1,1,1728]{3,2,1,0:T(2,128)(2,1)} %bitcast.190, bf16[]{:T(256)} %broadcast.220), dimensions={1,2}, to_apply=%bitcast.148.reduce_sub_computation | reduce | bytes 1769474
  49.3 4.0 reshape.448
  53.3 5.7 %all-to-all-start.1 = ((bf16[16,2,13824]{2,1,0:T(2,128)(2,1)}), bf16[16,2,13824]{2,1,0:T(2,128)(2,1)}, u32[]{:S(2)}, u32[]{:S(2)}) async-start(bf16[16,2,13824]{2,1,0:T(2,128)(2,1)} %reshape.448), calls=%async_computation.1 | async-start | bytes 1769472 | tf_op jit(solution)/shard_map/all_to_all | solution.py:130
  62.3 3.7 bitcast_reduce_fusion.1
  68.3 4.9 %all-to-all-done.1 = bf16[16,2,13824]{2,1,0:T(2,128)(2,1)} async-done(((bf16[16,2,13824]{2,1,0:T(2,128)(2,1)}), bf16[16,2,13824]{2,1,0:T(2,128)(2,1)}, u32[]{:S(2)}, u32[]{:S(2)}) %all-to-all-start.1) | async-done | bytes 884768 | tf_op jit(solution)/shard_map/all_to_all | solution.py:130
  73.2 6.0 %reshape.449 = bf16[256,1,1,1728]{3,2,1,0:T(2,128)(2,1)} reshape(bf16[16,2,13824]{2,1,0:T(2,128)(2,1)} %all-to-all-done.1) | data formatting | bytes 1769472
  79.2 7.6 %bitcast_reduce_fusion = bf16[256,1728]{1,0:T(8,128)(2,1)} fusion(bf16[256,1,1,1728]{3,2,1,0:T(2,128)(2,1)} %reshape.449), kind=kLoop, calls=%fused_computation.145 | loop fusion | bytes 1769472 | tf_op jit(solution)/shard_map/all_to_all | solution.py:130
  86.8 4.0 reshape.423
  100.5 4.8 %all-to-all-start.3 = ((bf16[1,16,16,576]{3,2,0,1:T(8,128)(2,1)}), bf16[1,16,16,576]{3,2,0,1:T(8,128)(2,1)}, u32[]{:S(2)}, u32[]{:S(2)}) async-start(bf16[1,16,16,576]{3,2,0,1:T(8,128)(2,1)} %bitcast.202), calls=%async_computation.3 | async-start | bytes 655360 | tf_op jit(solution)/shard_map/all_to_all | solution.py:135
  109.2 3.6 reshape.427
  113.2 5.5 %all-to-all-start.2 = ((bf16[1,16,16,1728]{3,2,0,1:T(8,128)(2,1)}), bf16[1,16,16,1728]{3,2,0,1:T(8,128)(2,1)}, u32[]{:S(2)}, u32[]{:S(2)}) async-start(bf16[1,16,16,1728]{3,2,0,1:T(8,128)(2,1)} %bitcast.193), calls=%async_computation.2 | async-start | bytes 1835008 | tf_op jit(solution)/shard_map/all_to_all | solution.py:136
  120.0 3.3 fusion.58
  123.3 9.8 %all-to-all-done.2 = bf16[1,16,16,1728]{3,2,0,1:T(8,128)(2,1)} async-done(((bf16[1,16,16,1728]{3,2,0,1:T(8,128)(2,1)}), bf16[1,16,16,1728]{3,2,0,1:T(8,128)(2,1)}, u32[]{:S(2)}, u32[]{:S(2)}) %all-to-all-start.2) | async-done | bytes 884768 | tf_op jit(solution)/shard_map/all_to_all | solution.py:136
  133.1 3.9 fusion.33
  146.4 5.8 %fusion.77 = f32[1152,1728]{0,1:T(8,128)} fusion(bf16[256,1728]{1,0:T(8,128)(2,1)} %bitcast.30, bf16[1,1,256,1152]{3,2,1,0:T(8,128)(2,1)S(1)} %get-tuple-element.39, f32[1152]{0:T(1024)S(1)} %copy-done.24, f32[1152]{0:T(1024)S(1)} %copy-done.20, f32[256]{0:T(256)S(1)} %copy-done.32, f32[256]{0:T(256)S(1)} %copy-done.30), kind=kOutput, calls=%fused_computation.139 | convolution fusion | flops 1020985344 | bytes 9448448 | tf_op jit(solution)/shard_map/dot_general | solution.py:34
  152.9 4.6 %fusion.74 = f32[1152,1728]{0,1:T(8,128)} fusion(bf16[256,1728]{0,1:T(8,128)(2,1)S(1)} %bitcast.191, bf16[1,1,256,1152]{3,2,1,0:T(8,128)(2,1)S(1)} %copy-done.2, f32[1152]{0:T(1024)S(1)} %copy-done.34, f32[1152]{0:T(1024)S(1)} %copy-done.22, f32[256]{0:T(256)S(1)} %copy-done.43, f32[256]{0:T(256)S(1)} %copy-done.41), kind=kOutput, calls=%fused_computation.138 | convolution fusion | flops 1020985344 | bytes 9448448 | tf_op jit(solution)/shard_map/dot_general | solution.py:34
  157.5 8.8 %pad_maximum_fusion = f32[1152,2304]{0,1:T(8,128)} fusion(f32[1152,576]{0,1:T(8,128)} %fusion.61, f32[1152,1728]{0,1:T(8,128)} %fusion.74), kind=kLoop, calls=%fused_computation | loop fusion | flops 2654208 | bytes 21233664 | tf_op jit(solution)/shard_map/concatenate | solution.py:105
  166.3 8.6 %pad_maximum_fusion.1 = f32[1152,2304]{0,1:T(8,128)} fusion(f32[1152,576]{0,1:T(8,128)} %fusion.58, f32[1152,1728]{0,1:T(8,128)} %fusion.77), kind=kLoop, calls=%fused_computation.1 | loop fusion | flops 2654208 | bytes 21233664 | tf_op jit(solution)/shard_map/concatenate | solution.py:105
  178.1 3.6 fusion.37
  183.1 51.1 %psum.7 = f32[1,6,1152]{2,0,1:T(1,128)} all-reduce(f32[1,6,1152]{2,0,1:T(1,128)S(1)} %constant_dynamic-update-slice_fusion), channel_id=1, replica_groups=mesh['dp'=8,'seq'=16] {'seq'}, use_global_device_ids=true, to_apply=%region_18.0 | all-reduce | flops 6912 | bytes 55296 | tf_op jit(solution)/shard_map/psum | solution.py:159
  235.4 164.3 %all-reduce.11.cloned.1.call-done = (f32[1152,2304]{0,1:T(8,128)}, f32[1152,2304]{0,1:T(8,128)}) async-done(((f32[1152,2304]{0,1:T(8,128)}, f32[1152,2304]{0,1:T(8,128)}), (f32[1152,2304]{0,1:T(8,128)}, f32[1152,2304]{0,1:T(8,128)})) %all-reduce.11.cloned.1.call-update) | async-done | bytes 21233680
  (169 shorter events, 62.8 us)
Async XLA Ops:
  7.2 22.8 %copy-start = (bf16[1152,576]{0,1:T(8,128)(2,1)S(1)}, bf16[1152,576]{0,1:T(8,128)(2,1)}, u32[]{:S(2)}) copy-start(bf16[1152,576]{0,1:T(8,128)(2,1)} %param.11) | copy-start | bytes 3981316
  8.7 15.4 %copy-start.21 = (f32[1152]{0:T(1024)}, f32[1152]{0:T(1024)S(1)}, u32[]{:S(2)}) copy-start(f32[1152]{0:T(1024)S(1)} %get-tuple-element.32) | copy-start | bytes 13828
  8.7 15.4 %copy-start.33 = (f32[1152]{0:T(1024)}, f32[1152]{0:T(1024)S(1)}, u32[]{:S(2)}) copy-start(f32[1152]{0:T(1024)S(1)} %get-tuple-element.31) | copy-start | bytes 13828
  11.5 11.7 %copy-start.2 = (bf16[1,1,256,1152]{3,2,1,0:T(8,128)(2,1)S(1)}, bf16[1,1,256,1152]{3,2,1,0:T(8,128)(2,1)}, u32[]{:S(2)}) copy-start(bf16[1,1,256,1152]{3,2,1,0:T(8,128)(2,1)} %param.7) | copy-start | bytes 1769476
  15.8 37.5 %all-to-all-start = ((bf16[16,2,4608]{2,1,0:T(2,128)(2,1)}), bf16[16,2,4608]{2,1,0:T(2,128)(2,1)}, u32[]{:S(2)}, u32[]{:S(2)}) async-start(bf16[16,2,4608]{2,1,0:T(2,128)(2,1)} %reshape.450), calls=%async_computation | async-start | bytes 589824 | tf_op jit(solution)/shard_map/all_to_all | solution.py:132
  23.3 4.5 %copy-start.40 = (f32[256]{0:T(256)}, f32[256]{0:T(256)S(1)}, u32[]{:S(2)}) copy-start(f32[256]{0:T(256)S(1)} %broadcast_multiply_fusion.1) | copy-start | bytes 3076
  23.6 4.1 copy-start.42
  30.0 2.1 copy-start.9
  30.4 3.1 copy-start.19
  30.4 3.1 copy-start.23
  30.4 3.1 copy-start.48
  53.3 19.9 %all-to-all-start.1 = ((bf16[16,2,13824]{2,1,0:T(2,128)(2,1)}), bf16[16,2,13824]{2,1,0:T(2,128)(2,1)}, u32[]{:S(2)}, u32[]{:S(2)}) async-start(bf16[16,2,13824]{2,1,0:T(2,128)(2,1)} %reshape.448), calls=%async_computation.1 | async-start | bytes 1769472 | tf_op jit(solution)/shard_map/all_to_all | solution.py:130
  93.1 3.8 copy-start.8
  93.1 3.7 copy-start.18
  100.5 12.7 %all-to-all-start.3 = ((bf16[1,16,16,576]{3,2,0,1:T(8,128)(2,1)}), bf16[1,16,16,576]{3,2,0,1:T(8,128)(2,1)}, u32[]{:S(2)}, u32[]{:S(2)}) async-start(bf16[1,16,16,576]{3,2,0,1:T(8,128)(2,1)} %bitcast.202), calls=%async_computation.3 | async-start | bytes 655360 | tf_op jit(solution)/shard_map/all_to_all | solution.py:135
  113.2 20.0 %all-to-all-start.2 = ((bf16[1,16,16,1728]{3,2,0,1:T(8,128)(2,1)}), bf16[1,16,16,1728]{3,2,0,1:T(8,128)(2,1)}, u32[]{:S(2)}, u32[]{:S(2)}) async-start(bf16[1,16,16,1728]{3,2,0,1:T(8,128)(2,1)} %bitcast.193), calls=%async_computation.2 | async-start | bytes 1835008 | tf_op jit(solution)/shard_map/all_to_all | solution.py:136
  118.6 281.1 %all-reduce.11.cloned.1.call-start = ((), (), s32[]{:S(2)}) async-start(), calls=%async_computation.4 | async-start | bytes 42467328
  133.1 3.9 copy-start.47
  133.1 3.9 copy-start.20
  133.1 3.9 copy-start.30
  133.1 3.9 copy-start.32
  139.7 4.1 copy-start.5
  182.0 52.1 %copy-start.6 = (bf16[1,1,256,1152]{3,2,1,0:T(8,128)(2,1)S(1)}, bf16[1,1,256,1152]{3,2,1,0:T(8,128)(2,1)}, u32[]{:S(2)}) copy-start(bf16[1,1,256,1152]{3,2,1,0:T(8,128)(2,1)} %copy-done.5) | copy-start | bytes 1769476
  403.8 4.6 %copy-start.1 = (bf16[1152,576]{0,1:T(8,128)(2,1)S(1)}, bf16[1152,576]{0,1:T(8,128)(2,1)}, u32[]{:S(2)}) copy-start(bf16[1152,576]{0,1:T(8,128)(2,1)} %param.11) | copy-start | bytes 3981316
  (30 other events, 34.9 us)
Sparse Core Ops, SparseCore 0:
  175.1 224.5 all-reduce.10
where the time goes:
time: 422 us; the launch traced here: 416 us
  waiting for transfers between devices  179 us (42%)
  local copies, waits for them, and re-layouts  61 us (14%)
  blocking collectives  51.1 us (12%)
  matrix products  45.6 us (11%)
  other arithmetic  40.4 us (10%)
  starting transfers between devices  23.4 us (6%)
  between operations  14.9 us (4%)
    unnamed x2, waiting for transfers between devices  164 us
    psum x1, blocking collectives, local(): lax.psum(jnp.concatenate([spatial_moments, temporal_moments], axis=1), 's...  51.1 us
    unnamed x112, local copies, waits for them, and re-layouts  26.9 us
    concatenate x2, other arithmetic, reduce_terms(): jnp.concatenate([matmul_tn(flattened, d_rows), matmul_tn(d_branch, mixed_...  17.4 us
    dot_general x4, matrix products, matmul_tn(): lax.dot_general(former, latter, (((0,), (0,)), ((), ())), preferred_eleme...  15.8 us
    dot_general x4, matrix products, matmul_nt(): lax.dot_general(former, latter, (((1,), (1,)), ((), ())), preferred_eleme...  11.3 us
    unnamed x2, other arithmetic  11.1 us
    all_to_all x1, waiting for transfers between devices, local(): lax.all_to_all(d_packed_pos, 'seq', split_axis=1, concat_axis=2, tiled=True)  9.85 us
  transfers between devices with their start and end apart: 5, of which 4 were waited for; matrix products, arithmetic and copies ran while one was open for 13% of the time, Pallas kernels for 0%

commit v1 on v0

v1 whole, which is shorter than its diff:
```python
import functools

import jax
import jax.numpy as jnp
from jax import lax
from jax.experimental import pallas as pl
from jax.experimental.pallas import tpu as pltpu
from jax.sharding import PartitionSpec as P

HEADS = 8
HEAD_DIM = 72
HE = HEADS * HEAD_DIM
PACKED = 3 * HE
D = 1152
TOKENS = 256
SEQ = 16
EPSILON = 1e-06
FACTOR = HEAD_DIM**-0.5
MESH = pl.DeviceIdType.MESH
F32 = jnp.float32
BF16 = jnp.bfloat16

NN = (((1,), (0,)), ((), ()))
NT = (((1,), (1,)), ((), ()))
TN = (((0,), (0,)), ((), ()))


def dot(a, b, dims=NN):
    return lax.dot_general(a, b, dims, preferred_element_type=F32)


def rows_of(i, size):
    return pl.ds(pl.multiple_of(i * size, size), size)


def normalise(source, mod, row, normed, scale, modulated):
    offset = mod[row : row + 1, :]
    stretch = 1.0 + mod[row + 1 : row + 2, :]

    def body(i, _):
        rows = rows_of(i, 32)
        x = source[rows, :].astype(F32)
        centred = x - jnp.mean(x, axis=-1, keepdims=True)
        spread = jnp.mean(centred * centred, axis=-1, keepdims=True)
        inverse = lax.rsqrt(spread + EPSILON)
        n = centred * inverse
        normed[rows, :] = n
        scale[rows, :] = inverse
        modulated[rows, :] = (n * stretch + offset).astype(BF16)
        return 0

    lax.fori_loop(0, TOKENS // 32, body, 0)


def project(modulated, weight, packed):
    def body(i, _):
        cols = rows_of(i, 256)
        packed[:, cols] = dot(modulated[...], weight[:, cols]).astype(BF16)
        return 0

    lax.fori_loop(0, 6, body, 0)
    packed[:, 1536:PACKED] = dot(modulated[...], weight[:, 1536:PACKED]).astype(BF16)


def project_back(rows_in, weight, out, width):
    def body(i, _):
        cols = rows_of(i, 384)
        out[:, cols] = dot(rows_in[...], weight[cols, :], NT).astype(out.dtype)
        return 0

    lax.fori_loop(0, width // 384, body, 0)


def head(ref, h, section=0):
    lane = section * HE + h * HEAD_DIM
    return ref[:, lane : lane + HEAD_DIM]


def probabilities(packed, h, mask):
    scores = dot(head(packed, h, 0), head(packed, h, 1), NT)
    raised = jnp.exp(scores * FACTOR)
    if mask is not None:
        raised = jnp.where(mask, raised, 0.0)
    return raised / jnp.sum(raised, axis=-1, keepdims=True)


def head_backward(probs, weights, packed, d_attended, h, d_packed):
    d_head = head(d_attended, h)
    d_weights = dot(d_head, head(packed, h, 2), NT)
    carried = jnp.sum(d_weights * probs, axis=-1, keepdims=True)
    d_scores = (probs * (d_weights - carried) * FACTOR).astype(BF16)
    lane = h * HEAD_DIM
    d_packed[:, lane : lane + HEAD_DIM] = dot(d_scores, head(packed, h, 1)).astype(BF16)
    d_packed[:, HE + lane : HE + lane + HEAD_DIM] = dot(d_scores, head(packed, h, 0), TN).astype(BF16)
    d_packed[:, 2 * HE + lane : 2 * HE + lane + HEAD_DIM] = dot(weights, d_head, TN).astype(BF16)


def fold(x):
    return sum(x[8 * i : 8 * i + 8] for i in range(x.shape[0] // 8))


def gated(source, mod, row, out):
    gate = mod[row : row + 1, :]

    def body(i, _):
        rows = rows_of(i, 32)
        out[rows, :] = (source[rows, :].astype(F32) * gate).astype(BF16)
        return 0

    lax.fori_loop(0, TOKENS // 32, body, 0)


def gate_sum(upstream, branch):
    def body(i, total):
        rows = rows_of(i, 32)
        return total + fold(upstream[rows, :].astype(F32) * branch[rows, :])

    total = lax.fori_loop(0, TOKENS // 32, body, jnp.zeros((8, D), F32))
    return jnp.sum(total, axis=0, keepdims=True)


def normalise_back(d_modulated, normed, scale, mod, row, upstream, out, after):
    stretch = 1.0 + mod[row + 1 : row + 2, :]

    def body(i, totals):
        rows = rows_of(i, 16)
        g = d_modulated[rows, :].astype(F32)
        n = normed[rows, :]
        dn = g * stretch
        gn = g * n
        first = jnp.mean(dn, axis=-1, keepdims=True)
        second = jnp.mean(dn * n, axis=-1, keepdims=True)
        dx = scale[rows, :] * (dn - first - n * second)
        out[rows, :] = (upstream[rows, :].astype(F32) + dx).astype(BF16)
        after(i)
        return totals[0] + fold(g), totals[1] + fold(gn)

    zero = jnp.zeros((8, D), F32)
    totals = lax.fori_loop(0, TOKENS // 16, body, (zero, zero))
    return tuple(jnp.sum(t, axis=0, keepdims=True) for t in totals)


def weight_gradient(left, right, flipped, out, width):
    def turn(i, _):
        cols = rows_of(i, 128)
        flipped[cols, :] = left[:, cols].T
        return 0

    lax.fori_loop(0, D // 128, turn, 0)

    def body(i, _):
        rows = rows_of(i, 128)
        out[rows, :] = dot(flipped[rows, :], right[...]).astype(BF16)
        return 0

    lax.fori_loop(0, D // 128, body, 0)


class Exchange:
    def __init__(self, source, target, send, recv):
        self.source, self.target, self.send, self.recv = source, target, send, recv
        self.me = lax.axis_index("seq")

    def to(self, j):
        peer = lax.rem(self.me + j, SEQ)
        return pltpu.make_async_remote_copy(
            src_ref=self.source.at[rows_of(peer, 16)],
            dst_ref=self.target.at[rows_of(self.me, 16)],
            send_sem=self.send.at[j],
            recv_sem=self.recv.at[j],
            device_id={"seq": peer},
            device_id_type=MESH,
        )

    def start(self, j):
        self.to(j).start()

    def wait_recv(self):
        def body(j, _):
            sender = lax.rem(self.me + SEQ - j, SEQ)
            pltpu.make_async_remote_copy(
                src_ref=self.source.at[rows_of(sender, 16)],
                dst_ref=self.target.at[rows_of(sender, 16)],
                send_sem=self.send.at[j],
                recv_sem=self.recv.at[j],
                device_id={"seq": sender},
                device_id_type=MESH,
            ).wait_recv()
            return 0

        lax.fori_loop(1, SEQ, body, 0)

    def wait_send(self):
        def body(j, _):
            self.to(j).wait_send()
            return 0

        lax.fori_loop(1, SEQ, body, 0)


def kernel(
    lat_hbm, cot_hbm, mod_hbm, wqs_hbm, wos_hbm, wqt_hbm, wot_hbm,
    grad_latents, moments, dqkv_s, dout_s, dqkv_t, dout_t,
    lat, cot, mod, wqs, wos, wqt, wot,
    normed_s, scale_s, modulated_s, packed_s, probs_s, attended_s, branch_s,
    normed_t, scale_t, modulated_t, packed_t, attended_t, branch_t,
    hidden_out, hidden, grad_out, grad_hidden,
    d_branch_s, d_branch_t, d_attended, d_packed_s, d_packed_t, d_modulated, flipped,
    load_sem, send_sem, recv_sem,
):
    me = lax.axis_index("seq")
    loads = [
        pltpu.make_async_copy(src, dst, load_sem.at[i])
        for i, (src, dst) in enumerate(
            [
                (lat_hbm, lat), (mod_hbm, mod), (wqs_hbm, wqs), (wot_hbm, wot),
                (wos_hbm, wos), (wqt_hbm, wqt),
                (cot_hbm.at[rows_of(me, 16)], cot.at[rows_of(me, 16)]),
            ]
        )
    ]
    for load in loads:
        load.start()

    barrier = pltpu.get_barrier_semaphore()

    def greet(j, _):
        pl.semaphore_signal(
            barrier, inc=1, device_id={"seq": lax.rem(me + j, SEQ)}, device_id_type=MESH
        )
        return 0

    lax.fori_loop(1, SEQ, greet, 0)
    loads[0].wait()
    loads[1].wait()
    normalise(lat, mod, 0, normed_s, scale_s, modulated_s)
    pl.semaphore_wait(barrier, SEQ - 1)

    cot_trip = Exchange(cot_hbm, cot, send_sem.at[0], recv_sem.at[0])
    hidden_trip = Exchange(hidden_out, hidden, send_sem.at[1], recv_sem.at[1])
    grad_trip = Exchange(grad_out, grad_hidden, send_sem.at[2], recv_sem.at[2])

    def send_cot(j, _):
        cot_trip.start(j)
        return 0

    lax.fori_loop(1, SEQ, send_cot, 0)

    loads[2].wait()
    project(modulated_s, wqs, packed_s)
    for h in range(HEADS):
        probs = probabilities(packed_s, h, None)
        probs_s[h] = probs
        lane = h * HEAD_DIM
        attended_s[:, lane : lane + HEAD_DIM] = dot(probs.astype(BF16), head(packed_s, h, 2)).astype(BF16)
    loads[4].wait()
    project_back(attended_s, wos, branch_s, D)

    gate_s = mod[2:3, :]

    def make_hidden(j, _):
        peer = lax.rem(me + j, SEQ)
        rows = rows_of(peer, 16)
        value = (lat[rows, :].astype(F32) + gate_s * branch_s[rows, :]).astype(BF16)
        hidden_out[rows, :] = value

        @pl.when(j < SEQ)
        def _():
            hidden_trip.start(j)

        return 0

    lax.fori_loop(1, SEQ + 1, make_hidden, 0)
    hidden[rows_of(me, 16), :] = hidden_out[rows_of(me, 16), :]

    loads[6].wait()
    cot_trip.wait_recv()
    loads[3].wait()
    gated(cot, mod, 5, d_branch_t)
    d_attended[...] = dot(d_branch_t[...], wot[...]).astype(BF16)
    hidden_trip.wait_recv()
    normalise(hidden, mod, 3, normed_t, scale_t, modulated_t)
    loads[5].wait()
    project(modulated_t, wqt, packed_t)
    patch_row = lax.rem(lax.broadcasted_iota(jnp.int32, (TOKENS, TOKENS), 0), 16)
    patch_col = lax.rem(lax.broadcasted_iota(jnp.int32, (TOKENS, TOKENS), 1), 16)
    mask = patch_row == patch_col
    for h in range(HEADS):
        probs = probabilities(packed_t, h, mask)
        weights = probs.astype(BF16)
        lane = h * HEAD_DIM
        attended_t[:, lane : lane + HEAD_DIM] = dot(weights, head(packed_t, h, 2)).astype(BF16)
        head_backward(probs, weights, packed_t, d_attended, h, d_packed_t)
    project_back(d_packed_t, wqt, d_modulated, D)

    def send_grad(i):
        @pl.when(i != me)
        def _():
            grad_trip.start(lax.rem(i + SEQ - me, SEQ))

    d_offset, d_stretch = normalise_back(
        d_modulated, normed_t, scale_t, mod, 3, cot, grad_out, send_grad
    )
    moments[3:4, :] = d_offset
    moments[4:5, :] = d_stretch
    grad_hidden[rows_of(me, 16), :] = grad_out[rows_of(me, 16), :]
    project_back(attended_t, wot, branch_t, D)
    moments[5:6, :] = gate_sum(cot, branch_t)
    weight_gradient(modulated_t, d_packed_t, flipped, dqkv_t, PACKED)
    weight_gradient(d_branch_t, attended_t, flipped, dout_t, HE)

    grad_trip.wait_recv()
    gated(grad_hidden, mod, 2, d_branch_s)
    moments[2:3, :] = gate_sum(grad_hidden, branch_s)
    d_attended[...] = dot(d_branch_s[...], wos[...]).astype(BF16)
    for h in range(HEADS):
        probs = probs_s[h]
        head_backward(probs, probs.astype(BF16), packed_s, d_attended, h, d_packed_s)
    project_back(d_packed_s, wqs, d_modulated, D)
    d_offset, d_stretch = normalise_back(
        d_modulated, normed_s, scale_s, mod, 0, grad_hidden, grad_latents, lambda i: None
    )
    moments[0:1, :] = d_offset
    moments[1:2, :] = d_stretch
    moments[6:8, :] = jnp.zeros((2, D), F32)
    weight_gradient(modulated_s, d_packed_s, flipped, dqkv_s, PACKED)
    weight_gradient(d_branch_s, attended_s, flipped, dout_s, HE)
    cot_trip.wait_send()
    hidden_trip.wait_send()
    grad_trip.wait_send()


def local(latents, cotangent, modulation, spatial_qkv, spatial_out, temporal_qkv, temporal_out):
    vm = pl.BlockSpec(memory_space=pltpu.VMEM)
    hbm = pl.BlockSpec(memory_space=pl.ANY)
    sds = jax.ShapeDtypeStruct
    wide = pltpu.VMEM((TOKENS, D), BF16)
    wide32 = pltpu.VMEM((TOKENS, D), F32)
    narrow = pltpu.VMEM((TOKENS, HE), BF16)
    three = pltpu.VMEM((TOKENS, PACKED), BF16)
    column = pltpu.VMEM((TOKENS, 1), F32)
    wq = pltpu.VMEM((D, PACKED), BF16)
    wo = pltpu.VMEM((D, HE), BF16)
    outs = pl.pallas_call(
        kernel,
        out_shape=[
            sds((TOKENS, D), BF16),
            sds((8, D), F32),
            sds((D, PACKED), BF16),
            sds((D, HE), BF16),
            sds((D, PACKED), BF16),
            sds((D, HE), BF16),
        ],
        in_specs=[hbm] * 7,
        out_specs=[vm] * 6,
        scratch_shapes=[
            wide, wide, pltpu.VMEM((6, D), F32), wq, wo, wq, wo,
            wide32, column, wide, three, pltpu.VMEM((HEADS, TOKENS, TOKENS), F32), narrow, wide32,
            wide32, column, wide, three, narrow, wide32,
            wide, wide, wide, wide,
            wide, wide, narrow, three, three, wide, pltpu.VMEM((D, TOKENS), BF16),
            pltpu.SemaphoreType.DMA((7,)),
            pltpu.SemaphoreType.DMA((3, SEQ)),
            pltpu.SemaphoreType.DMA((3, SEQ)),
        ],
        compiler_params=pltpu.CompilerParams(
            collective_id=0, has_side_effects=True, vmem_limit_bytes=62 * 2**20
        ),
    )(
        latents.reshape(TOKENS, D), cotangent.reshape(TOKENS, D), modulation.reshape(6, D),
        spatial_qkv, spatial_out, temporal_qkv, temporal_out,
    )
    grad, moments, dqkv_s, dout_s, dqkv_t, dout_t = outs
    grad_modulation = lax.psum(moments[:6], "seq")[None]

    def reduce(x):
        return lax.psum_scatter(x, ("dp", "seq"), scatter_dimension=0, tiled=True).astype(F32) / 8

    return (grad.reshape(latents.shape), grad_modulation, reduce(dqkv_s), reduce(dout_s), reduce(dqkv_t), reduce(dout_t))


def solution(mesh):
    in_specs = (
        P("dp", "seq", None, None),
        P("dp", "seq", None, None),
        P("dp", None, None),
        P(),
        P(),
        P(),
        P(),
    )
    out_specs = (
        P("dp", "seq", None, None),
        P("dp", None, None),
        P(("dp", "seq"), None),
        P(("dp", "seq"), None),
        P(("dp", "seq"), None),
        P(("dp", "seq"), None),
    )
    return jax.shard_map(local, mesh=mesh, in_specs=in_specs, out_specs=out_specs, check_vma=False)
```

time: 422 us -> 269 us (0.64)
  waiting for transfers between devices: 179 us -> 113 us
  Pallas kernels: 0 us -> 63.8 us
  matrix products: 45.6 us -> 0 us
  local copies, waits for them, and re-layouts: 61 us -> 19.2 us
  other arithmetic: 40.4 us -> 3.06 us
  starting transfers between devices: 23.4 us -> 0.04 us
    pallas_call x0 -> x1, Pallas kernels: none -> 63.8 us  [local(): pl.pallas_call(kernel, out_shape=[sds((TOKENS, D), BF16), sds((8, D), F32...]
    unnamed x2, waiting for transfers between devices: 164 us -> 113 us
    dot_general x24 -> x0, matrix products: 45.6 us -> none  [the longest x4 15.8 us: matmul_tn(): lax.dot_general(former, latter, (((0,), (0,)), ((), ())), preferred_eleme...]
    all_to_all x4 -> x0, starting transfers between devices: 23.3 us -> none  [the longest x1 7.33 us: local(): lax.all_to_all(d_mixed, 'seq', split_axis=2, concat_axis=1, tiled=True)]
    concatenate x2 -> x0, other arithmetic: 17.4 us -> none  [reduce_terms(): jnp.concatenate([matmul_tn(flattened, d_rows), matmul_tn(d_branch, mixed_...]
    reshape x5 -> x0, local copies, waits for them, and re-layouts: 15.5 us -> none  [the longest x2 7.59 us: attend(): stacked = packed.reshape(leading + (3, HEADS, HEAD_DIM))]
    all_to_all x4 -> x0, waiting for transfers between devices: 15 us -> none  [the longest x1 9.85 us: local(): lax.all_to_all(d_packed_pos, 'seq', split_axis=1, concat_axis=2, tiled=True)]
    all_to_all x2 -> x0, local copies, waits for them, and re-layouts: 11.3 us -> none  [the longest x1 7.63 us: local(): lax.all_to_all(packed, 'seq', split_axis=2, concat_axis=1, tiled=True)]
  transfers between devices with their start and end apart: 5 -> 1, of which waited for: 4 -> 1; matrix products, arithmetic and copies ran while one was open for 13% -> 0% of each run, Pallas kernels for 0% -> 0%
where the time goes in v1:
time: 269 us; the launch traced here: 267 us
  waiting for transfers between devices  113 us (42%)
  Pallas kernels  63.8 us (24%)
  blocking collectives  53.2 us (20%)
  local copies, waits for them, and re-layouts  19.2 us (7%)
  between operations  14.1 us (5%)
  other arithmetic  3.06 us (1%)
    unnamed x2, waiting for transfers between devices  113 us
    pallas_call x1, Pallas kernels, local(): pl.pallas_call(kernel, out_shape=[sds((TOKENS, D), BF16), sds((8, D), F32...  63.8 us
    psum x1, blocking collectives, local(): grad_modulation = lax.psum(moments[:6], 'seq')[None]  53.2 us
    unnamed x17, local copies, waits for them, and re-layouts  19.2 us
  transfers between devices with their start and end apart: 1, of which 1 were waited for; matrix products, arithmetic and copies ran while one was open for 0% of the time, Pallas kernels for 0%

profile of v1, /device:TPU:5, one launch (start us, length us, event | category | flops | bytes accessed | tf_op | source)
XLA Modules:
  0.0 266.7 jit_solution(10848140163297100334)
XLA Ops:
  7.2 0.0 all-reduce.7.cloned.1.call-start
  7.2 6.5 %copy.18.wqs_hbm = bf16[1152,1728]{1,0:T(8,128)(2,1)} copy(bf16[1152,1728]{0,1:T(8,128)(2,1)} %param.10) | data formatting | bytes 7962624 | tf_op args[3]
  13.7 0.0 copy-start
  13.7 0.0 copy-start.1
  13.7 6.6 %copy.20.wqt_hbm = bf16[1152,1728]{1,0:T(8,128)(2,1)} copy(bf16[1152,1728]{0,1:T(8,128)(2,1)} %param.12) | data formatting | bytes 7962624 | tf_op args[5]
  20.3 0.0 copy-done
  20.3 0.0 copy-start.4
  20.3 1.6 copy.19.wos_hbm
  21.9 0.0 copy-done.1
  22.0 1.6 copy.21.wot_hbm
  23.6 0.0 copy-done.4
  23.6 0.6 copy.25
  24.2 63.8 %shard_map.118 = (bf16[256,1152]{1,0:T(8,128)(2,1)}, f32[8,1152]{1,0:T(8,128)}, bf16[1152,1728]{1,0:T(8,128)(2,1)}, bf16[1152,576]{1,0:T(8,128)(2,1)}, bf16[1152...) custom-call(bf16[256,1152]{1,0:T(8,128)(2,1)} %bitcast.8, bf16[256,1152]{1,0:T(8,128)(2,1)} %bitcast.9, f32[6,1152]{1,0:T(8,128)} %bitcast.11, ...), custom_call_target="tpu_custom_call" | custom-call | tf_op jit(solution)/shard_map/pallas_call | solution.py:344
  88.0 0.0 copy-start.3
  88.0 0.0 copy-start.2
  88.0 0.0 all-reduce.7.cloned.1.call-update
  88.0 0.7 copy-done.3
  88.8 53.2 %psum.7 = f32[1,6,1152]{2,1,0:T(8,128)S(1)} all-reduce(f32[1,6,1152]{2,1,0:T(8,128)S(1)} %slice_bitcast_fusion), channel_id=1, replica_groups=mesh['dp'=8,'seq'=16] {'seq'}, use_global_device_ids=true, to_apply=%region_0.0 | all-reduce | flops 6912 | bytes 55296 | tf_op jit(solution)/shard_map/psum | solution.py:374
  142.0 0.6 copy.22
  142.6 113.4 %all-reduce.7.cloned.1.call-done = (bf16[1152,1728]{1,0:T(8,128)(2,1)}, bf16[1152,576]{1,0:T(8,128)(2,1)}, bf16[1152,1728]{1,0:T(8,128)(2,1)}, bf16[1152,576]{1,0:T(8,128)(2,1)}) async-done(((bf16[1152,1728]{1,0:T(8,128)(2,1)}, bf16[1152,576]{1,0:T(8,128)(2,1)}, bf16[1152,1728]{1,0:T(8,128)(2,1)}, bf16[1152,576]{1,0:T(8,128)(2,1)}), (bf16[1152,1728]{1,0:T(8,128)(2,1)}, bf16[1152,576]{1,0:T(8,128)(2,1)}, ...) | async-done | bytes 10616848
  256.0 1.4 convert_multiply_fusion.2
  257.4 1.6 convert_multiply_fusion
  259.1 0.0 copy-done.2
  259.1 0.8 copy.31
  (1 shorter events, 0.0 us)
Async XLA Ops:
  7.2 248.8 %all-reduce.7.cloned.1.call-start = ((), (), s32[]{:S(2)}) async-start(), calls=%async_computation | async-start | bytes 22413312
  13.7 6.6 %copy-start = (bf16[1152,576]{0,1:T(8,128)(2,1)S(1)}, bf16[1152,576]{0,1:T(8,128)(2,1)}, u32[]{:S(2)}) copy-start(bf16[1152,576]{0,1:T(8,128)(2,1)} %param.11) | copy-start | bytes 3981316
  13.7 8.2 %copy-start.1 = (bf16[1152,576]{0,1:T(8,128)(2,1)S(1)}, bf16[1152,576]{0,1:T(8,128)(2,1)}, u32[]{:S(2)}) copy-start(bf16[1152,576]{0,1:T(8,128)(2,1)} %param.13) | copy-start | bytes 3981316
  20.3 3.3 %copy-start.4 = (f32[1,6,1152]{2,0,1:T(1,128)S(1)}, f32[1,6,1152]{2,0,1:T(1,128)}, u32[]{:S(2)}) copy-start(f32[1,6,1152]{2,0,1:T(1,128)} %param.9) | copy-start | bytes 82948
  88.0 0.8 copy-start.3
  88.0 171.1 %copy-start.2 = (bf16[256,1152]{1,0:T(8,128)(2,1)S(1)}, bf16[256,1152]{1,0:T(8,128)(2,1)}, u32[]{:S(2)}) copy-start(bf16[256,1152]{1,0:T(8,128)(2,1)} %get-tuple-element.12) | copy-start | bytes 1769476
Sparse Core Ops, SparseCore 0:
  88.2 167.7 all-reduce.6

commit v2 on v1

--- a/solution.py
+++ b/solution.py
@@ -16,6 +16,8 @@
 SEQ = 16
 EPSILON = 1e-06
 FACTOR = HEAD_DIM**-0.5
+BLOCKS = 16
+BLOCK = 80
 MESH = pl.DeviceIdType.MESH
 F32 = jnp.float32
 BF16 = jnp.bfloat16
@@ -55,20 +57,30 @@
 def project(modulated, weight, packed):
     def body(i, _):
         cols = rows_of(i, 256)
-        packed[:, cols] = dot(modulated[...], weight[:, cols]).astype(BF16)
+        packed[:, cols] = dot(modulated[...], weight[cols, :], NT).astype(BF16)
         return 0
 
     lax.fori_loop(0, 6, body, 0)
-    packed[:, 1536:PACKED] = dot(modulated[...], weight[:, 1536:PACKED]).astype(BF16)
-
-
-def project_back(rows_in, weight, out, width):
+    packed[:, 1536:PACKED] = dot(modulated[...], weight[1536:PACKED, :], NT).astype(BF16)
+
+
+def project_out(right, weight, out):
     def body(i, _):
         cols = rows_of(i, 384)
-        out[:, cols] = dot(rows_in[...], weight[cols, :], NT).astype(out.dtype)
-        return 0
-
-    lax.fori_loop(0, width // 384, body, 0)
+        out[:, cols] = dot(right[1, :, HE:], weight[:, cols])
+        return 0
+
+    lax.fori_loop(0, 3, body, 0)
+
+
+def project_back(right, weight, out):
+    def body(i, _):
+        cols = rows_of(i, 384)
+        total = dot(right[0], weight[: 2 * HE, cols]) + dot(right[1, :, :HE], weight[2 * HE :, cols])
+        out[:, cols] = total.astype(BF16)
+        return 0
+
+    lax.fori_loop(0, 3, body, 0)
 
 
 def head(ref, h, section=0):
@@ -84,15 +96,20 @@
     return raised / jnp.sum(raised, axis=-1, keepdims=True)
 
 
-def head_backward(probs, weights, packed, d_attended, h, d_packed):
+def head_backward(probs, weights, packed, d_attended, h, right):
     d_head = head(d_attended, h)
     d_weights = dot(d_head, head(packed, h, 2), NT)
     carried = jnp.sum(d_weights * probs, axis=-1, keepdims=True)
     d_scores = (probs * (d_weights - carried) * FACTOR).astype(BF16)
     lane = h * HEAD_DIM
-    d_packed[:, lane : lane + HEAD_DIM] = dot(d_scores, head(packed, h, 1)).astype(BF16)
-    d_packed[:, HE + lane : HE + lane + HEAD_DIM] = dot(d_scores, head(packed, h, 0), TN).astype(BF16)
-    d_packed[:, 2 * HE + lane : 2 * HE + lane + HEAD_DIM] = dot(weights, d_head, TN).astype(BF16)
+    right[0, :, lane : lane + HEAD_DIM] = dot(d_scores, head(packed, h, 1)).astype(BF16)
+    right[0, :, HE + lane : HE + lane + HEAD_DIM] = dot(d_scores, head(packed, h, 0), TN).astype(BF16)
+    right[1, :, lane : lane + HEAD_DIM] = dot(weights, d_head, TN).astype(BF16)
+
+
+def attend(probs, packed, h, right):
+    lane = HE + h * HEAD_DIM
+    right[1, :, lane : lane + HEAD_DIM] = dot(probs, head(packed, h, 2)).astype(BF16)
 
 
 def fold(x):
@@ -140,20 +157,231 @@
     return tuple(jnp.sum(t, axis=0, keepdims=True) for t in totals)
 
 
-def weight_gradient(left, right, flipped, out, width):
+def flip(source, flipped, left):
     def turn(i, _):
         cols = rows_of(i, 128)
-        flipped[cols, :] = left[:, cols].T
+        flipped[cols, :] = source[:, cols].astype(F32).T
         return 0
 
     lax.fori_loop(0, D // 128, turn, 0)
-
-    def body(i, _):
-        rows = rows_of(i, 128)
-        out[rows, :] = dot(flipped[rows, :], right[...]).astype(BF16)
-        return 0
-
-    lax.fori_loop(0, D // 128, body, 0)
+    empty = jnp.zeros((BLOCK - 72, TOKENS), F32)
+    for k in range(BLOCKS):
+        rows = flipped[72 * k : 72 * k + 72, :]
+        left[k] = jnp.concatenate([rows, empty], axis=0).astype(BF16)
+
+
+def swap1(i):
+    return i + 1 - 2 * lax.rem(i, 2)
+
+
+class Place:
+    def __init__(self):
+        self.dp = lax.axis_index("dp")
+        self.seq = lax.axis_index("seq")
+        self.x = lax.rem(self.dp, 4)
+        self.yh = lax.div(self.dp, 4)
+        self.yl = lax.div(self.seq, 8)
+        self.y = 2 * self.yh + self.yl
+        self.z = lax.rem(lax.div(self.seq, 2), 4)
+        self.core = lax.rem(self.seq, 2)
+
+    def at(self, x=None, y=None, z=None, core=None):
+        x = self.x if x is None else x
+        y = self.y if y is None else y
+        z = self.z if z is None else z
+        core = self.core if core is None else core
+        return {
+            "dp": 4 * lax.div(y, 2) + x,
+            "seq": 8 * lax.rem(y, 2) + 2 * z + core,
+        }
+
+    def pair(self, i):
+        near, far = swap1(i), 3 - i
+        return near + self.core * (far - near), far + self.core * (near - far)
+
+
+def remote(src, dst, send, recv, device):
+    return pltpu.make_async_remote_copy(
+        src_ref=src, dst_ref=dst, send_sem=send, recv_sem=recv, device_id=device, device_id_type=MESH
+    )
+
+
+class PairTerms:
+    def __init__(self, place, left, right, left_in, right_in, send, recv):
+        self.core = place.core
+        other = place.at(core=1 - place.core)
+        self.left, self.right, self.left_in, self.right_in = left, right, left_in, right_in
+        self.copies = [
+            remote(left.at[0], left_in.at[0], send.at[0], recv.at[0], other),
+            remote(left.at[1], left_in.at[1], send.at[1], recv.at[1], other),
+            remote(right.at[1 - place.core], right_in, send.at[2], recv.at[2], other),
+        ]
+
+    def start(self, i):
+        if i == 1:
+            pl.when(self.core == 0)(self.copies[1].start)
+        else:
+            self.copies[i].start()
+
+    def wait_recv(self):
+        self.copies[0].wait_recv()
+        pl.when(self.core == 1)(self.copies[1].wait_recv)
+        self.copies[2].wait_recv()
+
+    def wait_send(self):
+        self.copies[0].wait_send()
+        pl.when(self.core == 0)(self.copies[1].wait_send)
+        self.copies[2].wait_send()
+
+    def multiply(self, chunk, out):
+        left = 0 if chunk == 0 else self.core
+        cols = slice(chunk * HE, chunk * HE + HE)
+
+        def body(i, _):
+            blocks = pl.ds(4 * i, 4)
+            own = self.left[left, blocks].reshape(4 * BLOCK, TOKENS)
+            theirs = self.left_in[left, blocks].reshape(4 * BLOCK, TOKENS)
+            total = dot(own, self.right[self.core, :, cols]) + dot(theirs, self.right_in[:, cols])
+            out[blocks] = total.astype(BF16).reshape(4, BLOCK, HE)
+            return 0
+
+        lax.fori_loop(0, BLOCKS // 4, body, 0)
+
+
+class Halving:
+    def __init__(self, place, x_first, whole, first, second, half, third, fourth, quarter, windows, final, other, send, recv):
+        self.place, self.x_first = place, x_first
+        self.whole, self.first, self.second = whole, first, second
+        self.half, self.third, self.fourth = half, third, fourth
+        self.quarter, self.windows, self.final, self.other = quarter, windows, final, other
+        x, y = place.x, place.y
+        self.a, self.b = (x, y) if x_first else (y, x)
+        self.a1, self.a2 = place.pair(self.a)
+        self.b1, self.b2 = place.pair(self.b)
+        far_a, far_b = lax.rem(self.a + 2, 4), lax.rem(self.b + 2, 4)
+        z = place.z
+
+        def copy(i, src, dst, device):
+            return remote(src, dst, send.at[i], recv.at[i], device)
+
+        to_a1, to_a2 = self.device(x_first, self.a1), self.device(x_first, self.a2)
+        to_b1, to_b2 = self.device(not x_first, self.b1), self.device(not x_first, self.b2)
+        self.copies = [
+            copy(0, self.block(far_a), first.at[1], to_a1),
+            copy(1, self.block(self.a1), first.at[0], to_a1),
+            copy(2, self.block(self.a2), second, to_a2),
+            copy(3, half.at[far_b], third.at[1], to_b1),
+            copy(4, half.at[self.b1], third.at[0], to_b1),
+            copy(5, half.at[self.b2], fourth, to_b2),
+        ]
+        for j in range(1, 4):
+            peer = lax.rem(z + j, 4)
+            self.copies.append(
+                copy(5 + j, quarter.at[rows_of_16(peer)], windows.at[j - 1], place.at(z=peer))
+            )
+        self.copies.append(copy(9, final, other, place.at(core=1 - place.core)))
+
+    def device(self, on_x, i):
+        return self.place.at(x=i) if on_x else self.place.at(y=i)
+
+    def block(self, i):
+        if self.x_first:
+            return self.whole.at[:, i]
+        return self.whole.at[lax.div(i, 2), :, lax.rem(i, 2)]
+
+    def parts(self, i):
+        if self.x_first:
+            return [self.whole.at[yh, i, yl] for yh in range(2) for yl in range(2)]
+        return [self.whole.at[lax.div(i, 2), x, lax.rem(i, 2)] for x in range(4)]
+
+    def slot(self, ref, j):
+        return ref.at[j // 2, j % 2] if self.x_first else ref.at[j]
+
+    def stage0(self):
+        self.copies[0].start()
+        self.copies[1].start()
+
+    def stage1(self):
+        self.copies[0].wait_recv()
+        for j, part in enumerate(self.parts(self.a2)):
+            part[...] = (part[...].astype(F32) + self.slot(self.first.at[1], j)[...].astype(F32)).astype(BF16)
+        self.copies[2].start()
+
+    def stage2(self):
+        self.copies[1].wait_recv()
+        self.copies[2].wait_recv()
+        for j, part in enumerate(self.parts(self.a)):
+            total = part[...].astype(F32) + self.slot(self.first.at[0], j)[...].astype(F32)
+            self.half[j] = (total + self.slot(self.second, j)[...].astype(F32)).astype(BF16)
+        self.copies[3].start()
+        self.copies[4].start()
+
+    def stage3(self):
+        self.copies[3].wait_recv()
+        kept = self.half.at[self.b2]
+        kept[...] = (kept[...].astype(F32) + self.third[1].astype(F32)).astype(BF16)
+        self.copies[5].start()
+
+    def stage4(self):
+        self.copies[4].wait_recv()
+        self.copies[5].wait_recv()
+        total = self.half[self.b].astype(F32) + self.third[0].astype(F32) + self.fourth[...].astype(F32)
+        self.quarter[...] = total.astype(BF16)
+        for j in range(6, 9):
+            self.copies[j].start()
+
+    def stage5(self):
+        for j in range(6, 9):
+            self.copies[j].wait_recv()
+        total = self.quarter[rows_of_16(self.place.z), :].astype(F32)
+        for j in range(3):
+            total = total + self.windows[j].astype(F32)
+        self.final[...] = total * (1.0 / 8)
+        self.copies[9].start()
+
+    def stage6(self):
+        self.copies[9].wait_recv()
+        shift = lax.rem(32 - 2 * self.place.z - 9 * self.place.core, 32)
+        own = pltpu.roll(self.final[...], shift, 0)[:16]
+        theirs = pltpu.roll(self.other[...], shift, 0)[:16]
+        low = self.place.core == 0
+        return jnp.where(low, own, theirs)[:9], jnp.where(low, theirs, own)[:9]
+
+    def wait_send(self):
+        for copy in self.copies:
+            copy.wait_send()
+
+
+def rows_of_16(i):
+    return pl.ds(pl.multiple_of(i * 16, 16), 32)
+
+
+class ClipSum:
+    def __init__(self, place, held, arrived, send, recv):
+        self.held, self.arrived = held, arrived
+        devices = [
+            place.at(core=1 - place.core),
+            place.at(z=swap1(place.z)),
+            place.at(z=3 - place.z),
+            place.at(y=swap1(place.y)),
+        ]
+        self.copies = [
+            remote(held.at[i], arrived.at[i], send.at[i], recv.at[i], device)
+            for i, device in enumerate(devices)
+        ]
+
+    def start(self):
+        self.copies[0].start()
+
+    def step(self, i):
+        self.copies[i].wait_recv()
+        self.held[i + 1] = self.held[i] + self.arrived[i]
+        if i < 3:
+            self.copies[i + 1].start()
+
+    def wait_send(self):
+        for copy in self.copies:
+            copy.wait_send()
 
 
 class Exchange:
@@ -202,13 +430,17 @@
     lat_hbm, cot_hbm, mod_hbm, wqs_hbm, wos_hbm, wqt_hbm, wot_hbm,
     grad_latents, moments, dqkv_s, dout_s, dqkv_t, dout_t,
     lat, cot, mod, wqs, wos, wqt, wot,
-    normed_s, scale_s, modulated_s, packed_s, probs_s, attended_s, branch_s,
-    normed_t, scale_t, modulated_t, packed_t, attended_t, branch_t,
+    normed_s, scale_s, modulated_s, packed_s, probs_s, branch_s,
+    normed_t, scale_t, modulated_t, packed_t, branch_t,
     hidden_out, hidden, grad_out, grad_hidden,
-    d_branch_s, d_branch_t, d_attended, d_packed_s, d_packed_t, d_modulated, flipped,
-    load_sem, send_sem, recv_sem,
+    d_branch_s, d_branch_t, d_attended, d_modulated, flipped,
+    left_s, right_s, left_in_s, right_in_s, left_t, right_t, left_in_t, right_in_t,
+    whole, first_x, first_y, second_x, second_y, half, third, fourth, quarter, windows, final, other,
+    held, arrived,
+    load_sem, send_sem, recv_sem, pair_send, pair_recv, sum_send, sum_recv, clip_send, clip_recv,
 ):
-    me = lax.axis_index("seq")
+    place = Place()
+    me = place.seq
     loads = [
         pltpu.make_async_copy(src, dst, load_sem.at[i])
         for i, (src, dst) in enumerate(
@@ -231,14 +463,30 @@
         return 0
 
     lax.fori_loop(1, SEQ, greet, 0)
+    for device in (place.at(x=swap1(place.x)), place.at(x=3 - place.x), place.at(y=3 - place.y)):
+        pl.semaphore_signal(barrier, inc=1, device_id=device, device_id_type=MESH)
     loads[0].wait()
     loads[1].wait()
     normalise(lat, mod, 0, normed_s, scale_s, modulated_s)
-    pl.semaphore_wait(barrier, SEQ - 1)
+    pl.semaphore_wait(barrier, SEQ + 2)
 
     cot_trip = Exchange(cot_hbm, cot, send_sem.at[0], recv_sem.at[0])
     hidden_trip = Exchange(hidden_out, hidden, send_sem.at[1], recv_sem.at[1])
     grad_trip = Exchange(grad_out, grad_hidden, send_sem.at[2], recv_sem.at[2])
+    pair_s = PairTerms(place, left_s, right_s, left_in_s, right_in_s, pair_send.at[0], pair_recv.at[0])
+    pair_t = PairTerms(place, left_t, right_t, left_in_t, right_in_t, pair_send.at[1], pair_recv.at[1])
+    sums_s, sums_t = [
+        [
+            Halving(
+                place, c == 0, whole.at[l, c], (first_x, first_y)[c].at[l], (second_x, second_y)[c].at[l],
+                half.at[l, c], third.at[l, c], fourth.at[l, c], quarter.at[l, c], windows.at[l, c],
+                final.at[l, c], other.at[l, c], sum_send.at[l, c], sum_recv.at[l, c],
+            )
+            for c in range(2)
+        ]
+        for l in range(2)
+    ]
+    clip = ClipSum(place, held, arrived, clip_send, clip_recv)
 
     def send_cot(j, _):
         cot_trip.start(j)
@@ -251,10 +499,9 @@
     for h in range(HEADS):
         probs = probabilities(packed_s, h, None)
         probs_s[h] = probs
-        lane = h * HEAD_DIM
-        attended_s[:, lane : lane + HEAD_DIM] = dot(probs.astype(BF16), head(packed_s, h, 2)).astype(BF16)
+        attend(probs.astype(BF16), packed_s, h, right_s)
     loads[4].wait()
-    project_back(attended_s, wos, branch_s, D)
+    project_out(right_s, wos, branch_s)
 
     gate_s = mod[2:3, :]
 
@@ -277,7 +524,9 @@
     cot_trip.wait_recv()
     loads[3].wait()
     gated(cot, mod, 5, d_branch_t)
-    d_attended[...] = dot(d_branch_t[...], wot[...]).astype(BF16)
+    d_attended[...] = dot(d_branch_t[...], wot[...], NT).astype(BF16)
+    flip(modulated_s, flipped, left_s.at[0])
+    flip(d_branch_t, flipped, left_t.at[1])
     hidden_trip.wait_recv()
     normalise(hidden, mod, 3, normed_t, scale_t, modulated_t)
     loads[5].wait()
@@ -288,10 +537,11 @@
     for h in range(HEADS):
         probs = probabilities(packed_t, h, mask)
         weights = probs.astype(BF16)
-        lane = h * HEAD_DIM
-        attended_t[:, lane : lane + HEAD_DIM] = dot(weights, head(packed_t, h, 2)).astype(BF16)
-        head_backward(probs, weights, packed_t, d_attended, h, d_packed_t)
-    project_back(d_packed_t, wqt, d_modulated, D)
+        attend(weights, packed_t, h, right_t)
+        head_backward(probs, weights, packed_t, d_attended, h, right_t)
+    pair_t.start(2)
+    pair_t.start(1)
+    project_back(right_t, wqt, d_modulated)
 
     def send_grad(i):
         @pl.when(i != me)
@@ -301,82 +551,136 @@
     d_offset, d_stretch = normalise_back(
         d_modulated, normed_t, scale_t, mod, 3, cot, grad_out, send_grad
     )
-    moments[3:4, :] = d_offset
-    moments[4:5, :] = d_stretch
+    clip_first = held.at[0]
+    clip_first[3:4, :] = d_offset
+    clip_first[4:5, :] = d_stretch
     grad_hidden[rows_of(me, 16), :] = grad_out[rows_of(me, 16), :]
-    project_back(attended_t, wot, branch_t, D)
-    moments[5:6, :] = gate_sum(cot, branch_t)
-    weight_gradient(modulated_t, d_packed_t, flipped, dqkv_t, PACKED)
-    weight_gradient(d_branch_t, attended_t, flipped, dout_t, HE)
+    flip(modulated_t, flipped, left_t.at[0])
+    pair_t.start(0)
+    project_out(right_t, wot, branch_t)
+    clip_first[5:6, :] = gate_sum(cot, branch_t)
+    pair_t.wait_recv()
+    for c in range(2):
+        pair_t.multiply(c, whole.at[1, c].reshape(BLOCKS, BLOCK, HE))
+        sums_t[c].stage0()
 
     grad_trip.wait_recv()
     gated(grad_hidden, mod, 2, d_branch_s)
-    moments[2:3, :] = gate_sum(grad_hidden, branch_s)
-    d_attended[...] = dot(d_branch_s[...], wos[...]).astype(BF16)
+    clip_first[2:3, :] = gate_sum(grad_hidden, branch_s)
+    d_attended[...] = dot(d_branch_s[...], wos[...], NT).astype(BF16)
+    flip(d_branch_s, flipped, left_s.at[1])
+    pair_s.start(0)
+    pair_s.start(1)
+    sums_t[0].stage1()
+    sums_t[1].stage1()
     for h in range(HEADS):
         probs = probs_s[h]
-        head_backward(probs, probs.astype(BF16), packed_s, d_attended, h, d_packed_s)
-    project_back(d_packed_s, wqs, d_modulated, D)
+        head_backward(probs, probs.astype(BF16), packed_s, d_attended, h, right_s)
+    pair_s.start(2)
+    sums_t[0].stage2()
+    sums_t[1].stage2()
+    pair_s.wait_recv()
+    for c in range(2):
+        pair_s.multiply(c, whole.at[0, c].reshape(BLOCKS, BLOCK, HE))
+        sums_s[c].stage0()
+    sums_t[0].stage3()
+    sums_t[1].stage3()
+    project_back(right_s, wqs, d_modulated)
+    sums_s[0].stage1()
+    sums_s[1].stage1()
     d_offset, d_stretch = normalise_back(
         d_modulated, normed_s, scale_s, mod, 0, grad_hidden, grad_latents, lambda i: None
     )
-    moments[0:1, :] = d_offset
-    moments[1:2, :] = d_stretch
-    moments[6:8, :] = jnp.zeros((2, D), F32)
-    weight_gradient(modulated_s, d_packed_s, flipped, dqkv_s, PACKED)
-    weight_gradient(d_branch_s, attended_s, flipped, dout_s, HE)
+    clip_first[0:1, :] = d_offset
+    clip_first[1:2, :] = d_stretch
+    clip_first[6:8, :] = jnp.zeros((2, D), F32)
+    clip.start()
+    sums_t[0].stage4()
+    sums_t[1].stage4()
+    clip.step(0)
+    sums_s[0].stage2()
+    sums_s[1].stage2()
+    clip.step(1)
+    sums_t[0].stage5()
+    sums_t[1].stage5()
+    sums_s[0].stage3()
+    sums_s[1].stage3()
+    clip.step(2)
+    results_t = [sums.stage6() for sums in sums_t]
+    sums_s[0].stage4()
+    sums_s[1].stage4()
+    clip.step(3)
+    sums_s[0].stage5()
+    sums_s[1].stage5()
+    results_s = [sums.stage6() for sums in sums_s]
+    moments[...] = held[4]
+    for (d_query, d_value), (d_key, d_out), dqkv, dout in (
+        (*results_s, dqkv_s, dout_s),
+        (*results_t, dqkv_t, dout_t),
+    ):
+        dqkv[:, :HE] = d_query
+        dqkv[:, HE : 2 * HE] = d_key
+        dqkv[:, 2 * HE :] = d_value
+        dout[...] = d_out
+
     cot_trip.wait_send()
     hidden_trip.wait_send()
     grad_trip.wait_send()
+    for part in (pair_s, pair_t, *sums_s, *sums_t, clip):
+        part.wait_send()
 
 
 def local(latents, cotangent, modulation, spatial_qkv, spatial_out, temporal_qkv, temporal_out):
     vm = pl.BlockSpec(memory_space=pltpu.VMEM)
     hbm = pl.BlockSpec(memory_space=pl.ANY)
     sds = jax.ShapeDtypeStruct
-    wide = pltpu.VMEM((TOKENS, D), BF16)
-    wide32 = pltpu.VMEM((TOKENS, D), F32)
-    narrow = pltpu.VMEM((TOKENS, HE), BF16)
-    three = pltpu.VMEM((TOKENS, PACKED), BF16)
-    column = pltpu.VMEM((TOKENS, 1), F32)
-    wq = pltpu.VMEM((D, PACKED), BF16)
-    wo = pltpu.VMEM((D, HE), BF16)
+
+    def bf16(*shape):
+        return pltpu.VMEM(shape, BF16)
+
+    def f32(*shape):
+        return pltpu.VMEM(shape, F32)
+
+    wide, wide32, column = bf16(TOKENS, D), f32(TOKENS, D), f32(TOKENS, 1)
+    three, wq, wo = bf16(TOKENS, PACKED), bf16(PACKED, D), bf16(HE, D)
+    left, right = bf16(2, BLOCKS, BLOCK, TOKENS), bf16(2, TOKENS, 2 * HE)
+    dma = pltpu.SemaphoreType.DMA
     outs = pl.pallas_call(
         kernel,
         out_shape=[
             sds((TOKENS, D), BF16),
             sds((8, D), F32),
-            sds((D, PACKED), BF16),
-            sds((D, HE), BF16),
-            sds((D, PACKED), BF16),
-            sds((D, HE), BF16),
+            sds((9, PACKED), F32),
+            sds((9, HE), F32),
+            sds((9, PACKED), F32),
+            sds((9, HE), F32),
         ],
         in_specs=[hbm] * 7,
         out_specs=[vm] * 6,
         scratch_shapes=[
-            wide, wide, pltpu.VMEM((6, D), F32), wq, wo, wq, wo,
-            wide32, column, wide, three, pltpu.VMEM((HEADS, TOKENS, TOKENS), F32), narrow, wide32,
-            wide32, column, wide, three, narrow, wide32,
+            wide, wide, f32(6, D), wq, wo, wq, wo,
+            wide32, column, wide, three, f32(HEADS, TOKENS, TOKENS), wide32,
+            wide32, column, wide, three, wide32,
             wide, wide, wide, wide,
-            wide, wide, narrow, three, three, wide, pltpu.VMEM((D, TOKENS), BF16),
-            pltpu.SemaphoreType.DMA((7,)),
-            pltpu.SemaphoreType.DMA((3, SEQ)),
-            pltpu.SemaphoreType.DMA((3, SEQ)),
+            wide, wide, bf16(TOKENS, HE), wide, f32(D, TOKENS),
+            left, right, left, bf16(TOKENS, 2 * HE), left, right, left, bf16(TOKENS, 2 * HE),
+            bf16(2, 2, 2, 4, 2, BLOCK, HE), bf16(2, 2, 2, 2, BLOCK, HE), bf16(2, 2, 4, BLOCK, HE),
+            bf16(2, 2, 2, BLOCK, HE), bf16(2, 4, BLOCK, HE),
+            bf16(2, 2, 4, BLOCK, HE), bf16(2, 2, 2, BLOCK, HE), bf16(2, 2, BLOCK, HE), bf16(2, 2, BLOCK, HE),
+            bf16(2, 2, 3, 32, HE), f32(2, 2, 32, HE), f32(2, 2, 32, HE),
+            f32(5, 8, D), f32(4, 8, D),
+            dma((7,)), dma((3, SEQ)), dma((3, SEQ)), dma((2, 3)), dma((2, 3)),
+            dma((2, 2, 10)), dma((2, 2, 10)), dma((4,)), dma((4,)),
         ],
         compiler_params=pltpu.CompilerParams(
             collective_id=0, has_side_effects=True, vmem_limit_bytes=62 * 2**20
         ),
     )(
         latents.reshape(TOKENS, D), cotangent.reshape(TOKENS, D), modulation.reshape(6, D),
-        spatial_qkv, spatial_out, temporal_qkv, temporal_out,
+        spatial_qkv.T, spatial_out.T, temporal_qkv.T, temporal_out.T,
     )
     grad, moments, dqkv_s, dout_s, dqkv_t, dout_t = outs
-    grad_modulation = lax.psum(moments[:6], "seq")[None]
-
-    def reduce(x):
-        return lax.psum_scatter(x, ("dp", "seq"), scatter_dimension=0, tiled=True).astype(F32) / 8
-
-    return (grad.reshape(latents.shape), grad_modulation, reduce(dqkv_s), reduce(dout_s), reduce(dqkv_t), reduce(dout_t))
+    return (grad.reshape(latents.shape), moments[:6][None], dqkv_s, dout_s, dqkv_t, dout_t)
 
 
 def solution(mesh):

time: 269 us -> 115 us (0.43)
  the two profiles are of different devices: /device:TPU:5 before, /device:TPU:1 now
where the time goes in v2:
time: 115 us
  Pallas kernels  104 us (90%)
  local copies, waits for them, and re-layouts  10.6 us (9%)
    pallas_call x1, Pallas kernels, local(): pl.pallas_call(kernel, out_shape=[sds((TOKENS, D), BF16), sds((8, D), F32...  104 us
    unnamed x7, local copies, waits for them, and re-layouts  9.82 us

profile of v2, /device:TPU:1, one launch (start us, length us, event | category | flops | bytes accessed | tf_op | source)
XLA Modules:
  0.0 114.8 jit_solution(649153514329480162)
XLA Ops:
  0.6 1.4 %copy.16 = f32[1,6,1152]{2,1,0:T(8,128)} copy(f32[1,6,1152]{2,0,1:T(1,128)} %param.9) | data formatting | bytes 55296
  2.0 103.5 %shard_map.118 = (bf16[256,1152]{1,0:T(8,128)(2,1)}, f32[8,1152]{1,0:T(8,128)}, f32[9,1728]{1,0:T(8,128)}, f32[9,576]{1,0:T(8,128)}, f32[9,1728]{1,0:T(8,128)}, /*index=5*/f32[9,576]{1,0:T(8,128)}) custom-call(bf16[256,1152]{1,0:T(8,128)(2,1)} %bitcast.17, bf16[256,1152]{1,0:T(8,128)(2,1)} %bitcast.18, f32[6,1152]{1,0:T(8,128)} %bitcast.19, ...), custom_call_target="tpu_custom_call" | custom-call | tf_op jit(solution)/shard_map/pallas_call | solution.py:648
  105.5 0.8 slice_bitcast_fusion
  106.3 0.6 copy.13
  106.9 1.9 %copy.22 = bf16[1,1,256,1152]{3,2,1,0:T(8,128)(2,1)} copy(bf16[1,1,256,1152]{3,2,1,0:T(8,128)(2,1)} %bitcast.16) | data formatting | bytes 1179648
  108.9 1.6 %copy.23 = f32[9,1728]{1,0:T(8,128)} copy(f32[9,1728]{1,0:T(8,128)} %get-tuple-element.32) | data formatting | bytes 124416
  110.4 1.4 %copy.24 = f32[9,576]{1,0:T(8,128)} copy(f32[9,576]{1,0:T(8,128)} %get-tuple-element.33) | data formatting | bytes 41472
  111.8 1.6 %copy.25 = f32[9,1728]{1,0:T(8,128)} copy(f32[9,1728]{1,0:T(8,128)} %get-tuple-element.34) | data formatting | bytes 124416
  113.4 1.4 %copy.26 = f32[9,576]{1,0:T(8,128)} copy(f32[9,576]{1,0:T(8,128)} %get-tuple-element.35) | data formatting | bytes 41472

commit v3 on v2

v3 whole, which is shorter than its diff:
```python
import functools

import jax
import jax.numpy as jnp
from jax import lax
from jax.experimental import pallas as pl
from jax.experimental.pallas import tpu as pltpu
from jax.sharding import PartitionSpec as P

HEADS = 8
HEAD_DIM = 72
HE = HEADS * HEAD_DIM
PACKED = 3 * HE
D = 1152
TOKENS = 256
SEQ = 16
EPSILON = 1e-06
FACTOR = HEAD_DIM**-0.5
BLOCKS = 16
BLOCK = 80
PART = 384
MESH = pl.DeviceIdType.MESH
F32 = jnp.float32
BF16 = jnp.bfloat16

NN = (((1,), (0,)), ((), ()))
NT = (((1,), (1,)), ((), ()))
TN = (((0,), (0,)), ((), ()))


def dot(a, b, dims=NN):
    return lax.dot_general(a, b, dims, preferred_element_type=F32)


def rows_of(i, size):
    return pl.ds(pl.multiple_of(i * size, size), size)


def normalise(read, mod, row, normed, scale, modulated):
    offset = mod[row]
    stretch = 1.0 + mod[row + 1]

    def body(i, _):
        rows = rows_of(i, 32)
        x = read(rows).astype(F32)
        centred = x - jnp.mean(x, axis=-1, keepdims=True)
        spread = jnp.mean(centred * centred, axis=-1, keepdims=True)
        inverse = lax.rsqrt(spread + EPSILON)
        n = centred * inverse
        normed[rows, :] = n
        scale[rows, :] = inverse
        modulated[rows, :] = (n * stretch + offset).astype(BF16)
        return 0

    lax.fori_loop(0, TOKENS // 32, body, 0)


def project(modulated, weight, packed):
    def body(i, _):
        cols = rows_of(i, 256)
        packed[:, cols] = dot(modulated[...], weight[cols, :], NT).astype(BF16)
        return 0

    lax.fori_loop(0, 6, body, 0)
    packed[:, 1536:PACKED] = dot(modulated[...], weight[1536:PACKED, :], NT).astype(BF16)


def project_out(attended, weight, out):
    def body(i, _):
        cols = rows_of(i, 384)
        out[:, cols] = dot(attended[...], weight[:, cols])
        return 0

    lax.fori_loop(0, 3, body, 0)


def project_back(right, weight, out):
    def body(i, _):
        cols = rows_of(i, 384)
        total = dot(right[0], weight[: 2 * HE, cols]) + dot(right[1, :, :HE], weight[2 * HE :, cols])
        out[:, cols] = total.astype(BF16)
        return 0

    lax.fori_loop(0, 3, body, 0)


def head(ref, h, section=0):
    lane = section * HE + h * HEAD_DIM
    return ref[:, lane : lane + HEAD_DIM]


def probabilities(packed, h, mask):
    scores = dot(head(packed, h, 0), head(packed, h, 1), NT)
    raised = jnp.exp(scores * FACTOR)
    if mask is not None:
        raised = jnp.where(mask, raised, 0.0)
    return raised / jnp.sum(raised, axis=-1, keepdims=True)


def head_backward(probs, weights, packed, d_attended, h, right):
    d_head = head(d_attended, h)
    d_weights = dot(d_head, head(packed, h, 2), NT)
    carried = jnp.sum(d_weights * probs, axis=-1, keepdims=True)
    d_scores = (probs * (d_weights - carried) * FACTOR).astype(BF16)
    lane = h * HEAD_DIM
    right[0, :, lane : lane + HEAD_DIM] = dot(d_scores, head(packed, h, 1)).astype(BF16)
    right[0, :, HE + lane : HE + lane + HEAD_DIM] = dot(d_scores, head(packed, h, 0), TN).astype(BF16)
    right[1, :, lane : lane + HEAD_DIM] = dot(weights, d_head, TN).astype(BF16)


def attend(weights, packed, h, attended):
    lane = h * HEAD_DIM
    attended[:, lane : lane + HEAD_DIM] = dot(weights, head(packed, h, 2)).astype(BF16)


def fold(x):
    return sum(x[8 * i : 8 * i + 8] for i in range(x.shape[0] // 8))


def gated(source, mod, row, out):
    gate = mod[row]

    def body(i, _):
        rows = rows_of(i, 32)
        out[rows, :] = (source[rows, :].astype(F32) * gate).astype(BF16)
        return 0

    lax.fori_loop(0, TOKENS // 32, body, 0)


def gate_sum(upstream, branch):
    def body(i, total):
        rows = rows_of(i, 32)
        return total + fold(upstream[rows, :].astype(F32) * branch[rows, :])

    total = lax.fori_loop(0, TOKENS // 32, body, jnp.zeros((8, D), F32))
    return jnp.sum(total, axis=0, keepdims=True)


def normalise_back(d_modulated, normed, scale, mod, row, upstream, out, branch=None, after=None):
    stretch = 1.0 + mod[row + 1]

    def body(i, totals):
        rows = rows_of(i, 16)
        g = d_modulated[rows, :].astype(F32)
        n = normed[rows, :]
        dn = g * stretch
        first = jnp.mean(dn, axis=-1, keepdims=True)
        second = jnp.mean(dn * n, axis=-1, keepdims=True)
        dx = scale[rows, :] * (dn - first - n * second)
        value = (upstream[rows, :].astype(F32) + dx).astype(BF16)
        out[rows, :] = value
        terms = [g, g * n]
        if branch is not None:
            terms.append(value.astype(F32) * branch[rows, :])
        if after is not None:
            after(i)
        return tuple(total + fold(term) for total, term in zip(totals, terms))

    zero = jnp.zeros((8, D), F32)
    totals = lax.fori_loop(0, TOKENS // 16, body, (zero,) * (2 if branch is None else 3))
    return tuple(jnp.sum(t, axis=0, keepdims=True) for t in totals)


def flip(source, flipped, left):
    def turn(i, _):
        cols = rows_of(i, 128)
        flipped[cols, :] = source[:, cols].astype(F32).T
        return 0

    lax.fori_loop(0, D // 128, turn, 0)
    empty = jnp.zeros((BLOCK - 72, TOKENS), F32)
    for k in range(BLOCKS):
        rows = flipped[72 * k : 72 * k + 72, :]
        left[k] = jnp.concatenate([rows, empty], axis=0).astype(BF16)


def swap1(i):
    return i + 1 - 2 * lax.rem(i, 2)


class Place:
    def __init__(self):
        self.dp = lax.axis_index("dp")
        self.seq = lax.axis_index("seq")
        self.x = lax.rem(self.dp, 4)
        self.yh = lax.div(self.dp, 4)
        self.yl = lax.div(self.seq, 8)
        self.y = 2 * self.yh + self.yl
        self.z = lax.rem(lax.div(self.seq, 2), 4)
        self.core = lax.rem(self.seq, 2)

    def at(self, x=None, y=None, z=None, core=None):
        x = self.x if x is None else x
        y = self.y if y is None else y
        z = self.z if z is None else z
        core = self.core if core is None else core
        return {
            "dp": 4 * lax.div(y, 2) + x,
            "seq": 8 * lax.rem(y, 2) + 2 * z + core,
        }


def remote(src, dst, send, recv, device):
    return pltpu.make_async_remote_copy(
        src_ref=src, dst_ref=dst, send_sem=send, recv_sem=recv, device_id=device, device_id_type=MESH
    )


class PairTerms:
    def __init__(self, place, left, right, left_in, right_in, send, recv):
        self.core = place.core
        other = place.at(core=1 - place.core)
        self.left, self.right, self.left_in, self.right_in = left, right, left_in, right_in
        self.copies = [
            remote(left.at[0], left_in.at[0], send.at[0], recv.at[0], other),
            remote(left.at[1], left_in.at[1], send.at[1], recv.at[1], other),
            remote(right.at[1 - place.core], right_in, send.at[2], recv.at[2], other),
        ]

    def start(self, i):
        if i == 1:
            pl.when(self.core == 0)(self.copies[1].start)
        else:
            self.copies[i].start()

    def wait_recv(self):
        self.copies[0].wait_recv()
        pl.when(self.core == 1)(self.copies[1].wait_recv)
        self.copies[2].wait_recv()

    def wait_send(self):
        self.copies[0].wait_send()
        pl.when(self.core == 0)(self.copies[1].wait_send)
        self.copies[2].wait_send()

    def multiply(self, part, out):
        first = PART * part
        pieces = [(first, first + PART)]
        if part == 1:
            pieces = [(first, HE), (HE, first + PART)]

        def body(i, _):
            blocks = pl.ds(4 * i, 4)
            for low, high in pieces:
                left = 0 if high <= HE else self.core
                own = self.left[left, blocks].reshape(4 * BLOCK, TOKENS)
                theirs = self.left_in[left, blocks].reshape(4 * BLOCK, TOKENS)
                total = dot(own, self.right[self.core, :, low:high]) + dot(theirs, self.right_in[:, low:high])
                out[blocks, :, low - first : high - first] = total.astype(BF16).reshape(4, BLOCK, high - low)
            return 0

        lax.fori_loop(0, BLOCKS // 4, body, 0)


class Reduction:
    def __init__(self, place, part, whole, first, half, second, quarter, third, final, mine, other, send, recv):
        self.place, self.part = place, part
        self.whole, self.first, self.half, self.second = whole, first, half, second
        self.quarter, self.third, self.final, self.mine, self.other = quarter, third, final, mine, other
        names = ("zyx", "xyz", "yxz")[part]
        self.at = [getattr(place, name) for name in names]
        self.copies = []
        for stage, name in enumerate(names):
            for j in range(1, 4):
                peer = lax.rem(self.at[stage] + j, 4)
                src, dst = (
                    lambda: (self.slab(peer), first.at[j - 1]),
                    lambda: (half.at[peer], second.at[j - 1]),
                    lambda: (quarter.at[window(peer)], third.at[j - 1]),
                )[stage]()
                i = 3 * stage + j - 1
                self.copies.append(remote(src, dst, send.at[i], recv.at[i], place.at(**{name: peer})))
        if part == 0:
            to = [place.at(x=place.z, z=place.x, core=c) for c in (1 - place.core, place.core)]
            self.copies.append(remote(final, other, send.at[9], recv.at[9], to[0]))
            self.trade = remote(final, mine, send.at[10], recv.at[10], to[1])
        else:
            self.copies.append(remote(final, other, send.at[9], recv.at[9], place.at(core=1 - place.core)))

    def slab(self, i):
        if self.part == 2:
            return self.whole.at[lax.div(i, 2), :, lax.rem(i, 2)]
        return self.whole.at[:, i]

    def start(self, stage):
        for i in range(3 * stage, 3 * stage + 3):
            self.copies[i].start()

    def wait(self, stage):
        for i in range(3 * stage, 3 * stage + 3):
            self.copies[i].wait_recv()

    def stage1(self):
        self.start(0)

    def stage2(self):
        self.wait(0)
        own = self.slab(self.at[0])
        for j in range(4):
            at = (j,) if self.part == 2 else (j // 2, j % 2)
            total = own[at].astype(F32)
            for k in range(3):
                total = total + self.first[(k, *at)].astype(F32)
            self.half[j] = total.astype(BF16)
        self.start(1)

    def stage3(self):
        self.wait(1)
        total = self.half[self.at[1]].astype(F32)
        for k in range(3):
            total = total + self.second[k].astype(F32)
        self.quarter[...] = total.astype(BF16)
        self.start(2)

    def stage4(self):
        self.wait(2)
        total = self.quarter[window(self.at[2]), :].astype(F32)
        for k in range(3):
            total = total + self.third[k].astype(F32)
        self.final[...] = total * (1.0 / 8)
        self.copies[9].start()
        if self.part == 0:
            pl.when(self.place.x != self.place.z)(self.trade.start)

    def stage5(self):
        mine = self.final
        if self.part == 0:
            mine = self.mine

            @pl.when(self.place.x == self.place.z)
            def _():
                self.mine[...] = self.final[...]

            pl.when(self.place.x != self.place.z)(self.trade.wait_recv)
        self.copies[9].wait_recv()
        shift = lax.rem(32 - 2 * self.place.z - 9 * self.place.core, 32)
        own = pltpu.roll(mine[...], shift, 0)[:16]
        theirs = pltpu.roll(self.other[...], shift, 0)[:16]
        low = self.place.core == 0
        return jnp.where(low, own, theirs)[:9], jnp.where(low, theirs, own)[:9]

    def wait_send(self):
        for copy in self.copies:
            copy.wait_send()
        if self.part == 0:
            pl.when(self.place.x != self.place.z)(self.trade.wait_send)


def window(i):
    return pl.ds(pl.multiple_of(i * 16, 16), 32)


class ClipSum:
    def __init__(self, place, held, arrived, send, recv):
        self.held, self.arrived = held, arrived
        devices = [
            place.at(core=1 - place.core),
            place.at(z=swap1(place.z)),
            place.at(z=3 - place.z),
            place.at(y=swap1(place.y)),
        ]
        self.copies = [
            remote(held.at[i], arrived.at[i], send.at[i], recv.at[i], device)
            for i, device in enumerate(devices)
        ]

    def start(self):
        self.copies[0].start()

    def step(self, i):
        self.copies[i].wait_recv()
        self.held[i + 1] = self.held[i] + self.arrived[i]
        if i < 3:
            self.copies[i + 1].start()

    def wait_send(self):
        for copy in self.copies:
            copy.wait_send()


class Exchange:
    def __init__(self, source, target, send, recv):
        self.source, self.target, self.send, self.recv = source, target, send, recv
        self.me = lax.axis_index("seq")

    def to(self, j):
        peer = lax.rem(self.me + j, SEQ)
        return pltpu.make_async_remote_copy(
            src_ref=self.source.at[rows_of(peer, 16)],
            dst_ref=self.target.at[rows_of(self.me, 16)],
            send_sem=self.send.at[j],
            recv_sem=self.recv.at[j],
            device_id={"seq": peer},
            device_id_type=MESH,
        )

    def start(self, j):
        self.to(j).start()

    def wait_recv(self):
        def body(j, _):
            sender = lax.rem(self.me + SEQ - j, SEQ)
            pltpu.make_async_remote_copy(
                src_ref=self.source.at[rows_of(sender, 16)],
                dst_ref=self.target.at[rows_of(sender, 16)],
                send_sem=self.send.at[j],
                recv_sem=self.recv.at[j],
                device_id={"seq": sender},
                device_id_type=MESH,
            ).wait_recv()
            return 0

        lax.fori_loop(1, SEQ, body, 0)

    def wait_send(self):
        def body(j, _):
            self.to(j).wait_send()
            return 0

        lax.fori_loop(1, SEQ, body, 0)


def kernel(
    lat_hbm, cot_hbm, mod_hbm, wqs_hbm, wos_hbm, wqt_hbm, wot_hbm,
    grad_latents, moments, dqkv_s, dout_s, dqkv_t, dout_t,
    lat, mod, wqs, wos, wqt, wot,
    normed_s, scale_s, modulated_s, packed_s, probs_s, attended_s,
    lat_p, attended_p, branch_s, cot, normed_t, scale_t, modulated_t, packed_t, attended_t, branch_t,
    grad_out, grad_hidden,
    d_branch_s, d_branch_t, d_attended, d_modulated, flipped,
    left_s, right_s, left_in_s, right_in_s, left_t, right_t, left_in_t, right_in_t,
    whole, first_a, first_b, half, second, quarter, third, final, mine, other,
    held, arrived,
    load_sem, send_sem, recv_sem, pair_send, pair_recv, sum_send, sum_recv, clip_send, clip_recv,
):
    place = Place()
    me = place.seq
    here = rows_of(me, 16)
    loads = [
        pltpu.make_async_copy(src, dst, load_sem.at[i])
        for i, (src, dst) in enumerate(
            [
                (lat_hbm, lat), (mod_hbm, mod), (wqs_hbm, wqs), (wos_hbm, wos), (wqt_hbm, wqt), (wot_hbm, wot),
                (lat_hbm.at[here], lat_p.at[here]), (cot_hbm.at[here], cot.at[here]),
            ]
        )
    ]
    for load in loads:
        load.start()

    barrier = pltpu.get_barrier_semaphore()

    def signal(device):
        pl.semaphore_signal(barrier, inc=1, device_id=device, device_id_type=MESH)

    def greet(j, _):
        signal({"seq": lax.rem(me + j, SEQ)})
        return 0

    lax.fori_loop(1, SEQ, greet, 0)
    for j in range(1, 4):
        signal(place.at(x=lax.rem(place.x + j, 4)))
    signal(place.at(y=lax.rem(place.y + 2, 4)))
    signal(place.at(y=3 - place.y))

    @pl.when(place.x != place.z)
    def _():
        signal(place.at(x=place.z, z=place.x))
        signal(place.at(x=place.z, z=place.x, core=1 - place.core))

    loads[0].wait()
    loads[1].wait()
    normalise(lambda rows: lat[rows, :], mod, 0, normed_s, scale_s, modulated_s)
    pl.semaphore_wait(barrier, jnp.where(place.x == place.z, SEQ + 4, SEQ + 6))

    trips = [
        Exchange(source, target, send_sem.at[i], recv_sem.at[i])
        for i, (source, target) in enumerate(
            [(lat_hbm, lat_p), (cot_hbm, cot), (attended_s, attended_p), (grad_out, grad_hidden)]
        )
    ]
    lat_trip, cot_trip, attended_trip, grad_trip = trips
    pair_s = PairTerms(place, left_s, right_s, left_in_s, right_in_s, pair_send.at[0], pair_recv.at[0])
    pair_t = PairTerms(place, left_t, right_t, left_in_t, right_in_t, pair_send.at[1], pair_recv.at[1])
    sums_s, sums_t = [
        [
            Reduction(
                place, p, whole.at[l, p], first_b.at[l] if p == 2 else first_a.at[l, p], half.at[l, p],
                second.at[l, p], quarter.at[l, p], third.at[l, p], final.at[l, p], mine.at[l], other.at[l, p],
                sum_send.at[l, p], sum_recv.at[l, p],
            )
            for p in range(3)
        ]
        for l in range(2)
    ]
    clip = ClipSum(place, held, arrived, clip_send, clip_recv)

    def send_all(trip):
        def body(j, _):
            trip.start(j)
            return 0

        lax.fori_loop(1, SEQ, body, 0)

    send_all(lat_trip)

    loads[2].wait()
    project(modulated_s, wqs, packed_s)
    for h in range(HEADS):
        probs = probabilities(packed_s, h, None)
        probs_s[h] = probs
        attend(probs.astype(BF16), packed_s, h, attended_s)
    send_all(attended_trip)
    send_all(cot_trip)
    attended_p[here, :] = attended_s[here, :]
    right_s[1, :, HE:] = attended_s[...]
    flip(modulated_s, flipped, left_s.at[0])

    loads[3].wait()
    attended_trip.wait_recv()
    project_out(attended_p, wos, branch_s)
    loads[6].wait()
    lat_trip.wait_recv()
    gate_s = mod[2]

    def hidden(rows):
        return (lat_p[rows, :].astype(F32) + gate_s * branch_s[rows, :]).astype(BF16)

    normalise(hidden, mod, 3, normed_t, scale_t, modulated_t)
    loads[4].wait()
    project(modulated_t, wqt, packed_t)
    loads[7].wait()
    cot_trip.wait_recv()
    loads[5].wait()
    gated(cot, mod, 5, d_branch_t)
    d_attended[...] = dot(d_branch_t[...], wot[...], NT).astype(BF16)
    patch_row = lax.rem(lax.broadcasted_iota(jnp.int32, (TOKENS, TOKENS), 0), 16)
    patch_col = lax.rem(lax.broadcasted_iota(jnp.int32, (TOKENS, TOKENS), 1), 16)
    mask = patch_row == patch_col
    for h in range(HEADS):
        probs = probabilities(packed_t, h, mask)
        weights = probs.astype(BF16)
        attend(weights, packed_t, h, attended_t)
        head_backward(probs, weights, packed_t, d_attended, h, right_t)
    right_t[1, :, HE:] = attended_t[...]
    pair_t.start(2)
    project_back(right_t, wqt, d_modulated)

    def send_grad(i):
        @pl.when(i != me)
        def _():
            grad_trip.start(lax.rem(i + SEQ - me, SEQ))

    d_offset, d_stretch, d_gate = normalise_back(
        d_modulated, normed_t, scale_t, mod, 3, cot, grad_out, branch_s, send_grad
    )
    clip_first = held.at[0]
    clip_first[2:3, :] = d_gate
    clip_first[3:4, :] = d_offset
    clip_first[4:5, :] = d_stretch
    grad_hidden[here, :] = grad_out[here, :]
    flip(modulated_t, flipped, left_t.at[0])
    pair_t.start(0)
    flip(d_branch_t, flipped, left_t.at[1])
    pair_t.start(1)
    project_out(attended_t, wot, branch_t)
    clip_first[5:6, :] = gate_sum(cot, branch_t)
    pair_t.wait_recv()
    for p in range(3):
        pair_t.multiply(p, whole.at[1, p].reshape(BLOCKS, BLOCK, PART))
        sums_t[p].stage1()

    grad_trip.wait_recv()
    gated(grad_hidden, mod, 2, d_branch_s)
    d_attended[...] = dot(d_branch_s[...], wos[...], NT).astype(BF16)
    flip(d_branch_s, flipped, left_s.at[1])
    pair_s.start(0)
    pair_s.start(1)
    for h in range(HEADS):
        probs = probs_s[h]
        head_backward(probs, probs.astype(BF16), packed_s, d_attended, h, right_s)
    pair_s.start(2)
    sums_t[0].stage2()
    pair_s.wait_recv()
    for p in range(3):
        pair_s.multiply(p, whole.at[0, p].reshape(BLOCKS, BLOCK, PART))
        sums_s[p].stage1()
    sums_t[1].stage2()
    sums_t[2].stage2()
    project_back(right_s, wqs, d_modulated)
    sums_t[0].stage3()
    d_offset, d_stretch = normalise_back(
        d_modulated, normed_s, scale_s, mod, 0, grad_hidden, grad_latents
    )
    clip_first[0:1, :] = d_offset
    clip_first[1:2, :] = d_stretch
    clip_first[6:8, :] = jnp.zeros((2, D), F32)
    clip.start()
    sums_t[1].stage3()
    sums_t[2].stage3()
    sums_t[0].stage4()
    clip.step(0)
    sums_t[1].stage4()
    sums_t[2].stage4()
    clip.step(1)
    for p in range(3):
        sums_s[p].stage2()
    clip.step(2)
    results_t = [sums.stage5() for sums in sums_t]
    write_rows(results_t, dqkv_t, dout_t)
    for p in range(3):
        sums_s[p].stage3()
    clip.step(3)
    for i in range(6):
        moments[i] = held[4, i : i + 1, :]
    for p in range(3):
        sums_s[p].stage4()
    for part in (*trips, pair_s, pair_t, *sums_t, clip):
        part.wait_send()
    results_s = [sums.stage5() for sums in sums_s]
    write_rows(results_s, dqkv_s, dout_s)
    for part in sums_s:
        part.wait_send()


def write_rows(results, dqkv, dout):
    for p, (low, high) in enumerate(results):
        dqkv[:, PART * p : PART * p + PART] = low
        start = 2 * HE + PART * p
        if p == 0:
            dqkv[:, start : start + PART] = high
        elif p == 1:
            dqkv[:, start:] = high[:, : PACKED - start]
            dout[:, : PART - (PACKED - start)] = high[:, PACKED - start :]
        else:
            dout[:, start - PACKED :] = high


def copy_out(*refs):
    sources, targets, sems = refs[:6], refs[6:12], refs[12]
    copies = [pltpu.make_async_copy(a, b, sems.at[i]) for i, (a, b) in enumerate(zip(sources, targets))]
    for copy in copies:
        copy.start()
    for copy in copies:
        copy.wait()


def local(latents, cotangent, modulation, spatial_qkv, spatial_out, temporal_qkv, temporal_out):
    vm = pl.BlockSpec(memory_space=pltpu.VMEM)
    hbm = pl.BlockSpec(memory_space=pl.ANY)
    sds = jax.ShapeDtypeStruct

    def bf16(*shape):
        return pltpu.VMEM(shape, BF16)

    def f32(*shape):
        return pltpu.VMEM(shape, F32)

    wide, wide32, column, narrow = bf16(TOKENS, D), f32(TOKENS, D), f32(TOKENS, 1), bf16(TOKENS, HE)
    three, wq, wo = bf16(TOKENS, PACKED), bf16(PACKED, D), bf16(HE, D)
    left, right = bf16(2, BLOCKS, BLOCK, TOKENS), bf16(2, TOKENS, 2 * HE)
    right_in = bf16(TOKENS, 2 * HE)
    dma = pltpu.SemaphoreType.DMA
    shapes = [
        sds((TOKENS, D), BF16),
        sds((6, 1, D), F32),
        sds((9, PACKED), F32),
        sds((9, HE), F32),
        sds((9, PACKED), F32),
        sds((9, HE), F32),
    ]
    outs = pl.pallas_call(
        kernel,
        out_shape=shapes,
        in_specs=[hbm] * 7,
        out_specs=[vm] * 6,
        scratch_shapes=[
            wide, f32(6, 1, D), wq, wo, wq, wo,
            wide32, column, wide, three, f32(HEADS, TOKENS, TOKENS), narrow,
            wide, narrow, wide32, wide, wide32, column, wide, three, narrow, wide32,
            wide, wide,
            wide, wide, narrow, wide, f32(D, TOKENS),
            left, right, left, right_in, left, right, left, right_in,
            bf16(2, 3, 2, 4, 2, BLOCK, PART), bf16(2, 2, 3, 2, 2, BLOCK, PART), bf16(2, 3, 4, BLOCK, PART),
            bf16(2, 3, 4, BLOCK, PART), bf16(2, 3, 3, BLOCK, PART), bf16(2, 3, BLOCK, PART),
            bf16(2, 3, 3, 32, PART), f32(2, 3, 32, PART), f32(2, 32, PART), f32(2, 3, 32, PART),
            f32(5, 8, D), f32(4, 8, D),
            dma((8,)), dma((4, SEQ)), dma((4, SEQ)), dma((2, 3)), dma((2, 3)),
            dma((2, 3, 11)), dma((2, 3, 11)), dma((4,)), dma((4,)),
        ],
        compiler_params=pltpu.CompilerParams(
            collective_id=0, has_side_effects=True, vmem_limit_bytes=62 * 2**20
        ),
    )(
        latents.reshape(TOKENS, D), cotangent.reshape(TOKENS, D), modulation.transpose(1, 0, 2),
        spatial_qkv.T, spatial_out.T, temporal_qkv.T, temporal_out.T,
    )
    grad, moments, *grads = pl.pallas_call(
        copy_out,
        out_shape=shapes,
        in_specs=[hbm] * 6,
        out_specs=[hbm] * 6,
        scratch_shapes=[dma((6,))],
    )(*outs)
    return (grad.reshape(latents.shape), moments.transpose(1, 0, 2), *grads)


def solution(mesh):
    in_specs = (
        P("dp", "seq", None, None),
        P("dp", "seq", None, None),
        P("dp", None, None),
        P(),
        P(),
        P(),
        P(),
    )
    out_specs = (
        P("dp", "seq", None, None),
        P("dp", None, None),
        P(("dp", "seq"), None),
        P(("dp", "seq"), None),
        P(("dp", "seq"), None),
        P(("dp", "seq"), None),
    )
    return jax.shard_map(local, mesh=mesh, in_specs=in_specs, out_specs=out_specs, check_vma=False)
```

time: 115 us -> 136 us (1.18)
  the two profiles are of different devices: /device:TPU:1 before, /device:TPU:5 now
where the time goes in v3:
time: 136 us
  Pallas kernels  135 us (99%)
    pallas_call x1, Pallas kernels, local(): pl.pallas_call(kernel, out_shape=shapes, in_specs=[hbm] * 7, out_specs=[v...  106 us
    pallas_call x1, Pallas kernels, local(): pl.pallas_call(copy_out, out_shape=shapes, in_specs=[hbm] * 6, out_specs=...  29.3 us

profile of v3, /device:TPU:5, one launch (start us, length us, event | category | flops | bytes accessed | tf_op | source)
XLA Modules:
  0.0 135.6 jit_solution(1046654806487274482)
XLA Ops:
  0.6 105.5 %shard_map.118 = (bf16[256,1152]{1,0:T(8,128)(2,1)}, f32[6,1,1152]{2,1,0:T(1,128)}, f32[9,1728]{1,0:T(8,128)}, f32[9,576]{1,0:T(8,128)}, f32[9,1728]{1,0:T(8,128)}, /*index=5*/f32[9,576]{1,0:T(8,128)}) custom-call(bf16[256,1152]{1,0:T(8,128)(2,1)} %bitcast.13, bf16[256,1152]{1,0:T(8,128)(2,1)} %bitcast.14, f32[6,1,1152]{2,1,0:T(1,128)} %bitcast.15, ...), custom_call_target="tpu_custom_call" | custom-call | tf_op jit(solution)/shard_map/pallas_call | solution.py:673
  106.2 29.3 %shard_map.119 = (bf16[256,1152]{1,0:T(8,128)(2,1)}, f32[6,1,1152]{2,1,0:T(1,128)}, f32[9,1728]{1,0:T(8,128)}, f32[9,576]{1,0:T(8,128)}, f32[9,1728]{1,0:T(8,128)}, /*index=5*/f32[9,576]{1,0:T(8,128)}) custom-call(bf16[256,1152]{1,0:T(8,128)(2,1)} %get-tuple-element.18.refs_0_, f32[6,1,1152]{2,1,0:T(1,128)} %get-tuple-element.19.refs_1_, ...), custom_call_target="tpu_custom_call" | custom-call | tf_op jit(solution)/shard_map/pallas_call | solution.py:699

commit v4 on v3

--- a/solution.py
+++ b/solution.py
@@ -36,13 +36,15 @@
     return pl.ds(pl.multiple_of(i * size, size), size)
 
 
-def normalise(read, mod, row, normed, scale, modulated):
+def chunks(size=32):
+    return [slice(i, i + size) for i in range(0, TOKENS, size)]
+
+
+def normalise(source, mod, row, normed, scale, modulated):
     offset = mod[row]
     stretch = 1.0 + mod[row + 1]
-
-    def body(i, _):
-        rows = rows_of(i, 32)
-        x = read(rows).astype(F32)
+    for rows in chunks():
+        x = source[rows, :].astype(F32)
         centred = x - jnp.mean(x, axis=-1, keepdims=True)
         spread = jnp.mean(centred * centred, axis=-1, keepdims=True)
         inverse = lax.rsqrt(spread + EPSILON)
@@ -50,38 +52,19 @@
         normed[rows, :] = n
         scale[rows, :] = inverse
         modulated[rows, :] = (n * stretch + offset).astype(BF16)
-        return 0
-
-    lax.fori_loop(0, TOKENS // 32, body, 0)
 
 
 def project(modulated, weight, packed):
-    def body(i, _):
-        cols = rows_of(i, 256)
-        packed[:, cols] = dot(modulated[...], weight[cols, :], NT).astype(BF16)
-        return 0
-
-    lax.fori_loop(0, 6, body, 0)
-    packed[:, 1536:PACKED] = dot(modulated[...], weight[1536:PACKED, :], NT).astype(BF16)
+    packed[...] = dot(modulated[...], weight[...], NT).astype(BF16)
 
 
 def project_out(attended, weight, out):
-    def body(i, _):
-        cols = rows_of(i, 384)
-        out[:, cols] = dot(attended[...], weight[:, cols])
-        return 0
-
-    lax.fori_loop(0, 3, body, 0)
+    out[...] = dot(attended[...], weight[...])
 
 
 def project_back(right, weight, out):
-    def body(i, _):
-        cols = rows_of(i, 384)
-        total = dot(right[0], weight[: 2 * HE, cols]) + dot(right[1, :, :HE], weight[2 * HE :, cols])
-        out[:, cols] = total.astype(BF16)
-        return 0
-
-    lax.fori_loop(0, 3, body, 0)
+    total = dot(right[0], weight[: 2 * HE, :]) + dot(right[2, :, :HE], weight[2 * HE :, :])
+    out[...] = total.astype(BF16)
 
 
 def head(ref, h, section=0):
@@ -90,27 +73,27 @@
 
 
 def probabilities(packed, h, mask):
-    scores = dot(head(packed, h, 0), head(packed, h, 1), NT)
+    scores = dot(head(packed, h, 1), head(packed, h, 0), NT)
     raised = jnp.exp(scores * FACTOR)
     if mask is not None:
         raised = jnp.where(mask, raised, 0.0)
-    return raised / jnp.sum(raised, axis=-1, keepdims=True)
+    return raised * (1.0 / jnp.sum(raised, axis=0, keepdims=True))
 
 
 def head_backward(probs, weights, packed, d_attended, h, right):
     d_head = head(d_attended, h)
-    d_weights = dot(d_head, head(packed, h, 2), NT)
-    carried = jnp.sum(d_weights * probs, axis=-1, keepdims=True)
+    d_weights = dot(head(packed, h, 2), d_head, NT)
+    carried = jnp.sum(d_weights * probs, axis=0, keepdims=True)
     d_scores = (probs * (d_weights - carried) * FACTOR).astype(BF16)
     lane = h * HEAD_DIM
-    right[0, :, lane : lane + HEAD_DIM] = dot(d_scores, head(packed, h, 1)).astype(BF16)
-    right[0, :, HE + lane : HE + lane + HEAD_DIM] = dot(d_scores, head(packed, h, 0), TN).astype(BF16)
-    right[1, :, lane : lane + HEAD_DIM] = dot(weights, d_head, TN).astype(BF16)
+    right[0, :, lane : lane + HEAD_DIM] = dot(d_scores, head(packed, h, 1), TN).astype(BF16)
+    right[0, :, HE + lane : HE + lane + HEAD_DIM] = dot(d_scores, head(packed, h, 0)).astype(BF16)
+    right[2, :, lane : lane + HEAD_DIM] = dot(weights, d_head).astype(BF16)
 
 
 def attend(weights, packed, h, attended):
     lane = h * HEAD_DIM
-    attended[:, lane : lane + HEAD_DIM] = dot(weights, head(packed, h, 2)).astype(BF16)
+    attended[:, lane : lane + HEAD_DIM] = dot(weights, head(packed, h, 2), TN).astype(BF16)
 
 
 def fold(x):
@@ -118,61 +101,29 @@
 
 
 def gated(source, mod, row, out):
-    gate = mod[row]
-
-    def body(i, _):
-        rows = rows_of(i, 32)
-        out[rows, :] = (source[rows, :].astype(F32) * gate).astype(BF16)
-        return 0
-
-    lax.fori_loop(0, TOKENS // 32, body, 0)
+    out[...] = (source[...].astype(F32) * mod[row]).astype(BF16)
 
 
 def gate_sum(upstream, branch):
-    def body(i, total):
-        rows = rows_of(i, 32)
-        return total + fold(upstream[rows, :].astype(F32) * branch[rows, :])
-
-    total = lax.fori_loop(0, TOKENS // 32, body, jnp.zeros((8, D), F32))
+    total = jnp.zeros((8, D), F32)
+    for rows in chunks():
+        total = total + fold(upstream[rows, :].astype(F32) * branch[rows, :])
     return jnp.sum(total, axis=0, keepdims=True)
 
 
-def normalise_back(d_modulated, normed, scale, mod, row, upstream, out, branch=None, after=None):
+def normalise_back(d_modulated, normed, scale, mod, row, upstream, out):
     stretch = 1.0 + mod[row + 1]
-
-    def body(i, totals):
-        rows = rows_of(i, 16)
+    totals = [jnp.zeros((8, D), F32)] * 2
+    for rows in chunks():
         g = d_modulated[rows, :].astype(F32)
         n = normed[rows, :]
         dn = g * stretch
         first = jnp.mean(dn, axis=-1, keepdims=True)
         second = jnp.mean(dn * n, axis=-1, keepdims=True)
         dx = scale[rows, :] * (dn - first - n * second)
-        value = (upstream[rows, :].astype(F32) + dx).astype(BF16)
-        out[rows, :] = value
-        terms = [g, g * n]
-        if branch is not None:
-            terms.append(value.astype(F32) * branch[rows, :])
-        if after is not None:
-            after(i)
-        return tuple(total + fold(term) for total, term in zip(totals, terms))
-
-    zero = jnp.zeros((8, D), F32)
-    totals = lax.fori_loop(0, TOKENS // 16, body, (zero,) * (2 if branch is None else 3))
-    return tuple(jnp.sum(t, axis=0, keepdims=True) for t in totals)
-
-
-def flip(source, flipped, left):
-    def turn(i, _):
-        cols = rows_of(i, 128)
-        flipped[cols, :] = source[:, cols].astype(F32).T
-        return 0
-
-    lax.fori_loop(0, D // 128, turn, 0)
-    empty = jnp.zeros((BLOCK - 72, TOKENS), F32)
-    for k in range(BLOCKS):
-        rows = flipped[72 * k : 72 * k + 72, :]
-        left[k] = jnp.concatenate([rows, empty], axis=0).astype(BF16)
+        out[rows, :] = (upstream[rows, :].astype(F32) + dx).astype(BF16)
+        totals = [total + fold(term) for total, term in zip(totals, (g, g * n))]
+    return [jnp.sum(t, axis=0, keepdims=True) for t in totals]
 
 
 def swap1(i):
@@ -208,14 +159,15 @@
 
 
 class PairTerms:
-    def __init__(self, place, left, right, left_in, right_in, send, recv):
+    def __init__(self, place, left, right, send, recv):
         self.core = place.core
         other = place.at(core=1 - place.core)
-        self.left, self.right, self.left_in, self.right_in = left, right, left_in, right_in
+        away = 2 - 2 * place.core
+        self.left, self.right = left, right
         self.copies = [
-            remote(left.at[0], left_in.at[0], send.at[0], recv.at[0], other),
-            remote(left.at[1], left_in.at[1], send.at[1], recv.at[1], other),
-            remote(right.at[1 - place.core], right_in, send.at[2], recv.at[2], other),
+            remote(left.at[0, 0], left.at[0, 1], send.at[0], recv.at[0], other),
+            remote(left.at[1, 0], left.at[1, 1], send.at[1], recv.at[1], other),
+            remote(right.at[away], right.at[away + 1], send.at[2], recv.at[2], other),
         ]
 
     def start(self, i):
@@ -239,18 +191,12 @@
         pieces = [(first, first + PART)]
         if part == 1:
             pieces = [(first, HE), (HE, first + PART)]
-
-        def body(i, _):
-            blocks = pl.ds(4 * i, 4)
-            for low, high in pieces:
-                left = 0 if high <= HE else self.core
-                own = self.left[left, blocks].reshape(4 * BLOCK, TOKENS)
-                theirs = self.left_in[left, blocks].reshape(4 * BLOCK, TOKENS)
-                total = dot(own, self.right[self.core, :, low:high]) + dot(theirs, self.right_in[:, low:high])
-                out[blocks, :, low - first : high - first] = total.astype(BF16).reshape(4, BLOCK, high - low)
-            return 0
-
-        lax.fori_loop(0, BLOCKS // 4, body, 0)
+        for low, high in pieces:
+            left = self.left[0 if high <= HE else self.core].reshape(2 * TOKENS, D)
+            right = self.right[pl.ds(2 * self.core, 2), :, low:high].reshape(2 * TOKENS, high - low)
+            total = dot(left, right, TN)
+            for k in range(BLOCKS):
+                out[k, :72, low - first : high - first] = total[72 * k : 72 * k + 72].astype(BF16)
 
 
 class Reduction:
@@ -425,11 +371,9 @@
     lat_hbm, cot_hbm, mod_hbm, wqs_hbm, wos_hbm, wqt_hbm, wot_hbm,
     grad_latents, moments, dqkv_s, dout_s, dqkv_t, dout_t,
     lat, mod, wqs, wos, wqt, wot,
-    normed_s, scale_s, modulated_s, packed_s, probs_s, attended_s,
-    lat_p, attended_p, branch_s, cot, normed_t, scale_t, modulated_t, packed_t, attended_t, branch_t,
-    grad_out, grad_hidden,
-    d_branch_s, d_branch_t, d_attended, d_modulated, flipped,
-    left_s, right_s, left_in_s, right_in_s, left_t, right_t, left_in_t, right_in_t,
+    normed_s, scale_s, packed_s, probs_s, attended_s, branch_s, hidden_out, hidden,
+    cot, normed_t, scale_t, packed_t, attended_t, branch_t, grad_out, grad_hidden, d_attended, d_modulated,
+    left_s, right_s, left_t, right_t,
     whole, first_a, first_b, half, second, quarter, third, final, mine, other,
     held, arrived,
     load_sem, send_sem, recv_sem, pair_send, pair_recv, sum_send, sum_recv, clip_send, clip_recv,
@@ -437,12 +381,14 @@
     place = Place()
     me = place.seq
     here = rows_of(me, 16)
+    modulated_s, d_branch_s = left_s.at[0, 0], left_s.at[1, 0]
+    modulated_t, d_branch_t = left_t.at[0, 0], left_t.at[1, 0]
     loads = [
         pltpu.make_async_copy(src, dst, load_sem.at[i])
         for i, (src, dst) in enumerate(
             [
                 (lat_hbm, lat), (mod_hbm, mod), (wqs_hbm, wqs), (wos_hbm, wos), (wqt_hbm, wqt), (wot_hbm, wot),
-                (lat_hbm.at[here], lat_p.at[here]), (cot_hbm.at[here], cot.at[here]),
+                (cot_hbm.at[here], cot.at[here]),
             ]
         )
     ]
@@ -471,18 +417,18 @@
 
     loads[0].wait()
     loads[1].wait()
-    normalise(lambda rows: lat[rows, :], mod, 0, normed_s, scale_s, modulated_s)
+    normalise(lat, mod, 0, normed_s, scale_s, modulated_s)
     pl.semaphore_wait(barrier, jnp.where(place.x == place.z, SEQ + 4, SEQ + 6))
 
     trips = [
         Exchange(source, target, send_sem.at[i], recv_sem.at[i])
         for i, (source, target) in enumerate(
-            [(lat_hbm, lat_p), (cot_hbm, cot), (attended_s, attended_p), (grad_out, grad_hidden)]
+            [(cot_hbm, cot), (hidden_out, hidden), (grad_out, grad_hidden)]
         )
     ]
-    lat_trip, cot_trip, attended_trip, grad_trip = trips
-    pair_s = PairTerms(place, left_s, right_s, left_in_s, right_in_s, pair_send.at[0], pair_recv.at[0])
-    pair_t = PairTerms(place, left_t, right_t, left_in_t, right_in_t, pair_send.at[1], pair_recv.at[1])
+    cot_trip, hidden_trip, grad_trip = trips
+    pair_s = PairTerms(place, left_s, right_s, pair_send.at[0], pair_recv.at[0])
+    pair_t = PairTerms(place, left_t, right_t, pair_send.at[1], pair_recv.at[1])
     sums_s, sums_t = [
         [
             Reduction(
@@ -497,13 +443,10 @@
     clip = ClipSum(place, held, arrived, clip_send, clip_recv)
 
     def send_all(trip):
-        def body(j, _):
+        for j in range(1, SEQ):
             trip.start(j)
-            return 0
-
-        lax.fori_loop(1, SEQ, body, 0)
-
-    send_all(lat_trip)
+
+    send_all(cot_trip)
 
     loads[2].wait()
     project(modulated_s, wqs, packed_s)
@@ -511,30 +454,26 @@
         probs = probabilities(packed_s, h, None)
         probs_s[h] = probs
         attend(probs.astype(BF16), packed_s, h, attended_s)
-    send_all(attended_trip)
-    send_all(cot_trip)
-    attended_p[here, :] = attended_s[here, :]
-    right_s[1, :, HE:] = attended_s[...]
-    flip(modulated_s, flipped, left_s.at[0])
-
     loads[3].wait()
-    attended_trip.wait_recv()
-    project_out(attended_p, wos, branch_s)
+    project_out(attended_s, wos, branch_s)
+    for rows in chunks():
+        hidden_out[rows, :] = (lat[rows, :].astype(F32) + mod[2] * branch_s[rows, :]).astype(BF16)
+    send_all(hidden_trip)
+    hidden[here, :] = hidden_out[here, :]
+    right_s[2, :, HE:] = attended_s[...]
+    pair_s.start(0)
+
     loads[6].wait()
-    lat_trip.wait_recv()
-    gate_s = mod[2]
-
-    def hidden(rows):
-        return (lat_p[rows, :].astype(F32) + gate_s * branch_s[rows, :]).astype(BF16)
-
-    normalise(hidden, mod, 3, normed_t, scale_t, modulated_t)
-    loads[4].wait()
-    project(modulated_t, wqt, packed_t)
-    loads[7].wait()
     cot_trip.wait_recv()
     loads[5].wait()
     gated(cot, mod, 5, d_branch_t)
     d_attended[...] = dot(d_branch_t[...], wot[...], NT).astype(BF16)
+    pair_t.start(1)
+    hidden_trip.wait_recv()
+    normalise(hidden, mod, 3, normed_t, scale_t, modulated_t)
+    pair_t.start(0)
+    loads[4].wait()
+    project(modulated_t, wqt, packed_t)
     patch_row = lax.rem(lax.broadcasted_iota(jnp.int32, (TOKENS, TOKENS), 0), 16)
     patch_col = lax.rem(lax.broadcasted_iota(jnp.int32, (TOKENS, TOKENS), 1), 16)
     mask = patch_row == patch_col
@@ -543,74 +482,59 @@
         weights = probs.astype(BF16)
         attend(weights, packed_t, h, attended_t)
         head_backward(probs, weights, packed_t, d_attended, h, right_t)
-    right_t[1, :, HE:] = attended_t[...]
+    right_t[2, :, HE:] = attended_t[...]
     pair_t.start(2)
     project_back(right_t, wqt, d_modulated)
-
-    def send_grad(i):
-        @pl.when(i != me)
-        def _():
-            grad_trip.start(lax.rem(i + SEQ - me, SEQ))
-
-    d_offset, d_stretch, d_gate = normalise_back(
-        d_modulated, normed_t, scale_t, mod, 3, cot, grad_out, branch_s, send_grad
+    d_offset, d_stretch = normalise_back(
+        d_modulated, normed_t, scale_t, mod, 3, cot, grad_out
     )
+    send_all(grad_trip)
     clip_first = held.at[0]
-    clip_first[2:3, :] = d_gate
     clip_first[3:4, :] = d_offset
     clip_first[4:5, :] = d_stretch
     grad_hidden[here, :] = grad_out[here, :]
-    flip(modulated_t, flipped, left_t.at[0])
-    pair_t.start(0)
-    flip(d_branch_t, flipped, left_t.at[1])
-    pair_t.start(1)
+    pair_t.wait_recv()
+    for p in range(3):
+        pair_t.multiply(p, whole.at[1, p].reshape(BLOCKS, BLOCK, PART))
+        sums_t[p].stage1()
     project_out(attended_t, wot, branch_t)
     clip_first[5:6, :] = gate_sum(cot, branch_t)
-    pair_t.wait_recv()
-    for p in range(3):
-        pair_t.multiply(p, whole.at[1, p].reshape(BLOCKS, BLOCK, PART))
-        sums_t[p].stage1()
 
     grad_trip.wait_recv()
     gated(grad_hidden, mod, 2, d_branch_s)
+    pair_s.start(1)
     d_attended[...] = dot(d_branch_s[...], wos[...], NT).astype(BF16)
-    flip(d_branch_s, flipped, left_s.at[1])
-    pair_s.start(0)
-    pair_s.start(1)
     for h in range(HEADS):
         probs = probs_s[h]
         head_backward(probs, probs.astype(BF16), packed_s, d_attended, h, right_s)
     pair_s.start(2)
-    sums_t[0].stage2()
     pair_s.wait_recv()
     for p in range(3):
         pair_s.multiply(p, whole.at[0, p].reshape(BLOCKS, BLOCK, PART))
         sums_s[p].stage1()
-    sums_t[1].stage2()
-    sums_t[2].stage2()
     project_back(right_s, wqs, d_modulated)
-    sums_t[0].stage3()
     d_offset, d_stretch = normalise_back(
         d_modulated, normed_s, scale_s, mod, 0, grad_hidden, grad_latents
     )
     clip_first[0:1, :] = d_offset
     clip_first[1:2, :] = d_stretch
+    clip_first[2:3, :] = gate_sum(grad_hidden, branch_s)
     clip_first[6:8, :] = jnp.zeros((2, D), F32)
     clip.start()
-    sums_t[1].stage3()
-    sums_t[2].stage3()
-    sums_t[0].stage4()
+    for p in range(3):
+        sums_t[p].stage2()
     clip.step(0)
-    sums_t[1].stage4()
-    sums_t[2].stage4()
+    for p in range(3):
+        sums_t[p].stage3()
     clip.step(1)
     for p in range(3):
         sums_s[p].stage2()
+    for p in range(3):
+        sums_t[p].stage4()
     clip.step(2)
-    results_t = [sums.stage5() for sums in sums_t]
-    write_rows(results_t, dqkv_t, dout_t)
     for p in range(3):
         sums_s[p].stage3()
+    write_rows([sums.stage5() for sums in sums_t], dqkv_t, dout_t)
     clip.step(3)
     for i in range(6):
         moments[i] = held[4, i : i + 1, :]
@@ -638,12 +562,8 @@
 
 
 def copy_out(*refs):
-    sources, targets, sems = refs[:6], refs[6:12], refs[12]
-    copies = [pltpu.make_async_copy(a, b, sems.at[i]) for i, (a, b) in enumerate(zip(sources, targets))]
-    for copy in copies:
-        copy.start()
-    for copy in copies:
-        copy.wait()
+    for source, target in zip(refs[:6], refs[6:]):
+        target[...] = source[...]
 
 
 def local(latents, cotangent, modulation, spatial_qkv, spatial_out, temporal_qkv, temporal_out):
@@ -659,8 +579,7 @@
 
     wide, wide32, column, narrow = bf16(TOKENS, D), f32(TOKENS, D), f32(TOKENS, 1), bf16(TOKENS, HE)
     three, wq, wo = bf16(TOKENS, PACKED), bf16(PACKED, D), bf16(HE, D)
-    left, right = bf16(2, BLOCKS, BLOCK, TOKENS), bf16(2, TOKENS, 2 * HE)
-    right_in = bf16(TOKENS, 2 * HE)
+    left, right = bf16(2, 2, TOKENS, D), bf16(4, TOKENS, 2 * HE)
     dma = pltpu.SemaphoreType.DMA
     shapes = [
         sds((TOKENS, D), BF16),
@@ -677,16 +596,14 @@
         out_specs=[vm] * 6,
         scratch_shapes=[
             wide, f32(6, 1, D), wq, wo, wq, wo,
-            wide32, column, wide, three, f32(HEADS, TOKENS, TOKENS), narrow,
-            wide, narrow, wide32, wide, wide32, column, wide, three, narrow, wide32,
-            wide, wide,
-            wide, wide, narrow, wide, f32(D, TOKENS),
-            left, right, left, right_in, left, right, left, right_in,
+            wide32, column, three, f32(HEADS, TOKENS, TOKENS), narrow, wide32, wide, wide,
+            wide, wide32, column, three, narrow, wide32, wide, wide, narrow, wide,
+            left, right, left, right,
             bf16(2, 3, 2, 4, 2, BLOCK, PART), bf16(2, 2, 3, 2, 2, BLOCK, PART), bf16(2, 3, 4, BLOCK, PART),
             bf16(2, 3, 4, BLOCK, PART), bf16(2, 3, 3, BLOCK, PART), bf16(2, 3, BLOCK, PART),
             bf16(2, 3, 3, 32, PART), f32(2, 3, 32, PART), f32(2, 32, PART), f32(2, 3, 32, PART),
             f32(5, 8, D), f32(4, 8, D),
-            dma((8,)), dma((4, SEQ)), dma((4, SEQ)), dma((2, 3)), dma((2, 3)),
+            dma((7,)), dma((3, SEQ)), dma((3, SEQ)), dma((2, 3)), dma((2, 3)),
             dma((2, 3, 11)), dma((2, 3, 11)), dma((4,)), dma((4,)),
         ],
         compiler_params=pltpu.CompilerParams(
@@ -699,9 +616,8 @@
     grad, moments, *grads = pl.pallas_call(
         copy_out,
         out_shape=shapes,
-        in_specs=[hbm] * 6,
-        out_specs=[hbm] * 6,
-        scratch_shapes=[dma((6,))],
+        in_specs=[vm] * 6,
+        out_specs=[vm] * 6,
     )(*outs)
     return (grad.reshape(latents.shape), moments.transpose(1, 0, 2), *grads)
 

time: 136 us -> 89.4 us (0.66)
  Pallas kernels: 135 us -> 87.2 us
    pallas_call x1, Pallas kernels: 29.3 us -> 2.1 us  [local(): pl.pallas_call(copy_out, out_shape=shapes, in_specs=[vm] * 6, out_specs=[...]
    pallas_call x1, Pallas kernels: 106 us -> 85.1 us  [local(): pl.pallas_call(kernel, out_shape=shapes, in_specs=[hbm] * 7, out_specs=[v...]
where the time goes in v4:
time: 89.4 us; the launch traced here: 87.9 us
  Pallas kernels  87.2 us (98%)
    pallas_call x1, Pallas kernels, local(): pl.pallas_call(kernel, out_shape=shapes, in_specs=[hbm] * 7, out_specs=[v...  85.1 us
    pallas_call x1, Pallas kernels, local(): pl.pallas_call(copy_out, out_shape=shapes, in_specs=[vm] * 6, out_specs=[...  2.1 us

profile of v4, /device:TPU:5, one launch (start us, length us, event | category | flops | bytes accessed | tf_op | source)
XLA Modules:
  0.0 87.9 jit_solution(18412567171607856878)
XLA Ops:
  0.6 85.1 %shard_map.118 = (bf16[256,1152]{1,0:T(8,128)(2,1)}, f32[6,1,1152]{2,1,0:T(1,128)}, f32[9,1728]{1,0:T(8,128)}, f32[9,576]{1,0:T(8,128)}, f32[9,1728]{1,0:T(8,128)}, /*index=5*/f32[9,576]{1,0:T(8,128)}) custom-call(bf16[256,1152]{1,0:T(8,128)(2,1)} %bitcast.13, bf16[256,1152]{1,0:T(8,128)(2,1)} %bitcast.14, f32[6,1,1152]{2,1,0:T(1,128)} %bitcast.15, ...), custom_call_target="tpu_custom_call" | custom-call | tf_op jit(solution)/shard_map/pallas_call | solution.py:592
  85.8 2.1 %shard_map.119 = (bf16[256,1152]{1,0:T(8,128)(2,1)}, f32[6,1,1152]{2,1,0:T(1,128)}, f32[9,1728]{1,0:T(8,128)}, f32[9,576]{1,0:T(8,128)}, f32[9,1728]{1,0:T(8,128)}, /*index=5*/f32[9,576]{1,0:T(8,128)}) custom-call(bf16[256,1152]{1,0:T(8,128)(2,1)} %get-tuple-element.18.refs_0_, f32[6,1,1152]{2,1,0:T(1,128)} %get-tuple-element.19.refs_1_, ...), custom_call_target="tpu_custom_call" | custom-call | tf_op jit(solution)/shard_map/pallas_call | solution.py:616

commit v5 on v4

--- a/solution.py
+++ b/solution.py
@@ -16,7 +16,7 @@
 SEQ = 16
 EPSILON = 1e-06
 FACTOR = HEAD_DIM**-0.5
-BLOCKS = 16
+SLAB = 144
 BLOCK = 80
 PART = 384
 MESH = pl.DeviceIdType.MESH
@@ -151,6 +151,10 @@
             "seq": 8 * lax.rem(y, 2) + 2 * z + core,
         }
 
+    def pair(self, i):
+        near, far = swap1(i), 3 - i
+        return near + self.core * (far - near), far + self.core * (near - far)
+
 
 def remote(src, dst, send, recv, device):
     return pltpu.make_async_remote_copy(
@@ -195,39 +199,41 @@
             left = self.left[0 if high <= HE else self.core].reshape(2 * TOKENS, D)
             right = self.right[pl.ds(2 * self.core, 2), :, low:high].reshape(2 * TOKENS, high - low)
             total = dot(left, right, TN)
-            for k in range(BLOCKS):
-                out[k, :72, low - first : high - first] = total[72 * k : 72 * k + 72].astype(BF16)
+            for yh in range(2):
+                for x in range(4):
+                    row = SLAB * (4 * yh + x)
+                    out[yh, x, :, low - first : high - first] = total[row : row + SLAB].astype(BF16)
 
 
 class Reduction:
-    def __init__(self, place, part, whole, first, half, second, quarter, third, final, mine, other, send, recv):
-        self.place, self.part = place, part
-        self.whole, self.first, self.half, self.second = whole, first, half, second
+    def __init__(self, place, names, whole, first, pair, half, second, quarter, third, final, mine, other, send, recv):
+        self.place, self.names = place, names
+        self.whole, self.first, self.pair, self.half, self.second = whole, first, pair, half, second
         self.quarter, self.third, self.final, self.mine, self.other = quarter, third, final, mine, other
-        names = ("zyx", "xyz", "yxz")[part]
         self.at = [getattr(place, name) for name in names]
-        self.copies = []
-        for stage, name in enumerate(names):
+        a = self.at[0]
+        a1, self.a2 = place.pair(a)
+        to_a1, to_a2 = place.at(**{names[0]: a1}), place.at(**{names[0]: self.a2})
+        self.copies = [
+            remote(whole.at[:, lax.rem(a + 2, 4)], first.at[1], send.at[0], recv.at[0], to_a1),
+            remote(whole.at[:, a1], first.at[0], send.at[1], recv.at[1], to_a1),
+            remote(whole.at[:, self.a2], pair, send.at[2], recv.at[2], to_a2),
+        ]
+        for stage in (1, 2):
             for j in range(1, 4):
                 peer = lax.rem(self.at[stage] + j, 4)
-                src, dst = (
-                    lambda: (self.slab(peer), first.at[j - 1]),
-                    lambda: (half.at[peer], second.at[j - 1]),
-                    lambda: (quarter.at[window(peer)], third.at[j - 1]),
-                )[stage]()
+                if stage == 1:
+                    src, dst = half.at[peer], second.at[j - 1]
+                else:
+                    src, dst = quarter.at[window(peer)], third.at[j - 1]
                 i = 3 * stage + j - 1
-                self.copies.append(remote(src, dst, send.at[i], recv.at[i], place.at(**{name: peer})))
-        if part == 0:
-            to = [place.at(x=place.z, z=place.x, core=c) for c in (1 - place.core, place.core)]
-            self.copies.append(remote(final, other, send.at[9], recv.at[9], to[0]))
-            self.trade = remote(final, mine, send.at[10], recv.at[10], to[1])
-        else:
-            self.copies.append(remote(final, other, send.at[9], recv.at[9], place.at(core=1 - place.core)))
-
-    def slab(self, i):
-        if self.part == 2:
-            return self.whole.at[lax.div(i, 2), :, lax.rem(i, 2)]
-        return self.whole.at[:, i]
+                self.copies.append(remote(src, dst, send.at[i], recv.at[i], place.at(**{names[stage]: peer})))
+        turned = {n: getattr(place, m) for n, m in zip("xyz", names)}
+        self.trades = names != "xyz"
+        self.moves = place.x != getattr(place, names[0])
+        core = 1 - place.core
+        self.copies.append(remote(final, other, send.at[9], recv.at[9], place.at(**turned, core=core)))
+        self.trade = remote(final, mine, send.at[10], recv.at[10], place.at(**turned)) if self.trades else None
 
     def start(self, stage):
         for i in range(3 * stage, 3 * stage + 3):
@@ -237,18 +243,25 @@
         for i in range(3 * stage, 3 * stage + 3):
             self.copies[i].wait_recv()
 
+    def stage0(self):
+        self.copies[0].start()
+        self.copies[1].start()
+
     def stage1(self):
-        self.start(0)
+        self.copies[0].wait_recv()
+        for yh in range(2):
+            kept = self.whole.at[yh, self.a2]
+            kept[...] = (kept[...].astype(F32) + self.first[1, yh].astype(F32)).astype(BF16)
+        self.copies[2].start()
 
     def stage2(self):
-        self.wait(0)
-        own = self.slab(self.at[0])
-        for j in range(4):
-            at = (j,) if self.part == 2 else (j // 2, j % 2)
-            total = own[at].astype(F32)
-            for k in range(3):
-                total = total + self.first[(k, *at)].astype(F32)
-            self.half[j] = total.astype(BF16)
+        self.copies[1].wait_recv()
+        self.copies[2].wait_recv()
+        for yh in range(2):
+            total = self.whole[yh, self.at[0]].astype(F32) + self.first[0, yh].astype(F32)
+            total = total + self.pair[yh].astype(F32)
+            self.half[2 * yh, :72] = total[:72].astype(BF16)
+            self.half[2 * yh + 1, :72] = total[72:].astype(BF16)
         self.start(1)
 
     def stage3(self):
@@ -266,19 +279,19 @@
             total = total + self.third[k].astype(F32)
         self.final[...] = total * (1.0 / 8)
         self.copies[9].start()
-        if self.part == 0:
-            pl.when(self.place.x != self.place.z)(self.trade.start)
+        if self.trades:
+            pl.when(self.moves)(self.trade.start)
 
     def stage5(self):
         mine = self.final
-        if self.part == 0:
+        if self.trades:
             mine = self.mine
 
-            @pl.when(self.place.x == self.place.z)
+            @pl.when(jnp.logical_not(self.moves))
             def _():
                 self.mine[...] = self.final[...]
 
-            pl.when(self.place.x != self.place.z)(self.trade.wait_recv)
+            pl.when(self.moves)(self.trade.wait_recv)
         self.copies[9].wait_recv()
         shift = lax.rem(32 - 2 * self.place.z - 9 * self.place.core, 32)
         own = pltpu.roll(mine[...], shift, 0)[:16]
@@ -289,8 +302,8 @@
     def wait_send(self):
         for copy in self.copies:
             copy.wait_send()
-        if self.part == 0:
-            pl.when(self.place.x != self.place.z)(self.trade.wait_send)
+        if self.trades:
+            pl.when(self.moves)(self.trade.wait_send)
 
 
 def window(i):
@@ -374,7 +387,7 @@
     normed_s, scale_s, packed_s, probs_s, attended_s, branch_s, hidden_out, hidden,
     cot, normed_t, scale_t, packed_t, attended_t, branch_t, grad_out, grad_hidden, d_attended, d_modulated,
     left_s, right_s, left_t, right_t,
-    whole, first_a, first_b, half, second, quarter, third, final, mine, other,
+    whole, first, pair, half, second, quarter, third, final, mine, other,
     held, arrived,
     load_sem, send_sem, recv_sem, pair_send, pair_recv, sum_send, sum_recv, clip_send, clip_recv,
 ):
@@ -415,10 +428,16 @@
         signal(place.at(x=place.z, z=place.x))
         signal(place.at(x=place.z, z=place.x, core=1 - place.core))
 
+    @pl.when(place.x != place.y)
+    def _():
+        signal(place.at(x=place.y, y=place.x))
+        signal(place.at(x=place.y, y=place.x, core=1 - place.core))
+
     loads[0].wait()
     loads[1].wait()
     normalise(lat, mod, 0, normed_s, scale_s, modulated_s)
-    pl.semaphore_wait(barrier, jnp.where(place.x == place.z, SEQ + 4, SEQ + 6))
+    traders = jnp.where(place.x == place.z, 0, 2) + jnp.where(place.x == place.y, 0, 2)
+    pl.semaphore_wait(barrier, SEQ + 4 + traders)
 
     trips = [
         Exchange(source, target, send_sem.at[i], recv_sem.at[i])
@@ -432,13 +451,13 @@
     sums_s, sums_t = [
         [
             Reduction(
-                place, p, whole.at[l, p], first_b.at[l] if p == 2 else first_a.at[l, p], half.at[l, p],
-                second.at[l, p], quarter.at[l, p], third.at[l, p], final.at[l, p], mine.at[l], other.at[l, p],
+                place, names[p], whole.at[l, p], first.at[l, p], pair.at[l, p], half.at[l, p], second.at[l, p],
+                quarter.at[l, p], third.at[l, p], final.at[l, p], mine.at[l, p], other.at[l, p],
                 sum_send.at[l, p], sum_recv.at[l, p],
             )
             for p in range(3)
         ]
-        for l in range(2)
+        for l, names in enumerate((("xyz", "yxz", "zyx"), ("xyz", "xyz", "yxz")))
     ]
     clip = ClipSum(place, held, arrived, clip_send, clip_recv)
 
@@ -495,12 +514,15 @@
     grad_hidden[here, :] = grad_out[here, :]
     pair_t.wait_recv()
     for p in range(3):
-        pair_t.multiply(p, whole.at[1, p].reshape(BLOCKS, BLOCK, PART))
-        sums_t[p].stage1()
+        pair_t.multiply(p, whole.at[1, p])
+        if p < 2:
+            sums_t[p].stage0()
     project_out(attended_t, wot, branch_t)
     clip_first[5:6, :] = gate_sum(cot, branch_t)
+    sums_t[0].stage1()
 
     grad_trip.wait_recv()
+    sums_t[2].stage0()
     gated(grad_hidden, mod, 2, d_branch_s)
     pair_s.start(1)
     d_attended[...] = dot(d_branch_s[...], wos[...], NT).astype(BF16)
@@ -509,9 +531,12 @@
         head_backward(probs, probs.astype(BF16), packed_s, d_attended, h, right_s)
     pair_s.start(2)
     pair_s.wait_recv()
-    for p in range(3):
-        pair_s.multiply(p, whole.at[0, p].reshape(BLOCKS, BLOCK, PART))
-        sums_s[p].stage1()
+    for p in (2, 1, 0):
+        pair_s.multiply(p, whole.at[0, p])
+        sums_s[p].stage0()
+    sums_t[1].stage1()
+    sums_t[0].stage2()
+    sums_t[2].stage1()
     project_back(right_s, wqs, d_modulated)
     d_offset, d_stretch = normalise_back(
         d_modulated, normed_s, scale_s, mod, 0, grad_hidden, grad_latents
@@ -521,24 +546,26 @@
     clip_first[2:3, :] = gate_sum(grad_hidden, branch_s)
     clip_first[6:8, :] = jnp.zeros((2, D), F32)
     clip.start()
-    for p in range(3):
-        sums_t[p].stage2()
+    sums_t[1].stage2()
+    for p in (2, 1, 0):
+        sums_s[p].stage1()
+    sums_t[2].stage2()
     clip.step(0)
     for p in range(3):
         sums_t[p].stage3()
     clip.step(1)
-    for p in range(3):
+    for p in (2, 1, 0):
         sums_s[p].stage2()
     for p in range(3):
         sums_t[p].stage4()
     clip.step(2)
-    for p in range(3):
+    for p in (2, 1, 0):
         sums_s[p].stage3()
     write_rows([sums.stage5() for sums in sums_t], dqkv_t, dout_t)
     clip.step(3)
     for i in range(6):
         moments[i] = held[4, i : i + 1, :]
-    for p in range(3):
+    for p in (2, 1, 0):
         sums_s[p].stage4()
     for part in (*trips, pair_s, pair_t, *sums_t, clip):
         part.wait_send()
@@ -599,9 +626,9 @@
             wide32, column, three, f32(HEADS, TOKENS, TOKENS), narrow, wide32, wide, wide,
             wide, wide32, column, three, narrow, wide32, wide, wide, narrow, wide,
             left, right, left, right,
-            bf16(2, 3, 2, 4, 2, BLOCK, PART), bf16(2, 2, 3, 2, 2, BLOCK, PART), bf16(2, 3, 4, BLOCK, PART),
+            bf16(2, 3, 2, 4, SLAB, PART), bf16(2, 3, 2, 2, SLAB, PART), bf16(2, 3, 2, SLAB, PART),
             bf16(2, 3, 4, BLOCK, PART), bf16(2, 3, 3, BLOCK, PART), bf16(2, 3, BLOCK, PART),
-            bf16(2, 3, 3, 32, PART), f32(2, 3, 32, PART), f32(2, 32, PART), f32(2, 3, 32, PART),
+            bf16(2, 3, 3, 32, PART), f32(2, 3, 32, PART), f32(2, 3, 32, PART), f32(2, 3, 32, PART),
             f32(5, 8, D), f32(4, 8, D),
             dma((7,)), dma((3, SEQ)), dma((3, SEQ)), dma((2, 3)), dma((2, 3)),
             dma((2, 3, 11)), dma((2, 3, 11)), dma((4,)), dma((4,)),

time: 89.4 us -> 91.8 us (1.027)
  Pallas kernels: 87.2 us -> 89.6 us
    pallas_call x1, Pallas kernels: 85.1 us -> 87.5 us  [local(): pl.pallas_call(kernel, out_shape=shapes, in_specs=[hbm] * 7, out_specs=[v...]
where the time goes in v5:
time: 91.8 us; the launch traced here: 90.2 us
  Pallas kernels  89.6 us (98%)
    pallas_call x1, Pallas kernels, local(): pl.pallas_call(kernel, out_shape=shapes, in_specs=[hbm] * 7, out_specs=[v...  87.5 us
    pallas_call x1, Pallas kernels, local(): pl.pallas_call(copy_out, out_shape=shapes, in_specs=[vm] * 6, out_specs=[...  2.1 us

profile of v5, /device:TPU:5, one launch (start us, length us, event | category | flops | bytes accessed | tf_op | source)
XLA Modules:
  0.0 90.2 jit_solution(6663070036864976328)
XLA Ops:
  0.6 87.5 %shard_map.118 = (bf16[256,1152]{1,0:T(8,128)(2,1)}, f32[6,1,1152]{2,1,0:T(1,128)}, f32[9,1728]{1,0:T(8,128)}, f32[9,576]{1,0:T(8,128)}, f32[9,1728]{1,0:T(8,128)}, /*index=5*/f32[9,576]{1,0:T(8,128)}) custom-call(bf16[256,1152]{1,0:T(8,128)(2,1)} %bitcast.13, bf16[256,1152]{1,0:T(8,128)(2,1)} %bitcast.14, f32[6,1,1152]{2,1,0:T(1,128)} %bitcast.15, ...), custom_call_target="tpu_custom_call" | custom-call | tf_op jit(solution)/shard_map/pallas_call | solution.py:619
  88.1 2.1 %shard_map.119 = (bf16[256,1152]{1,0:T(8,128)(2,1)}, f32[6,1,1152]{2,1,0:T(1,128)}, f32[9,1728]{1,0:T(8,128)}, f32[9,576]{1,0:T(8,128)}, f32[9,1728]{1,0:T(8,128)}, /*index=5*/f32[9,576]{1,0:T(8,128)}) custom-call(bf16[256,1152]{1,0:T(8,128)(2,1)} %get-tuple-element.18.refs_0_, f32[6,1,1152]{2,1,0:T(1,128)} %get-tuple-element.19.refs_1_, ...), custom_call_target="tpu_custom_call" | custom-call | tf_op jit(solution)/shard_map/pallas_call | solution.py:643

commit v6 on v5

--- a/solution.py
+++ b/solution.py
@@ -206,10 +206,10 @@
 
 
 class Reduction:
-    def __init__(self, place, names, whole, first, pair, half, second, quarter, third, final, mine, other, send, recv):
+    def __init__(self, place, names, whole, first, pair, half, second, quarter, third, final, other, send, recv):
         self.place, self.names = place, names
         self.whole, self.first, self.pair, self.half, self.second = whole, first, pair, half, second
-        self.quarter, self.third, self.final, self.mine, self.other = quarter, third, final, mine, other
+        self.quarter, self.third, self.final, self.other = quarter, third, final, other
         self.at = [getattr(place, name) for name in names]
         a = self.at[0]
         a1, self.a2 = place.pair(a)
@@ -219,29 +219,48 @@
             remote(whole.at[:, a1], first.at[0], send.at[1], recv.at[1], to_a1),
             remote(whole.at[:, self.a2], pair, send.at[2], recv.at[2], to_a2),
         ]
-        for stage in (1, 2):
-            for j in range(1, 4):
-                peer = lax.rem(self.at[stage] + j, 4)
-                if stage == 1:
-                    src, dst = half.at[peer], second.at[j - 1]
-                else:
-                    src, dst = quarter.at[window(peer)], third.at[j - 1]
-                i = 3 * stage + j - 1
-                self.copies.append(remote(src, dst, send.at[i], recv.at[i], place.at(**{names[stage]: peer})))
-        turned = {n: getattr(place, m) for n, m in zip("xyz", names)}
-        self.trades = names != "xyz"
-        self.moves = place.x != getattr(place, names[0])
-        core = 1 - place.core
-        self.copies.append(remote(final, other, send.at[9], recv.at[9], place.at(**turned, core=core)))
-        self.trade = remote(final, mine, send.at[10], recv.at[10], place.at(**turned)) if self.trades else None
-
-    def start(self, stage):
-        for i in range(3 * stage, 3 * stage + 3):
-            self.copies[i].start()
-
-    def wait(self, stage):
-        for i in range(3 * stage, 3 * stage + 3):
-            self.copies[i].wait_recv()
+        for j in range(1, 4):
+            peer = lax.rem(self.at[1] + j, 4)
+            self.copies.append(
+                remote(half.at[peer], second.at[j - 1], send.at[2 + j], recv.at[2 + j], place.at(**{names[1]: peer}))
+            )
+        x, y, z = place.x, place.y, place.z
+        owner = {n: getattr(place, m) for n, m in zip("xy", names)}
+        came = dict(zip(names[:2], (x, y)))
+        self.owns = [jnp.logical_and(jnp.logical_and(owner["x"] == x, owner["y"] == y), z == j) for j in range(4)]
+        self.took = [
+            jnp.logical_and(
+                jnp.logical_and(getattr(place, names[0]) == x, getattr(place, names[1]) == y), self.at[2] == k
+            )
+            for k in range(4)
+        ]
+        self.out = [
+            remote(
+                quarter.at[window(j)], third.at[self.at[2]], send.at[6 + j], recv.at[6 + self.at[2]],
+                place.at(**owner, z=j),
+            )
+            for j in range(4)
+        ]
+        self.back = [
+            remote(
+                quarter.at[window(z)], third.at[k], send.at[6 + k], recv.at[6 + k],
+                place.at(**came, **{names[2]: k}),
+            )
+            for k in range(4)
+        ]
+        self.swap = remote(final, other, send.at[10], recv.at[10], place.at(core=1 - place.core))
+
+    def start_out(self):
+        for j in range(4):
+            pl.when(jnp.logical_not(self.owns[j]))(self.out[j].start)
+
+            @pl.when(self.owns[j])
+            def _():
+                self.third[self.at[2]] = self.quarter[window(j), :]
+
+    def wait_back(self):
+        for k in range(4):
+            pl.when(jnp.logical_not(self.took[k]))(self.back[k].wait_recv)
 
     def stage0(self):
         self.copies[0].start()
@@ -262,48 +281,41 @@
             total = total + self.pair[yh].astype(F32)
             self.half[2 * yh, :72] = total[:72].astype(BF16)
             self.half[2 * yh + 1, :72] = total[72:].astype(BF16)
-        self.start(1)
+        for copy in self.copies[3:]:
+            copy.start()
 
     def stage3(self):
-        self.wait(1)
+        for copy in self.copies[3:]:
+            copy.wait_recv()
         total = self.half[self.at[1]].astype(F32)
         for k in range(3):
             total = total + self.second[k].astype(F32)
         self.quarter[...] = total.astype(BF16)
-        self.start(2)
+        self.start_out()
 
     def stage4(self):
-        self.wait(2)
-        total = self.quarter[window(self.at[2]), :].astype(F32)
-        for k in range(3):
+        self.wait_back()
+        total = self.third[0].astype(F32)
+        for k in range(1, 4):
             total = total + self.third[k].astype(F32)
-        self.final[...] = total * (1.0 / 8)
-        self.copies[9].start()
-        if self.trades:
-            pl.when(self.moves)(self.trade.start)
-
-    def stage5(self):
-        mine = self.final
-        if self.trades:
-            mine = self.mine
-
-            @pl.when(jnp.logical_not(self.moves))
-            def _():
-                self.mine[...] = self.final[...]
-
-            pl.when(self.moves)(self.trade.wait_recv)
-        self.copies[9].wait_recv()
-        shift = lax.rem(32 - 2 * self.place.z - 9 * self.place.core, 32)
-        own = pltpu.roll(mine[...], shift, 0)[:16]
-        theirs = pltpu.roll(self.other[...], shift, 0)[:16]
+        total = total * (1.0 / 8)
+        start, core = 2 * self.place.z, self.place.core
+        self.final[...] = pltpu.roll(total, lax.rem(32 - start - 9 * (1 - core), 32), 0)[:16]
+        self.swap.start()
+        return pltpu.roll(total, lax.rem(32 - start - 9 * core, 32), 0)[:16]
+
+    def stage5(self, own):
+        self.swap.wait_recv()
         low = self.place.core == 0
+        theirs = self.other[...]
         return jnp.where(low, own, theirs)[:9], jnp.where(low, theirs, own)[:9]
 
     def wait_send(self):
         for copy in self.copies:
             copy.wait_send()
-        if self.trades:
-            pl.when(self.moves)(self.trade.wait_send)
+        for j in range(4):
+            pl.when(jnp.logical_not(self.owns[j]))(self.out[j].wait_send)
+        self.swap.wait_send()
 
 
 def window(i):
@@ -385,9 +397,9 @@
     grad_latents, moments, dqkv_s, dout_s, dqkv_t, dout_t,
     lat, mod, wqs, wos, wqt, wot,
     normed_s, scale_s, packed_s, probs_s, attended_s, branch_s, hidden_out, hidden,
-    cot, normed_t, scale_t, packed_t, attended_t, branch_t, grad_out, grad_hidden, d_attended, d_modulated,
+    cot, normed_t, scale_t, packed_t, probs_t, attended_t, branch_t, grad_out, grad_hidden, d_attended, d_modulated,
     left_s, right_s, left_t, right_t,
-    whole, first, pair, half, second, quarter, third, final, mine, other,
+    whole, first, pair, half, second, quarter, third, final, other,
     held, arrived,
     load_sem, send_sem, recv_sem, pair_send, pair_recv, sum_send, sum_recv, clip_send, clip_recv,
 ):
@@ -419,26 +431,19 @@
 
     lax.fori_loop(1, SEQ, greet, 0)
     for j in range(1, 4):
-        signal(place.at(x=lax.rem(place.x + j, 4)))
+        for k in range(4):
+            signal(place.at(x=lax.rem(place.x + j, 4), z=k))
     signal(place.at(y=lax.rem(place.y + 2, 4)))
     signal(place.at(y=3 - place.y))
 
-    @pl.when(place.x != place.z)
-    def _():
-        signal(place.at(x=place.z, z=place.x))
-        signal(place.at(x=place.z, z=place.x, core=1 - place.core))
-
     @pl.when(place.x != place.y)
     def _():
-        signal(place.at(x=place.y, y=place.x))
-        signal(place.at(x=place.y, y=place.x, core=1 - place.core))
+        for k in range(4):
+            signal(place.at(x=place.y, y=place.x, z=k))
 
     loads[0].wait()
     loads[1].wait()
     normalise(lat, mod, 0, normed_s, scale_s, modulated_s)
-    traders = jnp.where(place.x == place.z, 0, 2) + jnp.where(place.x == place.y, 0, 2)
-    pl.semaphore_wait(barrier, SEQ + 4 + traders)
-
     trips = [
         Exchange(source, target, send_sem.at[i], recv_sem.at[i])
         for i, (source, target) in enumerate(
@@ -452,7 +457,7 @@
         [
             Reduction(
                 place, names[p], whole.at[l, p], first.at[l, p], pair.at[l, p], half.at[l, p], second.at[l, p],
-                quarter.at[l, p], third.at[l, p], final.at[l, p], mine.at[l, p], other.at[l, p],
+                quarter.at[l, p], third.at[l, p], final.at[l, p], other.at[l, p],
                 sum_send.at[l, p], sum_recv.at[l, p],
             )
             for p in range(3)
@@ -464,8 +469,6 @@
     def send_all(trip):
         for j in range(1, SEQ):
             trip.start(j)
-
-    send_all(cot_trip)
 
     loads[2].wait()
     project(modulated_s, wqs, packed_s)
@@ -477,17 +480,13 @@
     project_out(attended_s, wos, branch_s)
     for rows in chunks():
         hidden_out[rows, :] = (lat[rows, :].astype(F32) + mod[2] * branch_s[rows, :]).astype(BF16)
+    pl.semaphore_wait(barrier, SEQ + 13 + jnp.where(place.x == place.y, 0, 4))
     send_all(hidden_trip)
+    send_all(cot_trip)
     hidden[here, :] = hidden_out[here, :]
     right_s[2, :, HE:] = attended_s[...]
     pair_s.start(0)
 
-    loads[6].wait()
-    cot_trip.wait_recv()
-    loads[5].wait()
-    gated(cot, mod, 5, d_branch_t)
-    d_attended[...] = dot(d_branch_t[...], wot[...], NT).astype(BF16)
-    pair_t.start(1)
     hidden_trip.wait_recv()
     normalise(hidden, mod, 3, normed_t, scale_t, modulated_t)
     pair_t.start(0)
@@ -498,9 +497,18 @@
     mask = patch_row == patch_col
     for h in range(HEADS):
         probs = probabilities(packed_t, h, mask)
-        weights = probs.astype(BF16)
-        attend(weights, packed_t, h, attended_t)
-        head_backward(probs, weights, packed_t, d_attended, h, right_t)
+        probs_t[h] = probs
+        attend(probs.astype(BF16), packed_t, h, attended_t)
+    loads[5].wait()
+    project_out(attended_t, wot, branch_t)
+    loads[6].wait()
+    cot_trip.wait_recv()
+    gated(cot, mod, 5, d_branch_t)
+    d_attended[...] = dot(d_branch_t[...], wot[...], NT).astype(BF16)
+    pair_t.start(1)
+    for h in range(HEADS):
+        probs = probs_t[h]
+        head_backward(probs, probs.astype(BF16), packed_t, d_attended, h, right_t)
     right_t[2, :, HE:] = attended_t[...]
     pair_t.start(2)
     project_back(right_t, wqt, d_modulated)
@@ -517,7 +525,6 @@
         pair_t.multiply(p, whole.at[1, p])
         if p < 2:
             sums_t[p].stage0()
-    project_out(attended_t, wot, branch_t)
     clip_first[5:6, :] = gate_sum(cot, branch_t)
     sums_t[0].stage1()
 
@@ -530,6 +537,7 @@
         probs = probs_s[h]
         head_backward(probs, probs.astype(BF16), packed_s, d_attended, h, right_s)
     pair_s.start(2)
+    project_back(right_s, wqs, d_modulated)
     pair_s.wait_recv()
     for p in (2, 1, 0):
         pair_s.multiply(p, whole.at[0, p])
@@ -537,7 +545,6 @@
     sums_t[1].stage1()
     sums_t[0].stage2()
     sums_t[2].stage1()
-    project_back(right_s, wqs, d_modulated)
     d_offset, d_stretch = normalise_back(
         d_modulated, normed_s, scale_s, mod, 0, grad_hidden, grad_latents
     )
@@ -556,20 +563,18 @@
     clip.step(1)
     for p in (2, 1, 0):
         sums_s[p].stage2()
-    for p in range(3):
-        sums_t[p].stage4()
+    owned = [sums.stage4() for sums in sums_t]
     clip.step(2)
     for p in (2, 1, 0):
         sums_s[p].stage3()
-    write_rows([sums.stage5() for sums in sums_t], dqkv_t, dout_t)
+    write_rows([sums.stage5(own) for sums, own in zip(sums_t, owned)], dqkv_t, dout_t)
     clip.step(3)
     for i in range(6):
         moments[i] = held[4, i : i + 1, :]
-    for p in (2, 1, 0):
-        sums_s[p].stage4()
+    owned = [sums.stage4() for sums in sums_s]
     for part in (*trips, pair_s, pair_t, *sums_t, clip):
         part.wait_send()
-    results_s = [sums.stage5() for sums in sums_s]
+    results_s = [sums.stage5(own) for sums, own in zip(sums_s, owned)]
     write_rows(results_s, dqkv_s, dout_s)
     for part in sums_s:
         part.wait_send()
@@ -624,11 +629,11 @@
         scratch_shapes=[
             wide, f32(6, 1, D), wq, wo, wq, wo,
             wide32, column, three, f32(HEADS, TOKENS, TOKENS), narrow, wide32, wide, wide,
-            wide, wide32, column, three, narrow, wide32, wide, wide, narrow, wide,
+            wide, wide32, column, three, f32(HEADS, TOKENS, TOKENS), narrow, wide32, wide, wide, narrow, wide,
             left, right, left, right,
             bf16(2, 3, 2, 4, SLAB, PART), bf16(2, 3, 2, 2, SLAB, PART), bf16(2, 3, 2, SLAB, PART),
             bf16(2, 3, 4, BLOCK, PART), bf16(2, 3, 3, BLOCK, PART), bf16(2, 3, BLOCK, PART),
-            bf16(2, 3, 3, 32, PART), f32(2, 3, 32, PART), f32(2, 3, 32, PART), f32(2, 3, 32, PART),
+            bf16(2, 3, 4, 32, PART), f32(2, 3, 16, PART), f32(2, 3, 16, PART),
             f32(5, 8, D), f32(4, 8, D),
             dma((7,)), dma((3, SEQ)), dma((3, SEQ)), dma((2, 3)), dma((2, 3)),
             dma((2, 3, 11)), dma((2, 3, 11)), dma((4,)), dma((4,)),

time: 91.8 us -> 90.1 us (0.981); the launches traced: 90.2 us -> 90 us
  no operation moved by 1% of the time
where the time goes in v6:
time: 90.1 us; the launch traced here: 90 us
  Pallas kernels  89.3 us (99%)
    pallas_call x1, Pallas kernels, local(): pl.pallas_call(kernel, out_shape=shapes, in_specs=[hbm] * 7, out_specs=[v...  87.2 us
    pallas_call x1, Pallas kernels, local(): pl.pallas_call(copy_out, out_shape=shapes, in_specs=[vm] * 6, out_specs=[...  2.1 us

profile of v6, /device:TPU:5, one launch (start us, length us, event | category | flops | bytes accessed | tf_op | source)
XLA Modules:
  0.0 90.0 jit_solution(2504796119950641842)
XLA Ops:
  0.6 87.2 %shard_map.118 = (bf16[256,1152]{1,0:T(8,128)(2,1)}, f32[6,1,1152]{2,1,0:T(1,128)}, f32[9,1728]{1,0:T(8,128)}, f32[9,576]{1,0:T(8,128)}, f32[9,1728]{1,0:T(8,128)}, /*index=5*/f32[9,576]{1,0:T(8,128)}) custom-call(bf16[256,1152]{1,0:T(8,128)(2,1)} %bitcast.13, bf16[256,1152]{1,0:T(8,128)(2,1)} %bitcast.14, f32[6,1,1152]{2,1,0:T(1,128)} %bitcast.15, ...), custom_call_target="tpu_custom_call" | custom-call | tf_op jit(solution)/shard_map/pallas_call | solution.py:624
  87.9 2.1 %shard_map.119 = (bf16[256,1152]{1,0:T(8,128)(2,1)}, f32[6,1,1152]{2,1,0:T(1,128)}, f32[9,1728]{1,0:T(8,128)}, f32[9,576]{1,0:T(8,128)}, f32[9,1728]{1,0:T(8,128)}, /*index=5*/f32[9,576]{1,0:T(8,128)}) custom-call(bf16[256,1152]{1,0:T(8,128)(2,1)} %get-tuple-element.18.refs_0_, f32[6,1,1152]{2,1,0:T(1,128)} %get-tuple-element.19.refs_1_, ...), custom_call_target="tpu_custom_call" | custom-call | tf_op jit(solution)/shard_map/pallas_call | solution.py:648

commit v7 on v6

--- a/solution.py
+++ b/solution.py
@@ -433,8 +433,9 @@
     for j in range(1, 4):
         for k in range(4):
             signal(place.at(x=lax.rem(place.x + j, 4), z=k))
-    signal(place.at(y=lax.rem(place.y + 2, 4)))
-    signal(place.at(y=3 - place.y))
+    for k in range(4):
+        signal(place.at(y=lax.rem(place.y + 2, 4), z=k))
+        signal(place.at(y=3 - place.y, z=k))
 
     @pl.when(place.x != place.y)
     def _():
@@ -462,7 +463,7 @@
             )
             for p in range(3)
         ]
-        for l, names in enumerate((("xyz", "yxz", "zyx"), ("xyz", "xyz", "yxz")))
+        for l, names in enumerate((("xzy", "yxz", "zyx"), ("xyz", "xzy", "yxz")))
     ]
     clip = ClipSum(place, held, arrived, clip_send, clip_recv)
 
@@ -480,7 +481,7 @@
     project_out(attended_s, wos, branch_s)
     for rows in chunks():
         hidden_out[rows, :] = (lat[rows, :].astype(F32) + mod[2] * branch_s[rows, :]).astype(BF16)
-    pl.semaphore_wait(barrier, SEQ + 13 + jnp.where(place.x == place.y, 0, 4))
+    pl.semaphore_wait(barrier, SEQ + 19 + jnp.where(place.x == place.y, 0, 4))
     send_all(hidden_trip)
     send_all(cot_trip)
     hidden[here, :] = hidden_out[here, :]
@@ -533,18 +534,19 @@
     gated(grad_hidden, mod, 2, d_branch_s)
     pair_s.start(1)
     d_attended[...] = dot(d_branch_s[...], wos[...], NT).astype(BF16)
+    sums_t[1].stage1()
     for h in range(HEADS):
         probs = probs_s[h]
         head_backward(probs, probs.astype(BF16), packed_s, d_attended, h, right_s)
+        if h == 3:
+            sums_t[0].stage2()
     pair_s.start(2)
     project_back(right_s, wqs, d_modulated)
     pair_s.wait_recv()
     for p in (2, 1, 0):
         pair_s.multiply(p, whole.at[0, p])
         sums_s[p].stage0()
-    sums_t[1].stage1()
-    sums_t[0].stage2()
-    sums_t[2].stage1()
+    sums_t[1].stage2()
     d_offset, d_stretch = normalise_back(
         d_modulated, normed_s, scale_s, mod, 0, grad_hidden, grad_latents
     )
@@ -553,28 +555,30 @@
     clip_first[2:3, :] = gate_sum(grad_hidden, branch_s)
     clip_first[6:8, :] = jnp.zeros((2, D), F32)
     clip.start()
-    sums_t[1].stage2()
+    sums_t[2].stage1()
+    sums_t[0].stage3()
     for p in (2, 1, 0):
         sums_s[p].stage1()
+    clip.step(0)
+    sums_t[1].stage3()
     sums_t[2].stage2()
-    clip.step(0)
-    for p in range(3):
-        sums_t[p].stage3()
-    clip.step(1)
     for p in (2, 1, 0):
         sums_s[p].stage2()
-    owned = [sums.stage4() for sums in sums_t]
-    clip.step(2)
+    clip.step(1)
+    owned = [sums_t[0].stage4(), sums_t[1].stage4()]
+    sums_t[2].stage3()
     for p in (2, 1, 0):
         sums_s[p].stage3()
-    write_rows([sums.stage5(own) for sums, own in zip(sums_t, owned)], dqkv_t, dout_t)
+    clip.step(2)
+    owned.append(sums_t[2].stage4())
+    owned_s = [sums.stage4() for sums in sums_s]
     clip.step(3)
     for i in range(6):
         moments[i] = held[4, i : i + 1, :]
-    owned = [sums.stage4() for sums in sums_s]
+    write_rows([sums.stage5(own) for sums, own in zip(sums_t, owned)], dqkv_t, dout_t)
     for part in (*trips, pair_s, pair_t, *sums_t, clip):
         part.wait_send()
-    results_s = [sums.stage5(own) for sums, own in zip(sums_s, owned)]
+    results_s = [sums.stage5(own) for sums, own in zip(sums_s, owned_s)]
     write_rows(results_s, dqkv_s, dout_s)
     for part in sums_s:
         part.wait_send()

time: 90.1 us -> 94.2 us (1.046)
  Pallas kernels: 89.3 us -> 93.5 us
    pallas_call x1, Pallas kernels: 87.2 us -> 91.4 us  [local(): pl.pallas_call(kernel, out_shape=shapes, in_specs=[hbm] * 7, out_specs=[v...]
where the time goes in v7:
time: 94.2 us; the launch traced here: 94.1 us
  Pallas kernels  93.5 us (99%)
    pallas_call x1, Pallas kernels, local(): pl.pallas_call(kernel, out_shape=shapes, in_specs=[hbm] * 7, out_specs=[v...  91.4 us
    pallas_call x1, Pallas kernels, local(): pl.pallas_call(copy_out, out_shape=shapes, in_specs=[vm] * 6, out_specs=[...  2.1 us

profile of v7, /device:TPU:5, one launch (start us, length us, event | category | flops | bytes accessed | tf_op | source)
XLA Modules:
  0.0 94.1 jit_solution(8826382256998868226)
XLA Ops:
  0.6 91.4 %shard_map.118 = (bf16[256,1152]{1,0:T(8,128)(2,1)}, f32[6,1,1152]{2,1,0:T(1,128)}, f32[9,1728]{1,0:T(8,128)}, f32[9,576]{1,0:T(8,128)}, f32[9,1728]{1,0:T(8,128)}, /*index=5*/f32[9,576]{1,0:T(8,128)}) custom-call(bf16[256,1152]{1,0:T(8,128)(2,1)} %bitcast.13, bf16[256,1152]{1,0:T(8,128)(2,1)} %bitcast.14, f32[6,1,1152]{2,1,0:T(1,128)} %bitcast.15, ...), custom_call_target="tpu_custom_call" | custom-call | tf_op jit(solution)/shard_map/pallas_call | solution.py:628
  92.0 2.1 %shard_map.119 = (bf16[256,1152]{1,0:T(8,128)(2,1)}, f32[6,1,1152]{2,1,0:T(1,128)}, f32[9,1728]{1,0:T(8,128)}, f32[9,576]{1,0:T(8,128)}, f32[9,1728]{1,0:T(8,128)}, /*index=5*/f32[9,576]{1,0:T(8,128)}) custom-call(bf16[256,1152]{1,0:T(8,128)(2,1)} %get-tuple-element.18.refs_0_, f32[6,1,1152]{2,1,0:T(1,128)} %get-tuple-element.19.refs_1_, ...), custom_call_target="tpu_custom_call" | custom-call | tf_op jit(solution)/shard_map/pallas_call | solution.py:652

commit v8 on v6

--- a/solution.py
+++ b/solution.py
@@ -236,14 +236,14 @@
         ]
         self.out = [
             remote(
-                quarter.at[window(j)], third.at[self.at[2]], send.at[6 + j], recv.at[6 + self.at[2]],
+                quarter.at[j], third.at[self.at[2]], send.at[6 + j], recv.at[6 + self.at[2]],
                 place.at(**owner, z=j),
             )
             for j in range(4)
         ]
         self.back = [
             remote(
-                quarter.at[window(z)], third.at[k], send.at[6 + k], recv.at[6 + k],
+                quarter.at[0], third.at[k], send.at[6 + k], recv.at[6 + k],
                 place.at(**came, **{names[2]: k}),
             )
             for k in range(4)
@@ -256,7 +256,7 @@
 
             @pl.when(self.owns[j])
             def _():
-                self.third[self.at[2]] = self.quarter[window(j), :]
+                self.third[self.at[2]] = self.quarter[j]
 
     def wait_back(self):
         for k in range(4):
@@ -290,7 +290,11 @@
         total = self.half[self.at[1]].astype(F32)
         for k in range(3):
             total = total + self.second[k].astype(F32)
-        self.quarter[...] = total.astype(BF16)
+        for j in range(4):
+            main, rest = total[18 * j : 18 * j + 16], total[18 * j + 16 : 18 * j + 18]
+            strips = [rest[:, 128 * i : 128 * i + 128] for i in range(3)]
+            strips.append(jnp.zeros((10, 128), F32))
+            self.quarter[j] = jnp.concatenate([main, jnp.concatenate(strips, axis=0)], axis=1).astype(BF16)
         self.start_out()
 
     def stage4(self):
@@ -299,10 +303,12 @@
         for k in range(1, 4):
             total = total + self.third[k].astype(F32)
         total = total * (1.0 / 8)
-        start, core = 2 * self.place.z, self.place.core
-        self.final[...] = pltpu.roll(total, lax.rem(32 - start - 9 * (1 - core), 32), 0)[:16]
+        strips = [total[2 * i : 2 * i + 2, PART:] for i in range(3)]
+        rows = [total[:, :PART], jnp.concatenate(strips, axis=1), jnp.zeros((6, PART), F32)]
+        rows, core = jnp.concatenate(rows, axis=0), self.place.core
+        self.final[...] = pltpu.roll(rows, lax.rem(24 - 9 * (1 - core), 24), 0)[:16]
         self.swap.start()
-        return pltpu.roll(total, lax.rem(32 - start - 9 * core, 32), 0)[:16]
+        return pltpu.roll(rows, lax.rem(24 - 9 * core, 24), 0)[:16]
 
     def stage5(self, own):
         self.swap.wait_recv()
@@ -316,10 +322,6 @@
         for j in range(4):
             pl.when(jnp.logical_not(self.owns[j]))(self.out[j].wait_send)
         self.swap.wait_send()
-
-
-def window(i):
-    return pl.ds(pl.multiple_of(i * 16, 16), 32)
 
 
 class ClipSum:
@@ -397,7 +399,7 @@
     grad_latents, moments, dqkv_s, dout_s, dqkv_t, dout_t,
     lat, mod, wqs, wos, wqt, wot,
     normed_s, scale_s, packed_s, probs_s, attended_s, branch_s, hidden_out, hidden,
-    cot, normed_t, scale_t, packed_t, probs_t, attended_t, branch_t, grad_out, grad_hidden, d_attended, d_modulated,
+    cot, normed_t, scale_t, packed_t, probs_t, attended_t, branch_t, grad_out, grad_hidden, d_attended_out, d_attended, d_modulated,
     left_s, right_s, left_t, right_t,
     whole, first, pair, half, second, quarter, third, final, other,
     held, arrived,
@@ -412,8 +414,8 @@
         pltpu.make_async_copy(src, dst, load_sem.at[i])
         for i, (src, dst) in enumerate(
             [
-                (lat_hbm, lat), (mod_hbm, mod), (wqs_hbm, wqs), (wos_hbm, wos), (wqt_hbm, wqt), (wot_hbm, wot),
-                (cot_hbm.at[here], cot.at[here]),
+                (lat_hbm, lat), (mod_hbm, mod), (wqs_hbm, wqs), (wos_hbm, wos), (cot_hbm, grad_out), (wot_hbm, wot),
+                (wqt_hbm, wqt), (cot_hbm.at[here], cot.at[here]),
             ]
         )
     ]
@@ -447,10 +449,10 @@
     trips = [
         Exchange(source, target, send_sem.at[i], recv_sem.at[i])
         for i, (source, target) in enumerate(
-            [(cot_hbm, cot), (hidden_out, hidden), (grad_out, grad_hidden)]
+            [(cot_hbm, cot), (hidden_out, hidden), (grad_out, grad_hidden), (d_attended_out, d_attended)]
         )
     ]
-    cot_trip, hidden_trip, grad_trip = trips
+    cot_trip, hidden_trip, grad_trip, attended_trip = trips
     pair_s = PairTerms(place, left_s, right_s, pair_send.at[0], pair_recv.at[0])
     pair_t = PairTerms(place, left_t, right_t, pair_send.at[1], pair_recv.at[1])
     sums_s, sums_t = [
@@ -480,9 +482,15 @@
     project_out(attended_s, wos, branch_s)
     for rows in chunks():
         hidden_out[rows, :] = (lat[rows, :].astype(F32) + mod[2] * branch_s[rows, :]).astype(BF16)
+    loads[4].wait()
+    loads[5].wait()
+    gated(grad_out, mod, 5, d_modulated)
+    d_attended_out[...] = dot(d_modulated[...], wot[...], NT).astype(BF16)
     pl.semaphore_wait(barrier, SEQ + 13 + jnp.where(place.x == place.y, 0, 4))
     send_all(hidden_trip)
+    send_all(attended_trip)
     send_all(cot_trip)
+    d_attended[here, :] = d_attended_out[here, :]
     hidden[here, :] = hidden_out[here, :]
     right_s[2, :, HE:] = attended_s[...]
     pair_s.start(0)
@@ -490,7 +498,7 @@
     hidden_trip.wait_recv()
     normalise(hidden, mod, 3, normed_t, scale_t, modulated_t)
     pair_t.start(0)
-    loads[4].wait()
+    loads[6].wait()
     project(modulated_t, wqt, packed_t)
     patch_row = lax.rem(lax.broadcasted_iota(jnp.int32, (TOKENS, TOKENS), 0), 16)
     patch_col = lax.rem(lax.broadcasted_iota(jnp.int32, (TOKENS, TOKENS), 1), 16)
@@ -499,33 +507,32 @@
         probs = probabilities(packed_t, h, mask)
         probs_t[h] = probs
         attend(probs.astype(BF16), packed_t, h, attended_t)
-    loads[5].wait()
     project_out(attended_t, wot, branch_t)
-    loads[6].wait()
-    cot_trip.wait_recv()
-    gated(cot, mod, 5, d_branch_t)
-    d_attended[...] = dot(d_branch_t[...], wot[...], NT).astype(BF16)
-    pair_t.start(1)
+    attended_trip.wait_recv()
     for h in range(HEADS):
         probs = probs_t[h]
         head_backward(probs, probs.astype(BF16), packed_t, d_attended, h, right_t)
     right_t[2, :, HE:] = attended_t[...]
     pair_t.start(2)
     project_back(right_t, wqt, d_modulated)
+    loads[7].wait()
+    cot_trip.wait_recv()
     d_offset, d_stretch = normalise_back(
         d_modulated, normed_t, scale_t, mod, 3, cot, grad_out
     )
     send_all(grad_trip)
+    gated(cot, mod, 5, d_branch_t)
+    pair_t.start(1)
     clip_first = held.at[0]
     clip_first[3:4, :] = d_offset
     clip_first[4:5, :] = d_stretch
+    clip_first[5:6, :] = gate_sum(cot, branch_t)
     grad_hidden[here, :] = grad_out[here, :]
     pair_t.wait_recv()
     for p in range(3):
         pair_t.multiply(p, whole.at[1, p])
         if p < 2:
             sums_t[p].stage0()
-    clip_first[5:6, :] = gate_sum(cot, branch_t)
     sums_t[0].stage1()
 
     grad_trip.wait_recv()
@@ -538,11 +545,11 @@
         head_backward(probs, probs.astype(BF16), packed_s, d_attended, h, right_s)
     pair_s.start(2)
     project_back(right_s, wqs, d_modulated)
+    sums_t[1].stage1()
     pair_s.wait_recv()
     for p in (2, 1, 0):
         pair_s.multiply(p, whole.at[0, p])
         sums_s[p].stage0()
-    sums_t[1].stage1()
     sums_t[0].stage2()
     sums_t[2].stage1()
     d_offset, d_stretch = normalise_back(
@@ -557,24 +564,26 @@
     for p in (2, 1, 0):
         sums_s[p].stage1()
     sums_t[2].stage2()
+    sums_t[0].stage3()
+    sums_t[1].stage3()
     clip.step(0)
-    for p in range(3):
-        sums_t[p].stage3()
+    for p in (2, 1, 0):
+        sums_s[p].stage2()
+    sums_t[2].stage3()
+    owned = [sums_t[0].stage4(), sums_t[1].stage4()]
     clip.step(1)
     for p in (2, 1, 0):
-        sums_s[p].stage2()
-    owned = [sums.stage4() for sums in sums_t]
+        sums_s[p].stage3()
+    owned.append(sums_t[2].stage4())
     clip.step(2)
-    for p in (2, 1, 0):
-        sums_s[p].stage3()
-    write_rows([sums.stage5(own) for sums, own in zip(sums_t, owned)], dqkv_t, dout_t)
+    owned_s = [sums.stage4() for sums in sums_s]
     clip.step(3)
     for i in range(6):
         moments[i] = held[4, i : i + 1, :]
-    owned = [sums.stage4() for sums in sums_s]
+    write_rows([sums.stage5(own) for sums, own in zip(sums_t, owned)], dqkv_t, dout_t)
     for part in (*trips, pair_s, pair_t, *sums_t, clip):
         part.wait_send()
-    results_s = [sums.stage5(own) for sums, own in zip(sums_s, owned)]
+    results_s = [sums.stage5(own) for sums, own in zip(sums_s, owned_s)]
     write_rows(results_s, dqkv_s, dout_s)
     for part in sums_s:
         part.wait_send()
@@ -629,13 +638,13 @@
         scratch_shapes=[
             wide, f32(6, 1, D), wq, wo, wq, wo,
             wide32, column, three, f32(HEADS, TOKENS, TOKENS), narrow, wide32, wide, wide,
-            wide, wide32, column, three, f32(HEADS, TOKENS, TOKENS), narrow, wide32, wide, wide, narrow, wide,
+            wide, wide32, column, three, f32(HEADS, TOKENS, TOKENS), narrow, wide32, wide, wide, narrow, narrow, wide,
             left, right, left, right,
             bf16(2, 3, 2, 4, SLAB, PART), bf16(2, 3, 2, 2, SLAB, PART), bf16(2, 3, 2, SLAB, PART),
-            bf16(2, 3, 4, BLOCK, PART), bf16(2, 3, 3, BLOCK, PART), bf16(2, 3, BLOCK, PART),
-            bf16(2, 3, 4, 32, PART), f32(2, 3, 16, PART), f32(2, 3, 16, PART),
+            bf16(2, 3, 4, BLOCK, PART), bf16(2, 3, 3, BLOCK, PART), bf16(2, 3, 4, 16, PART + 128),
+            bf16(2, 3, 4, 16, PART + 128), f32(2, 3, 16, PART), f32(2, 3, 16, PART),
             f32(5, 8, D), f32(4, 8, D),
-            dma((7,)), dma((3, SEQ)), dma((3, SEQ)), dma((2, 3)), dma((2, 3)),
+            dma((8,)), dma((4, SEQ)), dma((4, SEQ)), dma((2, 3)), dma((2, 3)),
             dma((2, 3, 11)), dma((2, 3, 11)), dma((4,)), dma((4,)),
         ],
         compiler_params=pltpu.CompilerParams(

time: 90.1 us -> 88.6 us (0.983)
  Pallas kernels: 89.3 us -> 87.9 us
    pallas_call x1, Pallas kernels: 87.2 us -> 85.8 us  [local(): pl.pallas_call(kernel, out_shape=shapes, in_specs=[hbm] * 7, out_specs=[v...]
where the time goes in v8:
time: 88.6 us; the launch traced here: 88.5 us
  Pallas kernels  87.9 us (99%)
    pallas_call x1, Pallas kernels, local(): pl.pallas_call(kernel, out_shape=shapes, in_specs=[hbm] * 7, out_specs=[v...  85.8 us
    pallas_call x1, Pallas kernels, local(): pl.pallas_call(copy_out, out_shape=shapes, in_specs=[vm] * 6, out_specs=[...  2.1 us

profile of v8, /device:TPU:5, one launch (start us, length us, event | category | flops | bytes accessed | tf_op | source)
XLA Modules:
  0.0 88.5 jit_solution(13139357400748217705)
XLA Ops:
  0.6 85.8 %shard_map.118 = (bf16[256,1152]{1,0:T(8,128)(2,1)}, f32[6,1,1152]{2,1,0:T(1,128)}, f32[9,1728]{1,0:T(8,128)}, f32[9,576]{1,0:T(8,128)}, f32[9,1728]{1,0:T(8,128)}, /*index=5*/f32[9,576]{1,0:T(8,128)}) custom-call(bf16[256,1152]{1,0:T(8,128)(2,1)} %bitcast.13, bf16[256,1152]{1,0:T(8,128)(2,1)} %bitcast.14, f32[6,1,1152]{2,1,0:T(1,128)} %bitcast.15, ...), custom_call_target="tpu_custom_call" | custom-call | tf_op jit(solution)/shard_map/pallas_call | solution.py:633
  86.4 2.1 %shard_map.119 = (bf16[256,1152]{1,0:T(8,128)(2,1)}, f32[6,1,1152]{2,1,0:T(1,128)}, f32[9,1728]{1,0:T(8,128)}, f32[9,576]{1,0:T(8,128)}, f32[9,1728]{1,0:T(8,128)}, /*index=5*/f32[9,576]{1,0:T(8,128)}) custom-call(bf16[256,1152]{1,0:T(8,128)(2,1)} %get-tuple-element.18.refs_0_, f32[6,1,1152]{2,1,0:T(1,128)} %get-tuple-element.19.refs_1_, ...), custom_call_target="tpu_custom_call" | custom-call | tf_op jit(solution)/shard_map/pallas_call | solution.py:657

commit v9 on v8

--- a/solution.py
+++ b/solution.py
@@ -464,7 +464,7 @@
             )
             for p in range(3)
         ]
-        for l, names in enumerate((("xyz", "yxz", "zyx"), ("xyz", "xyz", "yxz")))
+        for l, names in enumerate((("xyz", "yxz", "zyx"), ("xyz", "yxz", "zyx")))
     ]
     clip = ClipSum(place, held, arrived, clip_send, clip_recv)
 
@@ -531,12 +531,10 @@
     pair_t.wait_recv()
     for p in range(3):
         pair_t.multiply(p, whole.at[1, p])
-        if p < 2:
-            sums_t[p].stage0()
+        sums_t[p].stage0()
     sums_t[0].stage1()
 
     grad_trip.wait_recv()
-    sums_t[2].stage0()
     gated(grad_hidden, mod, 2, d_branch_s)
     pair_s.start(1)
     d_attended[...] = dot(d_branch_s[...], wos[...], NT).astype(BF16)
@@ -546,12 +544,14 @@
     pair_s.start(2)
     project_back(right_s, wqs, d_modulated)
     sums_t[1].stage1()
+    sums_t[2].stage1()
     pair_s.wait_recv()
     for p in (2, 1, 0):
         pair_s.multiply(p, whole.at[0, p])
         sums_s[p].stage0()
     sums_t[0].stage2()
-    sums_t[2].stage1()
+    sums_t[1].stage2()
+    sums_t[2].stage2()
     d_offset, d_stretch = normalise_back(
         d_modulated, normed_s, scale_s, mod, 0, grad_hidden, grad_latents
     )
@@ -560,21 +560,17 @@
     clip_first[2:3, :] = gate_sum(grad_hidden, branch_s)
     clip_first[6:8, :] = jnp.zeros((2, D), F32)
     clip.start()
-    sums_t[1].stage2()
+    for p in range(3):
+        sums_t[p].stage3()
     for p in (2, 1, 0):
         sums_s[p].stage1()
-    sums_t[2].stage2()
-    sums_t[0].stage3()
-    sums_t[1].stage3()
     clip.step(0)
     for p in (2, 1, 0):
         sums_s[p].stage2()
-    sums_t[2].stage3()
-    owned = [sums_t[0].stage4(), sums_t[1].stage4()]
+    owned = [sums.stage4() for sums in sums_t]
     clip.step(1)
     for p in (2, 1, 0):
         sums_s[p].stage3()
-    owned.append(sums_t[2].stage4())
     clip.step(2)
     owned_s = [sums.stage4() for sums in sums_s]
     clip.step(3)

time: 88.6 us -> 92.5 us (1.044)
  the two profiles are of different devices: /device:TPU:5 before, /device:TPU:7 now
where the time goes in v9:
time: 92.5 us; the launch traced here: 92.4 us
  Pallas kernels  91.8 us (99%)
    pallas_call x1, Pallas kernels, local(): pl.pallas_call(kernel, out_shape=shapes, in_specs=[hbm] * 7, out_specs=[v...  89.7 us
    pallas_call x1, Pallas kernels, local(): pl.pallas_call(copy_out, out_shape=shapes, in_specs=[vm] * 6, out_specs=[...  2.1 us

profile of v9, /device:TPU:7, one launch (start us, length us, event | category | flops | bytes accessed | tf_op | source)
XLA Modules:
  0.0 92.4 jit_solution(6855427148638711953)
XLA Ops:
  0.6 89.7 %shard_map.118 = (bf16[256,1152]{1,0:T(8,128)(2,1)}, f32[6,1,1152]{2,1,0:T(1,128)}, f32[9,1728]{1,0:T(8,128)}, f32[9,576]{1,0:T(8,128)}, f32[9,1728]{1,0:T(8,128)}, /*index=5*/f32[9,576]{1,0:T(8,128)}) custom-call(bf16[256,1152]{1,0:T(8,128)(2,1)} %bitcast.13, bf16[256,1152]{1,0:T(8,128)(2,1)} %bitcast.14, f32[6,1,1152]{2,1,0:T(1,128)} %bitcast.15, ...), custom_call_target="tpu_custom_call" | custom-call | tf_op jit(solution)/shard_map/pallas_call | solution.py:629
  90.3 2.1 %shard_map.119 = (bf16[256,1152]{1,0:T(8,128)(2,1)}, f32[6,1,1152]{2,1,0:T(1,128)}, f32[9,1728]{1,0:T(8,128)}, f32[9,576]{1,0:T(8,128)}, f32[9,1728]{1,0:T(8,128)}, /*index=5*/f32[9,576]{1,0:T(8,128)}) custom-call(bf16[256,1152]{1,0:T(8,128)(2,1)} %get-tuple-element.18.refs_0_, f32[6,1,1152]{2,1,0:T(1,128)} %get-tuple-element.19.refs_1_, ...), custom_call_target="tpu_custom_call" | custom-call | tf_op jit(solution)/shard_map/pallas_call | solution.py:653

commit v10 on v9

--- a/solution.py
+++ b/solution.py
@@ -206,13 +206,13 @@
 
 
 class Reduction:
-    def __init__(self, place, names, whole, first, pair, half, second, quarter, third, final, other, send, recv):
+    def __init__(self, place, names, outer, whole, first, pair, half, second, quarter, third, final, other, send, recv):
         self.place, self.names = place, names
         self.whole, self.first, self.pair, self.half, self.second = whole, first, pair, half, second
         self.quarter, self.third, self.final, self.other = quarter, third, final, other
         self.at = [getattr(place, name) for name in names]
         a = self.at[0]
-        a1, self.a2 = place.pair(a)
+        a1, self.a2 = (3 - a, swap1(a)) if outer else place.pair(a)
         to_a1, to_a2 = place.at(**{names[0]: a1}), place.at(**{names[0]: self.a2})
         self.copies = [
             remote(whole.at[:, lax.rem(a + 2, 4)], first.at[1], send.at[0], recv.at[0], to_a1),
@@ -435,8 +435,9 @@
     for j in range(1, 4):
         for k in range(4):
             signal(place.at(x=lax.rem(place.x + j, 4), z=k))
-    signal(place.at(y=lax.rem(place.y + 2, 4)))
-    signal(place.at(y=3 - place.y))
+    for k in range(4):
+        signal(place.at(y=lax.rem(place.y + 2, 4), z=k))
+        signal(place.at(y=3 - place.y, z=k))
 
     @pl.when(place.x != place.y)
     def _():
@@ -458,13 +459,13 @@
     sums_s, sums_t = [
         [
             Reduction(
-                place, names[p], whole.at[l, p], first.at[l, p], pair.at[l, p], half.at[l, p], second.at[l, p],
+                place, names[p], l == 1 and p == 2, whole.at[l, p], first.at[l, p], pair.at[l, p], half.at[l, p], second.at[l, p],
                 quarter.at[l, p], third.at[l, p], final.at[l, p], other.at[l, p],
                 sum_send.at[l, p], sum_recv.at[l, p],
             )
             for p in range(3)
         ]
-        for l, names in enumerate((("xyz", "yxz", "zyx"), ("xyz", "yxz", "zyx")))
+        for l, names in enumerate((("xzy", "yxz", "zyx"), ("xzy", "xzy", "yxz")))
     ]
     clip = ClipSum(place, held, arrived, clip_send, clip_recv)
 
@@ -486,7 +487,7 @@
     loads[5].wait()
     gated(grad_out, mod, 5, d_modulated)
     d_attended_out[...] = dot(d_modulated[...], wot[...], NT).astype(BF16)
-    pl.semaphore_wait(barrier, SEQ + 13 + jnp.where(place.x == place.y, 0, 4))
+    pl.semaphore_wait(barrier, SEQ + 19 + jnp.where(place.x == place.y, 0, 4))
     send_all(hidden_trip)
     send_all(attended_trip)
     send_all(cot_trip)
@@ -545,32 +546,36 @@
     project_back(right_s, wqs, d_modulated)
     sums_t[1].stage1()
     sums_t[2].stage1()
+    sums_t[0].stage2()
     pair_s.wait_recv()
     for p in (2, 1, 0):
         pair_s.multiply(p, whole.at[0, p])
         sums_s[p].stage0()
-    sums_t[0].stage2()
-    sums_t[1].stage2()
-    sums_t[2].stage2()
     d_offset, d_stretch = normalise_back(
-        d_modulated, normed_s, scale_s, mod, 0, grad_hidden, grad_latents
+        d_modulated, normed_s, scale_s, mod, 0, grad_hidden, lat
     )
+    leave = pltpu.make_async_copy(lat, grad_latents, load_sem.at[8])
+    leave.start()
     clip_first[0:1, :] = d_offset
     clip_first[1:2, :] = d_stretch
     clip_first[2:3, :] = gate_sum(grad_hidden, branch_s)
     clip_first[6:8, :] = jnp.zeros((2, D), F32)
     clip.start()
-    for p in range(3):
-        sums_t[p].stage3()
+    sums_t[1].stage2()
+    sums_t[0].stage3()
+    sums_t[2].stage2()
     for p in (2, 1, 0):
         sums_s[p].stage1()
     clip.step(0)
+    sums_t[1].stage3()
+    sums_t[2].stage3()
     for p in (2, 1, 0):
         sums_s[p].stage2()
-    owned = [sums.stage4() for sums in sums_t]
+    owned = [sums_t[0].stage4(), sums_t[1].stage4()]
     clip.step(1)
     for p in (2, 1, 0):
         sums_s[p].stage3()
+    owned.append(sums_t[2].stage4())
     clip.step(2)
     owned_s = [sums.stage4() for sums in sums_s]
     clip.step(3)
@@ -583,6 +588,7 @@
     write_rows(results_s, dqkv_s, dout_s)
     for part in sums_s:
         part.wait_send()
+    leave.wait()
 
 
 def write_rows(results, dqkv, dout):
@@ -630,7 +636,7 @@
         kernel,
         out_shape=shapes,
         in_specs=[hbm] * 7,
-        out_specs=[vm] * 6,
+        out_specs=[hbm] + [vm] * 5,
         scratch_shapes=[
             wide, f32(6, 1, D), wq, wo, wq, wo,
             wide32, column, three, f32(HEADS, TOKENS, TOKENS), narrow, wide32, wide, wide,
@@ -640,7 +646,7 @@
             bf16(2, 3, 4, BLOCK, PART), bf16(2, 3, 3, BLOCK, PART), bf16(2, 3, 4, 16, PART + 128),
             bf16(2, 3, 4, 16, PART + 128), f32(2, 3, 16, PART), f32(2, 3, 16, PART),
             f32(5, 8, D), f32(4, 8, D),
-            dma((8,)), dma((4, SEQ)), dma((4, SEQ)), dma((2, 3)), dma((2, 3)),
+            dma((9,)), dma((4, SEQ)), dma((4, SEQ)), dma((2, 3)), dma((2, 3)),
             dma((2, 3, 11)), dma((2, 3, 11)), dma((4,)), dma((4,)),
         ],
         compiler_params=pltpu.CompilerParams(

time: 92.5 us -> 86 us (0.930)
  the two profiles are of different devices: /device:TPU:7 before, /device:TPU:5 now
where the time goes in v10:
time: 86 us; the launch traced here: 85.1 us
  Pallas kernels  84.5 us (98%)
    pallas_call x1, Pallas kernels, local(): pl.pallas_call(kernel, out_shape=shapes, in_specs=[hbm] * 7, out_specs=[h...  82.4 us
    pallas_call x1, Pallas kernels, local(): pl.pallas_call(copy_out, out_shape=shapes, in_specs=[vm] * 6, out_specs=[...  2.1 us

profile of v10, /device:TPU:5, one launch (start us, length us, event | category | flops | bytes accessed | tf_op | source)
XLA Modules:
  0.0 85.1 jit_solution(6743966421855140368)
XLA Ops:
  0.6 82.4 %shard_map.118 = (bf16[256,1152]{1,0:T(8,128)(2,1)}, f32[6,1,1152]{2,1,0:T(1,128)}, f32[9,1728]{1,0:T(8,128)}, f32[9,576]{1,0:T(8,128)}, f32[9,1728]{1,0:T(8,128)}, /*index=5*/f32[9,576]{1,0:T(8,128)}) custom-call(bf16[256,1152]{1,0:T(8,128)(2,1)} %bitcast.13, bf16[256,1152]{1,0:T(8,128)(2,1)} %bitcast.14, f32[6,1,1152]{2,1,0:T(1,128)} %bitcast.15, ...), custom_call_target="tpu_custom_call" | custom-call | tf_op jit(solution)/shard_map/pallas_call | solution.py:635
  83.0 2.1 %shard_map.119 = (bf16[256,1152]{1,0:T(8,128)(2,1)}, f32[6,1,1152]{2,1,0:T(1,128)}, f32[9,1728]{1,0:T(8,128)}, f32[9,576]{1,0:T(8,128)}, f32[9,1728]{1,0:T(8,128)}, /*index=5*/f32[9,576]{1,0:T(8,128)}) custom-call(bf16[256,1152]{1,0:T(8,128)(2,1)} %get-tuple-element.18.refs_0_, f32[6,1,1152]{2,1,0:T(1,128)} %get-tuple-element.19.refs_1_, ...), custom_call_target="tpu_custom_call" | custom-call | tf_op jit(solution)/shard_map/pallas_call | solution.py:659

commit v11 on v10

--- a/solution.py
+++ b/solution.py
@@ -180,10 +180,12 @@
         else:
             self.copies[i].start()
 
-    def wait_recv(self):
-        self.copies[0].wait_recv()
-        pl.when(self.core == 1)(self.copies[1].wait_recv)
-        self.copies[2].wait_recv()
+    def wait_recv(self, part):
+        if part == 0:
+            self.copies[0].wait_recv()
+            self.copies[2].wait_recv()
+        elif part == 1:
+            pl.when(self.core == 1)(self.copies[1].wait_recv)
 
     def wait_send(self):
         self.copies[0].wait_send()
@@ -319,6 +321,8 @@
     def wait_send(self):
         for copy in self.copies:
             copy.wait_send()
+
+    def wait_send_last(self):
         for j in range(4):
             pl.when(jnp.logical_not(self.owns[j]))(self.out[j].wait_send)
         self.swap.wait_send()
@@ -372,7 +376,7 @@
         self.to(j).start()
 
     def wait_recv(self):
-        def body(j, _):
+        for j in range(1, SEQ):
             sender = lax.rem(self.me + SEQ - j, SEQ)
             pltpu.make_async_remote_copy(
                 src_ref=self.source.at[rows_of(sender, 16)],
@@ -382,16 +386,10 @@
                 device_id={"seq": sender},
                 device_id_type=MESH,
             ).wait_recv()
-            return 0
-
-        lax.fori_loop(1, SEQ, body, 0)
 
     def wait_send(self):
-        def body(j, _):
+        for j in range(1, SEQ):
             self.to(j).wait_send()
-            return 0
-
-        lax.fori_loop(1, SEQ, body, 0)
 
 
 def kernel(
@@ -529,8 +527,8 @@
     clip_first[4:5, :] = d_stretch
     clip_first[5:6, :] = gate_sum(cot, branch_t)
     grad_hidden[here, :] = grad_out[here, :]
-    pair_t.wait_recv()
     for p in range(3):
+        pair_t.wait_recv(p)
         pair_t.multiply(p, whole.at[1, p])
         sums_t[p].stage0()
     sums_t[0].stage1()
@@ -547,7 +545,8 @@
     sums_t[1].stage1()
     sums_t[2].stage1()
     sums_t[0].stage2()
-    pair_s.wait_recv()
+    pair_s.wait_recv(0)
+    pair_s.wait_recv(1)
     for p in (2, 1, 0):
         pair_s.multiply(p, whole.at[0, p])
         sums_s[p].stage0()
@@ -563,6 +562,8 @@
     clip.start()
     sums_t[1].stage2()
     sums_t[0].stage3()
+    for part in (*trips, pair_s, pair_t):
+        part.wait_send()
     sums_t[2].stage2()
     for p in (2, 1, 0):
         sums_s[p].stage1()
@@ -577,17 +578,20 @@
         sums_s[p].stage3()
     owned.append(sums_t[2].stage4())
     clip.step(2)
-    owned_s = [sums.stage4() for sums in sums_s]
+    for part in (*sums_s, *sums_t):
+        part.wait_send()
+    write_rows([sums.stage5(own) for sums, own in zip(sums_t, owned)], dqkv_t, dout_t)
+    for part in sums_t:
+        part.wait_send_last()
     clip.step(3)
     for i in range(6):
         moments[i] = held[4, i : i + 1, :]
-    write_rows([sums.stage5(own) for sums, own in zip(sums_t, owned)], dqkv_t, dout_t)
-    for part in (*trips, pair_s, pair_t, *sums_t, clip):
-        part.wait_send()
+    clip.wait_send()
+    owned_s = [sums.stage4() for sums in sums_s]
     results_s = [sums.stage5(own) for sums, own in zip(sums_s, owned_s)]
     write_rows(results_s, dqkv_s, dout_s)
-    for part in sums_s:
-        part.wait_send()
+    for sums in sums_s:
+        sums.wait_send_last()
     leave.wait()
 
 

time: 86 us -> 85.9 us (level)
  no operation moved by 1% of the time
where the time goes in v11:
time: 85.9 us; the launch traced here: 85.6 us
  Pallas kernels  85 us (99%)
    pallas_call x1, Pallas kernels, local(): pl.pallas_call(kernel, out_shape=shapes, in_specs=[hbm] * 7, out_specs=[h...  82.9 us
    pallas_call x1, Pallas kernels, local(): pl.pallas_call(copy_out, out_shape=shapes, in_specs=[vm] * 6, out_specs=[...  2.1 us

profile of v11, /device:TPU:5, one launch (start us, length us, event | category | flops | bytes accessed | tf_op | source)
XLA Modules:
  0.0 85.6 jit_solution(14039712174267212161)
XLA Ops:
  0.6 82.9 %shard_map.118 = (bf16[256,1152]{1,0:T(8,128)(2,1)}, f32[6,1,1152]{2,1,0:T(1,128)}, f32[9,1728]{1,0:T(8,128)}, f32[9,576]{1,0:T(8,128)}, f32[9,1728]{1,0:T(8,128)}, /*index=5*/f32[9,576]{1,0:T(8,128)}) custom-call(bf16[256,1152]{1,0:T(8,128)(2,1)} %bitcast.13, bf16[256,1152]{1,0:T(8,128)(2,1)} %bitcast.14, f32[6,1,1152]{2,1,0:T(1,128)} %bitcast.15, ...), custom_call_target="tpu_custom_call" | custom-call | tf_op jit(solution)/shard_map/pallas_call | solution.py:639
  83.5 2.1 %shard_map.119 = (bf16[256,1152]{1,0:T(8,128)(2,1)}, f32[6,1,1152]{2,1,0:T(1,128)}, f32[9,1728]{1,0:T(8,128)}, f32[9,576]{1,0:T(8,128)}, f32[9,1728]{1,0:T(8,128)}, /*index=5*/f32[9,576]{1,0:T(8,128)}) custom-call(bf16[256,1152]{1,0:T(8,128)(2,1)} %get-tuple-element.18.refs_0_, f32[6,1,1152]{2,1,0:T(1,128)} %get-tuple-element.19.refs_1_, ...), custom_call_target="tpu_custom_call" | custom-call | tf_op jit(solution)/shard_map/pallas_call | solution.py:663

commit v12 on v11

--- a/solution.py
+++ b/solution.py
@@ -417,7 +417,7 @@
             ]
         )
     ]
-    for load in loads:
+    for load in loads[:3]:
         load.start()
 
     barrier = pltpu.get_barrier_semaphore()
@@ -472,6 +472,8 @@
             trip.start(j)
 
     loads[2].wait()
+    for load in loads[3:]:
+        load.start()
     project(modulated_s, wqs, packed_s)
     for h in range(HEADS):
         probs = probabilities(packed_s, h, None)
@@ -481,12 +483,12 @@
     project_out(attended_s, wos, branch_s)
     for rows in chunks():
         hidden_out[rows, :] = (lat[rows, :].astype(F32) + mod[2] * branch_s[rows, :]).astype(BF16)
+    pl.semaphore_wait(barrier, SEQ + 19 + jnp.where(place.x == place.y, 0, 4))
+    send_all(hidden_trip)
     loads[4].wait()
     loads[5].wait()
     gated(grad_out, mod, 5, d_modulated)
     d_attended_out[...] = dot(d_modulated[...], wot[...], NT).astype(BF16)
-    pl.semaphore_wait(barrier, SEQ + 19 + jnp.where(place.x == place.y, 0, 4))
-    send_all(hidden_trip)
     send_all(attended_trip)
     send_all(cot_trip)
     d_attended[here, :] = d_attended_out[here, :]

time: 85.9 us -> 85.4 us (level)
  no operation moved by 1% of the time
where the time goes in v12:
time: 85.4 us; the launch traced here: 85.2 us
  Pallas kernels  84.6 us (99%)
    pallas_call x1, Pallas kernels, local(): pl.pallas_call(kernel, out_shape=shapes, in_specs=[hbm] * 7, out_specs=[h...  82.5 us
    pallas_call x1, Pallas kernels, local(): pl.pallas_call(copy_out, out_shape=shapes, in_specs=[vm] * 6, out_specs=[...  2.1 us

profile of v12, /device:TPU:5, one launch (start us, length us, event | category | flops | bytes accessed | tf_op | source)
XLA Modules:
  0.0 85.2 jit_solution(11597204438805727198)
XLA Ops:
  0.6 82.5 %shard_map.118 = (bf16[256,1152]{1,0:T(8,128)(2,1)}, f32[6,1,1152]{2,1,0:T(1,128)}, f32[9,1728]{1,0:T(8,128)}, f32[9,576]{1,0:T(8,128)}, f32[9,1728]{1,0:T(8,128)}, /*index=5*/f32[9,576]{1,0:T(8,128)}) custom-call(bf16[256,1152]{1,0:T(8,128)(2,1)} %bitcast.13, bf16[256,1152]{1,0:T(8,128)(2,1)} %bitcast.14, f32[6,1,1152]{2,1,0:T(1,128)} %bitcast.15, ...), custom_call_target="tpu_custom_call" | custom-call | tf_op jit(solution)/shard_map/pallas_call | solution.py:641
  83.1 2.1 %shard_map.119 = (bf16[256,1152]{1,0:T(8,128)(2,1)}, f32[6,1,1152]{2,1,0:T(1,128)}, f32[9,1728]{1,0:T(8,128)}, f32[9,576]{1,0:T(8,128)}, f32[9,1728]{1,0:T(8,128)}, /*index=5*/f32[9,576]{1,0:T(8,128)}) custom-call(bf16[256,1152]{1,0:T(8,128)(2,1)} %get-tuple-element.18.refs_0_, f32[6,1,1152]{2,1,0:T(1,128)} %get-tuple-element.19.refs_1_, ...), custom_call_target="tpu_custom_call" | custom-call | tf_op jit(solution)/shard_map/pallas_call | solution.py:665
